TPU v7x, 32 devices: a whole 2x2x4 slice. The times are simulated.
32 devices in a mesh: wide: 4 (over y, x), narrow: 8 (over z, core).
Axes of the slice: x: 2, y: 2, z: 4, core: 2. Of those that a mesh axis runs over, the one named last changes fastest.
Arguments:
- features: bfloat16 [65536, 128], P(('wide', 'narrow')), may hold values from -6 to 6
- band_tiles: int32 [512, 8, 128, 128], P(('wide', 'narrow')), may hold values 0 or 1
- band_cols: int32 [512, 8], P(('wide', 'narrow')), may hold values from 0 to 15
- off_tiles: int32 [32, 4, 128, 128], P(('wide', 'narrow')), may hold values 0 or 1
- req_block: int32 [32, 4], P(('wide', 'narrow')), may hold values from 0 to 15
- req_row: int32 [32, 4], P(('wide', 'narrow')), may hold values from 0 to 15
- req_valid: int32 [32, 4], P(('wide', 'narrow')), may hold values 0 or 1
- weight_self: bfloat16 [128, 256], replicated, may hold values from -0.5 to 0.5
- weight_neigh: bfloat16 [128, 256], replicated, may hold values from -1.5 to 1.5
- bias_term: bfloat16 [256], replicated, may hold values from -3 to 3
- cotangent: bfloat16 [65536, 256], P(('wide', 'narrow')), may hold values from -6 to 6
Outputs:
- layer_out: bfloat16 [65536, 256], P(('wide', 'narrow'))
- grad_features: float32 [65536, 128], P(('wide', 'narrow'))
- grad_self: float32 [128, 256], replicated
- grad_neigh: float32 [128, 256], replicated
- grad_bias: float32 [256], replicated
All inputs are finite; a program needn't handle non-finite values. No bound on the sum of `band_tiles` or of `off_tiles` or of `req_valid` on one device may be relied on, other than what follows from the above.
Results may differ from a plain program's by a relative error of at most 0.007.
Values may be sent and summed in bfloat16 or wider, within the bound.
No kernel may reach another device: no remote copies, remote signals or barrier semaphores. Data moves between devices by JAX's collectives and lax.ppermute only.
A program may use at most 128 MiB of HBM per device.

v0:
```python
from functools import partial

import jax
import jax.numpy as jnp
from jax import lax
from jax.sharding import PartitionSpec as P


def passed_along(x, axis, by):
    peers = lax.axis_size(axis)
    return lax.ppermute(x, axis, [(i, (i + by) % peers) for i in range(peers)])


def shards(
    features,
    band_tiles,
    band_cols,
    off_tiles,
    req_block,
    req_row,
    req_valid,
    weight_self,
    weight_neigh,
    bias_term,
    cotangent,
):
    row_count, in_width = features.shape
    block_count = band_tiles.shape[0]
    block_size = band_tiles.shape[2]
    loop_size = lax.axis_size("narrow")
    wide_size = lax.axis_size("wide")
    my_index = lax.axis_index("narrow")
    highest = lax.Precision.HIGHEST
    tile_half = band_tiles.astype(jnp.bfloat16)
    block_ids = jnp.arange(block_count, dtype=jnp.int32)

    def band_add(totals, current, which):
        columns = lax.dynamic_index_in_dim(band_cols, which, 1, keepdims=False)
        tiles_now = lax.dynamic_index_in_dim(tile_half, which, 1, keepdims=False)
        picked = jnp.take(current.reshape(block_count, block_size, in_width), columns, axis=0)
        return totals + jnp.einsum(
            "bij,bjf->bif", tiles_now, picked, preferred_element_type=jnp.float32
        )

    start_totals = band_add(
        jnp.zeros((block_count, block_size, in_width), jnp.float32), features, my_index
    )

    def advance_one(offset, state_in):
        current, totals = state_in
        current = passed_along(current, "narrow", 1)
        return (current, band_add(totals, current, (my_index - offset) % loop_size))

    _, band_sum = lax.fori_loop(1, loop_size, advance_one, (features, start_totals))
    ask_ids = req_block[0]
    row_slots = req_row[0]
    off_mask = (off_tiles[0] * req_valid[0][:, None, None]).astype(jnp.bfloat16)
    placing = (row_slots[:, None] == block_ids[None, :]).astype(jnp.float32)
    whole_group = lax.all_gather(features, "wide", axis=0, tiled=True).reshape(
        wide_size, block_count, block_size, in_width
    )
    fetched = whole_group[jnp.arange(wide_size), ask_ids]
    pulled = jnp.einsum("wij,wjf->wif", off_mask, fetched, preferred_element_type=jnp.float32)
    gathered = band_sum + jnp.einsum("wb,wif->bif", placing, pulled, precision=highest)
    off_degree = jnp.sum(off_mask.astype(jnp.float32), axis=2)
    degree = jnp.sum(band_tiles.astype(jnp.float32), axis=(1, 3)) + jnp.einsum(
        "wb,wi->bi", placing, off_degree, precision=highest
    )
    denom = degree + 1.0
    aggregate = (gathered / denom[:, :, None]).reshape(row_count, in_width).astype(jnp.bfloat16)
    pre = jnp.dot(features, weight_self, preferred_element_type=jnp.float32)
    pre = (
        pre
        + jnp.dot(aggregate, weight_neigh, preferred_element_type=jnp.float32)
        + bias_term.astype(jnp.float32)
    )
    activated, pullback = jax.vjp(partial(jax.nn.gelu, approximate=True), pre)
    layer_out = activated.astype(jnp.bfloat16)
    grad_pre = pullback(cotangent.astype(jnp.float32))[0].astype(jnp.bfloat16)
    local_self = jnp.dot(features.T, grad_pre, preferred_element_type=jnp.float32)
    local_neigh = jnp.dot(aggregate.T, grad_pre, preferred_element_type=jnp.float32)
    local_bias = jnp.sum(grad_pre.astype(jnp.float32), axis=0)
    total_self, total_neigh, total_bias = lax.psum(
        (local_self, local_neigh, local_bias), ("wide", "narrow")
    )
    factor = (wide_size * loop_size * row_count) ** (-0.5)
    grad_agg = jnp.dot(grad_pre, weight_neigh.T, preferred_element_type=jnp.float32)
    signal = (grad_agg.reshape(block_count, block_size, in_width) / denom[:, :, None]).astype(
        jnp.bfloat16
    )
    slab_count = row_count * lax.axis_size("narrow") // row_count
    moved = jnp.einsum("bsji,bjf->sbif", tile_half, signal, preferred_element_type=jnp.float32)
    one_hot = (band_cols.T[:, :, None] == block_ids[None, None, :]).astype(jnp.float32)
    placed = jnp.einsum("sbt,sbif->stif", one_hot, moved, precision=highest)
    band_back = lax.psum_scatter(
        placed.reshape(slab_count * row_count, in_width).astype(jnp.bfloat16),
        "narrow",
        scatter_dimension=0,
        tiled=True,
    ).astype(jnp.float32)
    signal_rows = jnp.take(signal, row_slots, axis=0)
    pushed = jnp.einsum("wji,wjf->wif", off_mask, signal_rows, preferred_element_type=jnp.float32)
    peer_count = row_count * lax.axis_size("wide") // row_count
    owner_hot = (ask_ids[:, None] == block_ids[None, :]).astype(jnp.float32)
    placed = jnp.einsum("sb,sif->sbif", owner_hot, pushed, precision=highest)
    off_back = lax.psum_scatter(
        placed.reshape(peer_count * row_count, in_width).astype(jnp.bfloat16),
        "wide",
        scatter_dimension=0,
        tiled=True,
    ).astype(jnp.float32)
    grad_features = jnp.dot(grad_pre, weight_self.T, preferred_element_type=jnp.float32) + (
        band_back + off_back
    )
    return (
        layer_out,
        grad_features,
        total_self * factor,
        total_neigh * factor,
        total_bias * factor,
    )


def solution(mesh):
    placed = (
        P(("wide", "narrow"), None),
        P(("wide", "narrow"), None, None, None),
        P(("wide", "narrow"), None),
        P(("wide", "narrow"), None, None, None),
        P(("wide", "narrow"), None),
        P(("wide", "narrow"), None),
        P(("wide", "narrow"), None),
        P(),
        P(),
        P(),
        P(("wide", "narrow"), None),
    )
    return jax.shard_map(
        shards,
        mesh=mesh,
        in_specs=placed,
        out_specs=(P(("wide", "narrow"), None), P(("wide", "narrow"), None), P(), P(), P()),
        check_vma=False,
    )
```

profile of v0, /device:TPU:0, one launch (start us, length us, event | category | flops | bytes accessed | tf_op | source)
XLA Modules:
  0.0 370.7 jit_solution(17717550799384248572)
XLA Ops:
  10.9 4.1 %convert_reduce_fusion = f32[16,128]{1,0:T(8,128)S(1)} fusion(s32[16,8,128,128]{3,2,1,0:T(8,128)} %param.16), kind=kLoop, calls=%fused_computation.18 | loop fusion | flops 4192256 | bytes 8396800 | tf_op jit(solution)/shard_map/reduce_sum | solution.py:66
  16.2 4.6 %copy_convert_fusion = bf16[16,8,128,128]{3,2,0,1:T(8,128)(2,1)S(1)} fusion(s32[16,8,128,128]{3,2,1,0:T(8,128)} %param.16), kind=kLoop, calls=%fused_computation.17 | loop fusion | flops 2097152 | bytes 12582912 | tf_op jit(solution)/shard_map/convert_element_type | solution.py:34
  20.8 1.9 copy-done.1
  24.9 23.0 %all-gather.2.cloned.1.call-done = bf16[8192,128]{1,0:T(8,128)(2,1)} async-done(((bf16[2048,128]{1,0:T(8,128)(2,1)}), bf16[8192,128]{1,0:T(8,128)(2,1)}) %all-gather.2.cloned.1.call-update) | async-done | bytes 2097168 | tf_op jit(solution)/shard_map/all_gather | solution.py:59
  47.9 2.2 gather_fusion.1
  51.0 89.2 %while.17 = (s32[]{:T(128)}, bf16[2048,128]{1,0:T(8,128)(2,1)S(1)}, f32[16,128,128]{2,1,0:T(8,128)S(1)}, s32[]{:T(128)}, bf16[16,8,128,128]{3,2,0,1:T(8,128)(2,1...) while((s32[]{:T(128)}, bf16[2048,128]{1,0:T(8,128)(2,1)S(1)}, ...), condition=%wide.region_1.3_spmd, body=%wide.region_0.2_spmd.sunk | while | flops 67634288 | bytes 7344720 | solution.py:54
  51.0 10.4 %collective-permute-done = bf16[2048,128]{1,0:T(8,128)(2,1)S(1)} collective-permute-done((bf16[2048,128]{1,0:T(8,128)(2,1)S(1)}, bf16[2048,128]{1,0:T(8,128)(2,1)S(1)}, u32[]{:S(2)}, u32[]{:S(2)}) %collective-permute-start) | collective-permute-done | bytes 524320 | tf_op jit(solution)/shard_map/while/body/eval_jaxpr/ppermute | solution.py:11
  63.8 10.3 %collective-permute-done = bf16[2048,128]{1,0:T(8,128)(2,1)S(1)} collective-permute-done((bf16[2048,128]{1,0:T(8,128)(2,1)S(1)}, bf16[2048,128]{1,0:T(8,128)(2,1)S(1)}, u32[]{:S(2)}, u32[]{:S(2)}) %collective-permute-start) | collective-permute-done | bytes 524320 | tf_op jit(solution)/shard_map/while/body/eval_jaxpr/ppermute | solution.py:11
  76.5 10.3 %collective-permute-done = bf16[2048,128]{1,0:T(8,128)(2,1)S(1)} collective-permute-done((bf16[2048,128]{1,0:T(8,128)(2,1)S(1)}, bf16[2048,128]{1,0:T(8,128)(2,1)S(1)}, u32[]{:S(2)}, u32[]{:S(2)}) %collective-permute-start) | collective-permute-done | bytes 524320 | tf_op jit(solution)/shard_map/while/body/eval_jaxpr/ppermute | solution.py:11
  89.3 10.3 %collective-permute-done = bf16[2048,128]{1,0:T(8,128)(2,1)S(1)} collective-permute-done((bf16[2048,128]{1,0:T(8,128)(2,1)S(1)}, bf16[2048,128]{1,0:T(8,128)(2,1)S(1)}, u32[]{:S(2)}, u32[]{:S(2)}) %collective-permute-start) | collective-permute-done | bytes 524320 | tf_op jit(solution)/shard_map/while/body/eval_jaxpr/ppermute | solution.py:11
  102.0 10.3 %collective-permute-done = bf16[2048,128]{1,0:T(8,128)(2,1)S(1)} collective-permute-done((bf16[2048,128]{1,0:T(8,128)(2,1)S(1)}, bf16[2048,128]{1,0:T(8,128)(2,1)S(1)}, u32[]{:S(2)}, u32[]{:S(2)}) %collective-permute-start) | collective-permute-done | bytes 524320 | tf_op jit(solution)/shard_map/while/body/eval_jaxpr/ppermute | solution.py:11
  114.8 10.3 %collective-permute-done = bf16[2048,128]{1,0:T(8,128)(2,1)S(1)} collective-permute-done((bf16[2048,128]{1,0:T(8,128)(2,1)S(1)}, bf16[2048,128]{1,0:T(8,128)(2,1)S(1)}, u32[]{:S(2)}, u32[]{:S(2)}) %collective-permute-start) | collective-permute-done | bytes 524320 | tf_op jit(solution)/shard_map/while/body/eval_jaxpr/ppermute | solution.py:11
  127.5 10.3 %collective-permute-done = bf16[2048,128]{1,0:T(8,128)(2,1)S(1)} collective-permute-done((bf16[2048,128]{1,0:T(8,128)(2,1)S(1)}, bf16[2048,128]{1,0:T(8,128)(2,1)S(1)}, u32[]{:S(2)}, u32[]{:S(2)}) %collective-permute-start) | collective-permute-done | bytes 524320 | tf_op jit(solution)/shard_map/while/body/eval_jaxpr/ppermute | solution.py:11
  140.2 2.5 fusion.26
  142.9 3.0 convert_reduce_fusion.1
  153.0 6.7 %fusion.9 = f32[16,128,8,128]{3,1,2,0:T(8,128)} fusion(bf16[16,8,128,128]{3,2,0,1:T(8,128)(2,1)} %get-tuple-element.276, bf16[16,128,128,1]{2,0,1,3:T(8,128)(2,1)S(1)} %fusion.80), kind=kOutput, calls=%fused_computation.19 | convolution fusion | flops 536870912 | bytes 13107200 | tf_op jit(solution)/shard_map/bsji,bjf->sbif/dot_general | solution.py:92
  159.8 9.2 %copy.39 = f32[16,128,8,128]{1,0,3,2:T(8,128)} copy(f32[16,128,8,128]{3,1,2,0:T(8,128)} %fusion.9) | data formatting | bytes 16777216 | tf_op jit(solution)/shard_map/bsji,bjf->sbif/dot_general | solution.py:92
  169.0 7.9 %fusion.12 = bf16[8,16,128,128]{3,1,2,0:T(8,128)(2,1)S(1)} fusion(f32[16,128,8,128]{1,0,3,2:T(8,128)} %copy.39, s32[8,16]{1,0:T(8,128)S(1)} %bitcast.85), kind=kOutput, calls=%fused_computation.26 | convolution fusion | flops 404752384 | bytes 12583424 | tf_op jit(solution)/shard_map/sbt,sbif->stif/dot_general | solution.py:94
  176.9 3.1 copy.30
  180.0 37.0 %psum.23 = f32[256]{0:T(256)S(1)} all-reduce(f32[256]{0:T(256)S(1)} %get-tuple-element.188), channel_id=1, replica_groups=mesh['wide'=4,'narrow'=8] {'wide','narrow'}, use_global_device_ids=true, to_apply=%region_9.11 | all-reduce | flops 256 | bytes 2048 | tf_op jit(solution)/shard_map/psum | solution.py:83
  217.5 54.5 %all-reduce.3.cloned.1.call-done = (f32[128,256]{0,1:T(8,128)}, f32[128,256]{0,1:T(8,128)}) async-done(((f32[128,256]{0,1:T(8,128)}, f32[128,256]{0,1:T(8,128)}), (f32[128,256]{0,1:T(8,128)}, f32[128,256]{0,1:T(8,128)})) %all-reduce.3.cloned.1.call-update) | async-done | bytes 262160 | tf_op jit(solution)/shard_map/psum | solution.py:83
  274.5 34.7 %reduce-scatter.5.cloned.1.call-done = bf16[2048,128]{1,0:T(8,128)(2,1)} async-done(((bf16[8192,128]{1,0:T(8,128)(2,1)}), bf16[2048,128]{1,0:T(8,128)(2,1)}) %reduce-scatter.5.cloned.1.call-update) | async-done | bytes 524304 | tf_op jit(solution)/shard_map/reduce_scatter | solution.py:106
  309.2 52.3 %reduce-scatter.3.cloned.1.call-done = bf16[2048,128]{1,0:T(8,128)(2,1)} async-done(((bf16[16384,128]{1,0:T(8,128)(2,1)}), bf16[2048,128]{1,0:T(8,128)(2,1)}) %reduce-scatter.3.cloned.1.call-update) | async-done | bytes 524304 | tf_op jit(solution)/shard_map/reduce_scatter | solution.py:95
  361.5 2.6 convolution_add_fusion.2
  (97 shorter events, 34.5 us)
Async XLA Ops:
  7.2 135.7 %copy-start = (bf16[128,256]{1,0:T(8,128)(2,1)S(1)}, bf16[128,256]{1,0:T(8,128)(2,1)}, u32[]{:S(2)}) copy-start(bf16[128,256]{1,0:T(8,128)(2,1)} %param.23) | copy-start | bytes 196612
  7.2 40.7 %all-gather.2.cloned.1.call-start = ((), (), s32[]{:S(2)}) async-start(), calls=%async_computation.2 | async-start | bytes 2621440 | tf_op jit(solution)/shard_map/all_gather | solution.py:59
  7.9 264.1 %all-reduce.3.cloned.1.call-start = ((), (), s32[]{:S(2)}) async-start(), calls=%async_computation.5 | async-start | bytes 524288 | tf_op jit(solution)/shard_map/psum | solution.py:83
  10.9 4.1 %copy-start.8 = (s32[1,4]{1,0:T(1,128)S(1)}, s32[1,4]{1,0:T(1,128)}, u32[]{:S(2)}) copy-start(s32[1,4]{1,0:T(1,128)} %param.20) | copy-start | bytes 52
  10.9 4.5 %copy-start.5 = (s32[16,8]{0,1:T(8,128)S(1)}, s32[16,8]{0,1:T(8,128)}, u32[]{:S(2)}) copy-start(s32[16,8]{0,1:T(8,128)} %param.17) | copy-start | bytes 1540
  10.9 4.5 %copy-start.2 = (bf16[2048,128]{1,0:T(8,128)(2,1)S(1)}, bf16[2048,128]{1,0:T(8,128)(2,1)}, u32[]{:S(2)}) copy-start(bf16[2048,128]{1,0:T(8,128)(2,1)} %param.15) | copy-start | bytes 1572868
  10.9 5.2 %copy-start.6 = (s32[1,4]{1,0:T(1,128)S(1)}, s32[1,4]{1,0:T(1,128)}, u32[]{:S(2)}) copy-start(s32[1,4]{1,0:T(1,128)} %param.19) | copy-start | bytes 52
  20.8 2.0 copy-start.1
  20.8 2.3 copy-start.4
  51.0 10.4 %collective-permute-start = (bf16[2048,128]{1,0:T(8,128)(2,1)S(1)}, bf16[2048,128]{1,0:T(8,128)(2,1)S(1)}, u32[]{:S(2)}, u32[]{:S(2)}) collective-permute-start(bf16[2048,128]{1,0:T(8,128)(2,1)S(1)} %get-tuple-element.249), channel_id=1, source_target_pairs={{0,1},{1,2},{2,3},{3,4},{4,5},{5,6},{6,7},{7,0},{8,9},{9,10},{10,1... | collective-permute-start | bytes 1572872 | tf_op jit(solution)/shard_map/while/body/eval_jaxpr/ppermute | solution.py:11
  63.7 10.5 %collective-permute-start = (bf16[2048,128]{1,0:T(8,128)(2,1)S(1)}, bf16[2048,128]{1,0:T(8,128)(2,1)S(1)}, u32[]{:S(2)}, u32[]{:S(2)}) collective-permute-start(bf16[2048,128]{1,0:T(8,128)(2,1)S(1)} %get-tuple-element.249), channel_id=1, source_target_pairs={{0,1},{1,2},{2,3},{3,4},{4,5},{5,6},{6,7},{7,0},{8,9},{9,10},{10,1... | collective-permute-start | bytes 1572872 | tf_op jit(solution)/shard_map/while/body/eval_jaxpr/ppermute | solution.py:11
  76.4 10.5 %collective-permute-start = (bf16[2048,128]{1,0:T(8,128)(2,1)S(1)}, bf16[2048,128]{1,0:T(8,128)(2,1)S(1)}, u32[]{:S(2)}, u32[]{:S(2)}) collective-permute-start(bf16[2048,128]{1,0:T(8,128)(2,1)S(1)} %get-tuple-element.249), channel_id=1, source_target_pairs={{0,1},{1,2},{2,3},{3,4},{4,5},{5,6},{6,7},{7,0},{8,9},{9,10},{10,1... | collective-permute-start | bytes 1572872 | tf_op jit(solution)/shard_map/while/body/eval_jaxpr/ppermute | solution.py:11
  89.2 10.5 %collective-permute-start = (bf16[2048,128]{1,0:T(8,128)(2,1)S(1)}, bf16[2048,128]{1,0:T(8,128)(2,1)S(1)}, u32[]{:S(2)}, u32[]{:S(2)}) collective-permute-start(bf16[2048,128]{1,0:T(8,128)(2,1)S(1)} %get-tuple-element.249), channel_id=1, source_target_pairs={{0,1},{1,2},{2,3},{3,4},{4,5},{5,6},{6,7},{7,0},{8,9},{9,10},{10,1... | collective-permute-start | bytes 1572872 | tf_op jit(solution)/shard_map/while/body/eval_jaxpr/ppermute | solution.py:11
  101.9 10.5 %collective-permute-start = (bf16[2048,128]{1,0:T(8,128)(2,1)S(1)}, bf16[2048,128]{1,0:T(8,128)(2,1)S(1)}, u32[]{:S(2)}, u32[]{:S(2)}) collective-permute-start(bf16[2048,128]{1,0:T(8,128)(2,1)S(1)} %get-tuple-element.249), channel_id=1, source_target_pairs={{0,1},{1,2},{2,3},{3,4},{4,5},{5,6},{6,7},{7,0},{8,9},{9,10},{10,1... | collective-permute-start | bytes 1572872 | tf_op jit(solution)/shard_map/while/body/eval_jaxpr/ppermute | solution.py:11
  114.7 10.5 %collective-permute-start = (bf16[2048,128]{1,0:T(8,128)(2,1)S(1)}, bf16[2048,128]{1,0:T(8,128)(2,1)S(1)}, u32[]{:S(2)}, u32[]{:S(2)}) collective-permute-start(bf16[2048,128]{1,0:T(8,128)(2,1)S(1)} %get-tuple-element.249), channel_id=1, source_target_pairs={{0,1},{1,2},{2,3},{3,4},{4,5},{5,6},{6,7},{7,0},{8,9},{9,10},{10,1... | collective-permute-start | bytes 1572872 | tf_op jit(solution)/shard_map/while/body/eval_jaxpr/ppermute | solution.py:11
  127.4 10.5 %collective-permute-start = (bf16[2048,128]{1,0:T(8,128)(2,1)S(1)}, bf16[2048,128]{1,0:T(8,128)(2,1)S(1)}, u32[]{:S(2)}, u32[]{:S(2)}) collective-permute-start(bf16[2048,128]{1,0:T(8,128)(2,1)S(1)} %get-tuple-element.249), channel_id=1, source_target_pairs={{0,1},{1,2},{2,3},{3,4},{4,5},{5,6},{6,7},{7,0},{8,9},{9,10},{10,1... | collective-permute-start | bytes 1572872 | tf_op jit(solution)/shard_map/while/body/eval_jaxpr/ppermute | solution.py:11
  140.2 2.7 copy-start.3
  140.2 2.7 copy-start.7
  149.4 159.8 %reduce-scatter.5.cloned.1.call-start = ((), (), s32[]{:S(2)}) async-start(), calls=%async_computation.4 | async-start | bytes 2621440 | tf_op jit(solution)/shard_map/reduce_scatter | solution.py:106
  152.1 209.4 %reduce-scatter.3.cloned.1.call-start = ((), (), s32[]{:S(2)}) async-start(), calls=%async_computation.3 | async-start | bytes 4718592 | tf_op jit(solution)/shard_map/reduce_scatter | solution.py:95
Sparse Core Ops, SparseCore 0:
  9.9 38.0 all-gather.1
  149.6 122.3 all-reduce.2
  275.0 34.2 reduce-scatter.4
  311.5 49.9 reduce-scatter.2
where the time goes:
time: 372 us; the launch traced here: 371 us
  waiting for transfers between devices  238 us (64%)
  matrix products  39.9 us (11%)
  blocking collectives  37 us (10%)
  local copies, waits for them, and re-layouts  25.4 us (7%)
  other arithmetic  15.5 us (4%)
  between operations  14 us (4%)
    ppermute x7, waiting for transfers between devices, passed_along(): return lax.ppermute(x, axis, [(i, (i + by) % peers) for i in range(peers)])  72.4 us
    psum x1, waiting for transfers between devices, shards(): lax.psum((local_self, local_neigh, local_bias), ('wide', 'narrow'))  54.5 us
    reduce_scatter x1, waiting for transfers between devices, shards(): lax.psum_scatter(placed.reshape(slab_count * row_count, in_width).astype(...  52.3 us
    psum x1, blocking collectives, shards(): lax.psum((local_self, local_neigh, local_bias), ('wide', 'narrow'))  37 us
    reduce_scatter x1, waiting for transfers between devices, shards(): lax.psum_scatter(placed.reshape(peer_count * row_count, in_width).astype(...  34.7 us
    all_gather x1, waiting for transfers between devices, shards(): lax.all_gather(features, 'wide', axis=0, tiled=True)  23 us
    dot_general x8, matrix products, band_add(): jnp.einsum('bij,bjf->bif', tiles_now, picked, preferred_element_type=jnp....  11.4 us
    dot_general x1, local copies, waits for them, and re-layouts, shards(): jnp.einsum('bsji,bjf->sbif', tile_half, signal, preferred_element_type=jn...  9.21 us
  transfers between devices with their start and end apart: 11, of which 11 were waited for; matrix products, arithmetic and copies ran while one was open for 13% of the time, Pallas kernels for 0%

commit v1 on v0

v1 whole, which is shorter than its diff:
```python
from functools import partial

import jax
import jax.numpy as jnp
from jax import lax
from jax.experimental import pallas as pl
from jax.experimental.pallas import tpu as pltpu
from jax.sharding import PartitionSpec as P

F32 = jnp.float32
BF16 = jnp.bfloat16
BLK = 128
ROWS_PER = 4
VMEM = 48 * 1024 * 1024


def mm(a, b, lhs=1, rhs=0):
    return lax.dot_general(a, b, (((lhs,), (rhs,)), ((), ())), preferred_element_type=F32)


def params():
    return pltpu.CompilerParams(vmem_limit_bytes=VMEM)


def cost(flops, nbytes, trans=0):
    return pl.CostEstimate(flops=flops, bytes_accessed=nbytes, transcendentals=trans)


def prep_kernel(t_ref, plain_ref, turned_ref, deg_ref):
    total = jnp.zeros((BLK, BLK), F32)
    for k in range(t_ref.shape[1]):
        t = t_ref[0, k].astype(F32)
        total = total + t
        plain_ref[0, k] = t.astype(BF16)
        turned_ref[0, k] = t.T.astype(BF16)
    deg_ref[...] = jnp.broadcast_to(jnp.sum(total, axis=1, keepdims=True), (BLK, BLK))


def prep(tiles):
    g, n = tiles.shape[:2]
    tile_spec = pl.BlockSpec((1, n, BLK, BLK), lambda i: (i, 0, 0, 0))
    return pl.pallas_call(
        prep_kernel,
        grid=(g,),
        in_specs=[tile_spec],
        out_specs=[tile_spec, tile_spec, pl.BlockSpec((BLK, BLK), lambda i: (i, 0))],
        out_shape=[
            jax.ShapeDtypeStruct(tiles.shape, BF16),
            jax.ShapeDtypeStruct(tiles.shape, BF16),
            jax.ShapeDtypeStruct((g * BLK, BLK), F32),
        ],
        compiler_params=params(),
        cost_estimate=cost(tiles.size, tiles.size * 8),
        name="prep",
    )(tiles)


def block(ref, index):
    return ref[pl.ds(pl.multiple_of(index * BLK, BLK), BLK), :]


def pull_sum(ids, cols, tiles_ref, own_ref, sib_ref, b, g, n, step):
    core, chip = ids[0], ids[1 + step]
    own = block(own_ref, cols[g * n + chip * 2 + core])
    sib = block(sib_ref, cols[g * n + chip * 2 + 1 - core])
    return mm(tiles_ref[b, core], own) + mm(tiles_ref[b, 1 - core], sib)


def pull_kernel(ids, cols, *refs, n, step, first):
    if first:
        tiles_ref, own_ref, sib_ref, out_ref = refs
    else:
        tiles_ref, own_ref, sib_ref, acc_ref, out_ref = refs
    i = pl.program_id(0)
    for b in range(ROWS_PER):
        rows = pl.ds(b * BLK, BLK)
        part = pull_sum(ids, cols, tiles_ref, own_ref, sib_ref, b, i * ROWS_PER + b, n, step)
        out_ref[rows, :] = part if first else acc_ref[rows, :] + part


def pull(ids, cols, tiles, own, sib, acc, step):
    g, n = tiles.shape[:2]
    rows, width = own.shape
    whole = pl.BlockSpec((rows, width), lambda i, ids, cols: (0, 0))
    part = pl.BlockSpec((ROWS_PER * BLK, width), lambda i, ids, cols: (i, 0))
    pair = pl.BlockSpec((ROWS_PER, 2, BLK, BLK), lambda i, ids, cols: (i, ids[1 + step], 0, 0))
    more = () if acc is None else (acc,)
    return pl.pallas_call(
        partial(pull_kernel, n=n, step=step, first=acc is None),
        grid_spec=pltpu.PrefetchScalarGridSpec(
            num_scalar_prefetch=2,
            grid=(g // ROWS_PER,),
            in_specs=[pair, whole, whole] + [part] * len(more),
            out_specs=part,
        ),
        out_shape=jax.ShapeDtypeStruct((rows, width), F32),
        compiler_params=params(),
        cost_estimate=cost(4 * rows * BLK * width, 12 * rows * width),
        name=f"pull{step}",
    )(ids, cols, tiles, own, sib, *more)


def off_kernel(asked, row, valid, off_ref, *refs, wide):
    fetched, (acc_in, deg_in, acc_ref, deg_ref) = refs[:wide], refs[wide:]
    acc_ref[...] = acc_in[...]
    deg_ref[...] = deg_in[...]
    here = lax.axis_index("wide")
    for k in range(wide):
        src = source(here, k, wide)
        mask = off_ref[0, src].astype(F32) * valid[src].astype(F32)
        at = pl.ds(pl.multiple_of(row[src] * BLK, BLK), BLK)
        acc_ref[at, :] += mm(mask.astype(BF16), fetched[k][...])
        deg_ref[at, :] += jnp.broadcast_to(jnp.sum(mask, axis=1, keepdims=True), (BLK, BLK))


def off_band(asked, row, valid, off_tiles, by_peer, acc, deg):
    wide = len(by_peer)
    rows, width = acc.shape

    def spec_of(k):
        return pl.BlockSpec(
            (BLK, width), lambda i, asked, row, valid: (asked[wide + k], 0)
        )

    full = pl.BlockSpec((rows, width), lambda i, *s: (0, 0))
    offs = pl.BlockSpec(off_tiles.shape, lambda i, *s: (0, 0, 0, 0))
    return pl.pallas_call(
        partial(off_kernel, wide=wide),
        grid_spec=pltpu.PrefetchScalarGridSpec(
            num_scalar_prefetch=3,
            grid=(1,),
            in_specs=[offs] + [spec_of(k) for k in range(wide)] + [full, full],
            out_specs=[full, full],
        ),
        out_shape=[jax.ShapeDtypeStruct((rows, width), F32)] * 2,
        compiler_params=params(),
        cost_estimate=cost(2 * wide * BLK**3, 16 * rows * width),
        name="off_band",
    )(asked, row, valid, off_tiles, *by_peer, acc, deg)


def place(cols, turned, signal_rows, place_ref, g, core, chip, n):
    for j in range(2):
        which = core if j == 0 else 1 - core
        at = pl.ds(pl.multiple_of(cols[g * n + chip * 2 + which] * BLK, BLK), BLK)
        place_ref[j, at, :] += mm(turned(which), signal_rows)


def middle_kernel(
    ids, cols, tiles_ref, own_ref, sib_ref, acc_ref, deg_ref, feat_ref, cot_ref,
    wself_ref, wneigh_ref, bias_ref, turned_ref,
    out_ref, gp_ref, agg_ref, sig_ref, keep_ref, send_ref, place_ref, *, n, steps,
):
    i = pl.program_id(0)

    @pl.when(i == 0)
    def _():
        place_ref[...] = jnp.zeros_like(place_ref)

    inverse = 1.0 / (deg_ref[...] + 1.0)
    sums = [
        pull_sum(ids, cols, tiles_ref, own_ref, sib_ref, b, i * ROWS_PER + b, n, steps - 1)
        for b in range(ROWS_PER)
    ]
    gathered = acc_ref[...] + jnp.concatenate(sums, axis=0)
    aggregate = (gathered * inverse).astype(BF16)
    agg_ref[...] = aggregate
    pre = mm(feat_ref[...], wself_ref[...]) + mm(aggregate, wneigh_ref[...])
    pre = pre + bias_ref[...].astype(F32)
    slope = 0.7978845608028654
    square = pre * pre
    bent = jnp.tanh(slope * (pre + 0.044715 * (square * pre)))
    half = 0.5 * (1.0 + bent)
    out_ref[...] = (pre * half).astype(BF16)
    deriv = half + (0.5 * pre) * (1.0 - bent * bent) * (slope + (3 * 0.044715 * slope) * square)
    grad_pre = (cot_ref[...].astype(F32) * deriv).astype(BF16)
    gp_ref[...] = grad_pre
    signal = (mm(grad_pre, wneigh_ref[...], 1, 1) * inverse).astype(BF16)
    sig_ref[...] = signal
    core, chip = ids[0], ids[2]
    for b in range(ROWS_PER):
        place(
            cols, lambda which, b=b: turned_ref[b, which], signal[b * BLK : (b + 1) * BLK],
            place_ref, i * ROWS_PER + b, core, chip, n,
        )

    @pl.when(i == pl.num_programs(0) - 1)
    def _():
        keep_ref[...] = place_ref[0].astype(BF16)
        send_ref[...] = place_ref[1].astype(BF16)


def middle(ids, cols, tiles, turned, own, sib, acc, deg, features, cot, w_self, w_neigh, bias, steps):
    g, n = tiles.shape[:2]
    rows, width = features.shape
    outw = w_self.shape[1]
    tall = ROWS_PER * BLK

    def whole(r, c):
        return pl.BlockSpec((r, c), lambda i, ids, cols: (0, 0))

    def part(c):
        return pl.BlockSpec((tall, c), lambda i, ids, cols: (i, 0))

    def pair(at):
        return pl.BlockSpec((ROWS_PER, 2, BLK, BLK), lambda i, ids, cols: (i, ids[at], 0, 0))

    def shape(c, t):
        return jax.ShapeDtypeStruct((rows, c), t)

    return pl.pallas_call(
        partial(middle_kernel, n=n, steps=steps),
        grid_spec=pltpu.PrefetchScalarGridSpec(
            num_scalar_prefetch=2,
            grid=(g // ROWS_PER,),
            in_specs=[
                pair(steps), whole(rows, width), whole(rows, width), part(width), part(width),
                part(width), part(outw), whole(width, outw), whole(width, outw), whole(1, outw),
                pair(2),
            ],
            out_specs=[
                part(outw), part(outw), part(width), part(width),
                whole(rows, width), whole(rows, width),
            ],
            scratch_shapes=[pltpu.VMEM((2, rows, width), F32)],
        ),
        out_shape=[
            shape(outw, BF16), shape(outw, BF16), shape(width, BF16), shape(width, BF16),
            shape(width, BF16), shape(width, BF16),
        ],
        compiler_params=params(),
        cost_estimate=cost(8 * rows * BLK * width + 6 * rows * width * outw, 30 * rows * width, rows * outw),
        name="middle",
    )(ids, cols, tiles, own, sib, acc, deg, features, cot, w_self, w_neigh, bias, turned)


def push_kernel(ids, cols, sig_ref, turned_ref, keep_ref, send_ref, place_ref, *, n, steps):
    p = pl.program_id(0)
    chip = ids[1 + lax.rem(p + 2, steps)]
    place_ref[...] = jnp.zeros_like(place_ref)
    for g in range(turned_ref.shape[0]):
        place(
            cols, lambda which, g=g: turned_ref[g, which], sig_ref[g * BLK : (g + 1) * BLK, :],
            place_ref, g, ids[0], chip, n,
        )
    keep_ref[0] = place_ref[0].astype(BF16)
    send_ref[0] = place_ref[1].astype(BF16)


def push(ids, cols, signal, turned, steps):
    g, n = turned.shape[:2]
    rows, width = signal.shape
    out = pl.BlockSpec((1, rows, width), lambda p, ids, cols: (p, 0, 0))
    return pl.pallas_call(
        partial(push_kernel, n=n, steps=steps),
        grid_spec=pltpu.PrefetchScalarGridSpec(
            num_scalar_prefetch=2,
            grid=(steps - 1,),
            in_specs=[
                pl.BlockSpec((rows, width), lambda p, ids, cols: (0, 0)),
                pl.BlockSpec(
                    (g, 2, BLK, BLK),
                    lambda p, ids, cols: (0, ids[1 + lax.rem(p + 2, steps)], 0, 0),
                ),
            ],
            out_specs=[out, out],
            scratch_shapes=[pltpu.VMEM((2, rows, width), F32)],
        ),
        out_shape=[jax.ShapeDtypeStruct((steps - 1, rows, width), BF16)] * 2,
        compiler_params=params(),
        cost_estimate=cost(4 * (steps - 1) * rows * BLK * width, 8 * (steps - 1) * rows * width),
        name="push",
    )(ids, cols, signal, turned)


def split(x):
    high = x.astype(BF16)
    return high, (x - high.astype(F32)).astype(BF16)


def message_kernel(asked, row, valid, off_ref, sig_ref, feat_ref, agg_ref, gp_ref, msg_ref, *, wide):
    here = lax.axis_index("wide")
    tall = 4 * BLK
    dself = dneigh = dbias = None
    for i in range(feat_ref.shape[0] // tall):
        rows = pl.ds(i * tall, tall)
        gp = gp_ref[rows, :]
        a = mm(feat_ref[rows, :], gp, 0, 0)
        b = mm(agg_ref[rows, :], gp, 0, 0)
        c = jnp.sum(gp.astype(F32), axis=0, keepdims=True)
        dself, dneigh, dbias = (a, b, c) if i == 0 else (dself + a, dneigh + b, dbias + c)
    parts = []
    for d in (dself, dneigh):
        high, low = split(d)
        parts += [high[:, :BLK], high[:, BLK:], low[:, :BLK], low[:, BLK:]]
    grads = jnp.concatenate(parts, axis=0)
    bias_high, bias_low = split(jnp.broadcast_to(dbias, (16, 2 * BLK)))
    line = lax.broadcasted_iota(jnp.int32, (16, BLK), 0)
    for k in range(wide):
        peer = target(here, k, wide)
        mask = (off_ref[0, peer] * valid[peer]).astype(F32).astype(BF16)
        at = pl.ds(pl.multiple_of(row[peer] * BLK, BLK), BLK)
        msg_ref[k, pl.ds(0, BLK), :] = mm(mask, sig_ref[at, :], 0, 0).astype(BF16)
        index = jnp.full((16, BLK), asked[peer], jnp.int32).astype(F32)
        extra = jnp.where(line == 0, index, 0.0)
        for r, v in enumerate(
            (bias_high[:, :BLK], bias_high[:, BLK:], bias_low[:, :BLK], bias_low[:, BLK:])
        ):
            extra = jnp.where(line == r + 1, v.astype(F32), extra)
        msg_ref[k, pl.ds(BLK, 16), :] = extra.astype(BF16)
        msg_ref[k, pl.ds(BLK + 16, 8 * BLK), :] = grads


def messages(asked, row, valid, off_tiles, signal, features, aggregate, grad_pre):
    wide = off_tiles.shape[1]
    tall = 9 * BLK + 16
    rows, width = features.shape

    def whole(x):
        return pl.BlockSpec(x.shape, lambda i, *s: (0,) * x.ndim)

    ins = (off_tiles, signal, features, aggregate, grad_pre)
    return pl.pallas_call(
        partial(message_kernel, wide=wide),
        grid_spec=pltpu.PrefetchScalarGridSpec(
            num_scalar_prefetch=3,
            grid=(1,),
            in_specs=[whole(x) for x in ins],
            out_specs=pl.BlockSpec((wide, tall, width), lambda i, *s: (0, 0, 0)),
        ),
        out_shape=jax.ShapeDtypeStruct((wide, tall, width), BF16),
        compiler_params=params(),
        cost_estimate=cost(8 * rows * width * width, 16 * rows * width),
        name="messages",
    )(asked, row, valid, *ins)


def base_kernel(places, gp_ref, wself_ref, keep_ref, come_ref, pushed_ref, out_ref):
    tall = 4 * BLK
    for i in range(out_ref.shape[0] // tall):
        rows = pl.ds(i * tall, tall)
        both = keep_ref[rows, :].astype(F32) + come_ref[rows, :].astype(F32)
        out_ref[rows, :] = mm(gp_ref[rows, :], wself_ref[...], 1, 1) + both
    for k in range(pushed_ref.shape[0]):
        at = pl.ds(pl.multiple_of(places[k] * BLK, BLK), BLK)
        out_ref[at, :] += pushed_ref[k].astype(F32)


def base(places, grad_pre, w_self, keep, come, pushed):
    rows, width = keep.shape

    def whole(x):
        return pl.BlockSpec(x.shape, lambda i, *s: (0,) * x.ndim)

    ins = (grad_pre, w_self, keep, come, pushed)
    return pl.pallas_call(
        base_kernel,
        grid_spec=pltpu.PrefetchScalarGridSpec(
            num_scalar_prefetch=1,
            grid=(1,),
            in_specs=[whole(x) for x in ins],
            out_specs=pl.BlockSpec((rows, width), lambda i, *s: (0, 0)),
        ),
        out_shape=jax.ShapeDtypeStruct((rows, width), F32),
        compiler_params=params(),
        cost_estimate=cost(4 * rows * width * width, 12 * rows * width),
        name="base",
    )(places, *ins)


def power(size):
    return size & (size - 1) == 0


def target(i, k, size):
    return i ^ k if power(size) else lax.rem(i + k, size)


def source(i, k, size):
    return i ^ k if power(size) else lax.rem(i + size - k, size)


def to_peer(x, axis, k):
    size = lax.axis_size(axis)
    return lax.ppermute(x, axis, [(i, i ^ k if power(size) else (i + k) % size) for i in range(size)])


def tree_sum(parts):
    while len(parts) > 1:
        pairs = [a + b for a, b in zip(parts[::2], parts[1::2])]
        parts = pairs + parts[len(pairs) * 2 :]
    return parts[0]


def shards(
    features,
    band_tiles,
    band_cols,
    off_tiles,
    req_block,
    req_row,
    req_valid,
    weight_self,
    weight_neigh,
    bias_term,
    cotangent,
):
    row_count, width = features.shape
    n = lax.axis_size("narrow")
    wide = lax.axis_size("wide")
    steps = n // 2
    fold = [0] + list(range(1, steps, 2)) + list(range(2, steps, 2))[::-1]
    after = {a: b for a, b in zip(fold, fold[1:] + fold[:1])}

    def onward(x):
        return lax.ppermute(x, "narrow", [(i, after[i // 2] * 2 + i % 2) for i in range(n)])

    def swap(x):
        return to_peer(x, "narrow", 1)

    me = lax.axis_index("narrow")
    here = lax.axis_index("wide")
    chips = jnp.array(
        [[fold[(fold.index(z) - s) % steps] for s in range(steps)] for z in range(steps)], jnp.int32
    )[me // 2]
    ids = jnp.concatenate([(me % 2)[None].astype(jnp.int32), chips])
    cols = band_cols.reshape(-1)
    asked, row, valid = req_block[0], req_row[0], req_valid[0]
    sources = jnp.stack([source(here, k, wide) for k in range(wide)])
    asked_by = jnp.concatenate([asked, asked[sources]])

    own, sib = features, swap(features)
    by_peer = [features] + [to_peer(features, "wide", k) for k in range(1, wide)]
    tiles, turned, degree = prep(band_tiles)
    acc = None
    for s in range(steps - 1):
        following = onward(own)
        acc = pull(ids, cols, tiles, own, sib, acc, s)
        own = following
        sib = swap(own)
    acc, degree = off_band(asked_by, row, valid, off_tiles, by_peer, acc, degree)
    layer_out, grad_pre, aggregate, signal, keep, send = middle(
        ids, cols, tiles, turned, own, sib, acc, degree, features, cotangent,
        weight_self, weight_neigh, bias_term.reshape(1, -1), steps,
    )

    going = (keep.astype(F32) + swap(send).astype(F32)).astype(BF16)
    keeps, sends = push(ids, cols, signal, turned, steps)
    come = swap(sends)
    for s in range(steps - 2):
        got = onward(going)
        going = (got.astype(F32) + (keeps[s].astype(F32) + come[s].astype(F32))).astype(BF16)
    got = onward(going)

    msgs = messages(asked, row, valid, off_tiles, signal, features, aggregate, grad_pre)
    arrived = [msgs[0]] + [to_peer(msgs[k], "wide", k) for k in range(1, wide)]
    places = jnp.stack([a[BLK, 0] for a in arrived]).astype(jnp.int32)
    pushed = jnp.stack([a[:BLK] for a in arrived])
    rest = base(places, grad_pre, weight_self, keeps[-1], come[-1], pushed)
    grad_features = rest + got.astype(F32)

    def grads_of(a):
        g = a[BLK + 16 :].reshape(2, 2, 2, BLK, BLK).astype(F32)
        g = (g[:, 0] + g[:, 1]).transpose(0, 2, 1, 3).reshape(2, BLK, 2 * BLK)
        e = a[BLK + 1 : BLK + 5].astype(F32)
        e = (e[:2] + e[2:]).reshape(1, 1, 2 * BLK)
        e = jnp.concatenate([e, jnp.zeros((1, 1, 2 * BLK), F32)], axis=0)
        e = jnp.concatenate([e, jnp.zeros((2, 7, 2 * BLK), F32)], axis=1)
        return jnp.concatenate([g, e], axis=1)

    sums = tree_sum([grads_of(a) for a in arrived])
    core = me % 2
    mine = lax.dynamic_index_in_dim(sums, core, 0, keepdims=False)
    other = lax.dynamic_index_in_dim(sums, 1 - core, 0, keepdims=False)
    total = mine + swap(other)
    if power(steps):
        k = 1
        while k < steps:
            total = total + to_peer(total, "narrow", 2 * k)
            k *= 2
    else:
        total = lax.psum(total, "narrow", axis_index_groups=[list(range(c, n, 2)) for c in (0, 1)])
    total = total * ((wide * n * row_count) ** (-0.5))
    paired = swap(total)
    first = jnp.where(core == 0, total, paired)
    second = jnp.where(core == 0, paired, total)
    return layer_out, grad_features, first[:BLK], second[:BLK], first[BLK]


def solution(mesh):
    both = ("wide", "narrow")
    placed = (
        P(both, None),
        P(both, None, None, None),
        P(both, None),
        P(both, None, None, None),
        P(both, None),
        P(both, None),
        P(both, None),
        P(),
        P(),
        P(),
        P(both, None),
    )
    return jax.shard_map(
        shards,
        mesh=mesh,
        in_specs=placed,
        out_specs=(P(both, None), P(both, None), P(), P(), P()),
        check_vma=False,
    )
```

time: 372 us -> 190 us (0.51)
  waiting for transfers between devices: 238 us -> 65.6 us
  matrix products: 39.9 us -> 0 us
  Pallas kernels: 0 us -> 38.7 us
  blocking collectives: 37 us -> 0 us
  local copies, waits for them, and re-layouts: 25.4 us -> 45.9 us
  starting transfers between devices: 0.69 us -> 20 us
  between operations: 14 us -> 1.06 us
    reduce_scatter x2 -> x0, waiting for transfers between devices: 87 us -> none  [the longest x1 52.3 us: shards(): lax.psum_scatter(placed.reshape(slab_count * row_count, in_width).astype(...]
    psum x1 -> x0, waiting for transfers between devices: 54.5 us -> none  [shards(): lax.psum((local_self, local_neigh, local_bias), ('wide', 'narrow'))]
    dot_general x20 -> x0, matrix products: 39.9 us -> none  [the longest x8 11.4 us: band_add(): jnp.einsum('bij,bjf->bif', tiles_now, picked, preferred_element_type=jnp....]
    pallas_call x0 -> x9, Pallas kernels: none -> 38.7 us  [the longest x1 12 us: prep(): pl.pallas_call(prep_kernel, grid=(g,), in_specs=[tile_spec], out_specs=[t...]
    psum x1 -> x0, blocking collectives: 37 us -> none  [shards(): lax.psum((local_self, local_neigh, local_bias), ('wide', 'narrow'))]
    all_gather x1 -> x0, waiting for transfers between devices: 23 us -> none  [shards(): lax.all_gather(features, 'wide', axis=0, tiled=True)]
    ppermute x7 -> x22, starting transfers between devices: 0.35 us -> 20 us  [the longest x16 12.7 us: to_peer(): lax.ppermute(x, axis, [(i, i ^ k if power(size) else (i + k) % size) for...]
    unnamed x21 -> x53, local copies, waits for them, and re-layouts: 4.56 us -> 19.3 us
  transfers between devices with their start and end apart: 11 -> 22, of which waited for: 11 -> 8; matrix products, arithmetic and copies ran while one was open for 13% -> 28% of each run, Pallas kernels for 0% -> 13%
where the time goes in v1:
time: 190 us; the launch traced here: 188 us
  waiting for transfers between devices  65.6 us (35%)
  local copies, waits for them, and re-layouts  45.9 us (24%)
  Pallas kernels  38.7 us (20%)
  starting transfers between devices  20 us (11%)
  other arithmetic  16.5 us (9%)
    ppermute x6, waiting for transfers between devices, onward(): lax.ppermute(x, 'narrow', [(i, after[i // 2] * 2 + i % 2) for i in range(...  52.4 us
    unnamed x53, local copies, waits for them, and re-layouts  19.3 us
    ppermute x16, waiting for transfers between devices, to_peer(): lax.ppermute(x, axis, [(i, i ^ k if power(size) else (i + k) % size) for...  13.2 us
    ppermute x16, starting transfers between devices, to_peer(): lax.ppermute(x, axis, [(i, i ^ k if power(size) else (i + k) % size) for...  12.7 us
    pallas_call x1, Pallas kernels, prep(): pl.pallas_call(prep_kernel, grid=(g,), in_specs=[tile_spec], out_specs=[t...  12 us
    pallas_call x3, Pallas kernels, pull(): pl.pallas_call(partial(pull_kernel, n=n, step=step, first=acc is None), g...  9.96 us
    pallas_call x1, Pallas kernels, middle(): pl.pallas_call(partial(middle_kernel, n=n, steps=steps), grid_spec=pltpu....  7.32 us
    ppermute x6, starting transfers between devices, onward(): lax.ppermute(x, 'narrow', [(i, after[i // 2] * 2 + i % 2) for i in range(...  7.3 us
  transfers between devices with their start and end apart: 22, of which 8 were waited for; matrix products, arithmetic and copies ran while one was open for 28% of the time, Pallas kernels for 13%

profile of v1, /device:TPU:0, one launch (start us, length us, event | category | flops | bytes accessed | tf_op | source)
XLA Modules:
  0.0 187.8 jit_solution(17199325539902606400)
XLA Ops:
  0.6 3.1 %collective-permute-start = (bf16[2048,128]{1,0:T(8,128)(2,1)}, bf16[2048,128]{1,0:T(8,128)(2,1)S(1)}, u32[]{:S(2)}, u32[]{:S(2)}) collective-permute-start(bf16[2048,128]{1,0:T(8,128)(2,1)} %feat_ref.3), channel_id=1, source_target_pairs={{0,2},{1,3},{2,6},{3,7},{4,0},{5,1},{6,4},{7,5},{8,10},{9,11},{10,... | collective-permute-start | bytes 1572872 | tf_op jit(solution)/shard_map/ppermute | solution.py:416
  3.7 13.1 %collective-permute-done.refs_1_ = bf16[2048,128]{1,0:T(8,128)(2,1)S(1)} collective-permute-done((bf16[2048,128]{1,0:T(8,128)(2,1)}, bf16[2048,128]{1,0:T(8,128)(2,1)S(1)}, u32[]{:S(2)}, u32[]{:S(2)}) %collective-permute-start) | collective-permute-done | bytes 524320 | tf_op jit(solution)/shard_map/ppermute | solution.py:416
  18.3 12.6 %collective-permute-done.1.refs_1_ = bf16[2048,128]{1,0:T(8,128)(2,1)S(1)} collective-permute-done((bf16[2048,128]{1,0:T(8,128)(2,1)S(1)}, bf16[2048,128]{1,0:T(8,128)(2,1)S(1)}, u32[]{:S(2)}, u32[]{:S(2)}) %collective-permute-start.1) | collective-permute-done | bytes 524320 | tf_op jit(solution)/shard_map/ppermute | solution.py:416
  35.7 8.3 %collective-permute-done.2.own_ref = bf16[2048,128]{1,0:T(8,128)(2,1)S(1)} collective-permute-done((bf16[2048,128]{1,0:T(8,128)(2,1)S(1)}, bf16[2048,128]{1,0:T(8,128)(2,1)S(1)}, u32[]{:S(2)}, u32[]{:S(2)}) %collective-permute-start.2) | collective-permute-done | bytes 524320 | tf_op jit(solution)/shard_map/ppermute | solution.py:416
  46.9 12.0 %prep.1 = (bf16[16,8,128,128]{3,2,1,0:T(8,128)(2,1)S(1)}, bf16[16,8,128,128]{3,2,1,0:T(8,128)(2,1)}, f32[2048,128]{1,0:T(8,128)S(1)}) custom-call(s32[16,8,128,128]{3,2,1,0:T(8,128)} %t_ref.1), custom_call_target="tpu_custom_call" | custom-call | flops 2097152 | bytes 16777216 | tf_op jit(solution)/shard_map/prep/pallas_call | solution.py:42
  58.9 2.0 %copy-done.1 = bf16[16,8,128,128]{3,2,1,0:T(8,128)(2,1)} copy-done((bf16[16,8,128,128]{3,2,1,0:T(8,128)(2,1)}, bf16[16,8,128,128]{3,2,1,0:T(8,128)(2,1)S(1)}, u32[]{:S(2)}) %copy-start.1) | copy-done | bytes 4194328
  62.7 3.2 %pull0.1.refs_3_ = f32[2048,128]{1,0:T(8,128)S(1)} custom-call(s32[5]{0:T(128)S(1)} %pad_add_fusion.ids, s32[128]{0:T(128)S(1)} %reshape.233.cols, bf16[16,8,128,128]{3,2,1,0:T(8,128)(2,1)} %copy-done.1, bf16[2048,128]{1,0:T(8,128)(2,1)S(1)} %copy-done.2, bf16[2048,128]{1,0:T(8,128)(2,1)S(1)} %copy-done.8), custom_call_target="tpu_custom_call" | custom-call | flops 134217728 | bytes 3145728 | tf_op jit(solution)/shard_map/pull0/pallas_call | solution.py:88
  65.9 3.4 %pull1.1.refs_3_ = f32[2048,128]{1,0:T(8,128)S(1)} custom-call(s32[5]{0:T(128)S(1)} %pad_add_fusion.ids, s32[128]{0:T(128)S(1)} %reshape.233.cols, bf16[16,8,128,128]{3,2,1,0:T(8,128)(2,1)} %copy-done.1, bf16[2048,128]{1,0:T(8,128)(2,1)S(1)} %collective-permute-done.refs_1_, bf16[2048,128]{1,0:T(8,128)(2,1)} %collective-permute-done.8.refs_2_, ...), custom_call_target="tpu_custom_call" | custom-call | flops 134217728 | bytes 3145728 | tf_op jit(solution)/shard_map/pull1/pallas_call | solution.py:88
  69.4 3.4 %pull2.1.refs_4_ = f32[2048,128]{1,0:T(8,128)S(1)} custom-call(s32[5]{0:T(128)S(1)} %pad_add_fusion.ids, s32[128]{0:T(128)S(1)} %reshape.233.cols, bf16[16,8,128,128]{3,2,1,0:T(8,128)(2,1)} %copy-done.1, bf16[2048,128]{1,0:T(8,128)(2,1)S(1)} %collective-permute-done.1.refs_1_, bf16[2048,128]{1,0:T(8,128)(2,1)} %collective-permute-done.7.refs_2_, ...), custom_call_target="tpu_custom_call" | custom-call | flops 134217728 | bytes 3145728 | tf_op jit(solution)/shard_map/pull2/pallas_call | solution.py:88
  72.8 2.1 %off_band.1 = (f32[2048,128]{1,0:T(8,128)S(1)}, f32[2048,128]{1,0:T(8,128)S(1)}) custom-call(s32[8]{0:T(128)S(1)} %pad_add_fusion.1.asked, s32[4]{0:T(128)S(1)} %bitcast.81, s32[4]{0:T(128)S(1)} %bitcast.83, s32[1,4,128,128]{3,2,1,0:T(8,128)S(1)} %copy-done.5, bf16[2048,128]{1,0:T(8,128)(2,1)S(1)} %copy-done.2, ...), custom_call_target="tpu_custom_call" | custom-call | flops 16777216 | bytes 4194304 | tf_op jit(solution)/shard_map/off_band/pallas_call | solution.py:127
  75.9 7.3 %middle.1 = (bf16[2048,256]{1,0:T(8,128)(2,1)}, bf16[2048,256]{1,0:T(8,128)(2,1)S(1)}, bf16[2048,128]{1,0:T(8,128)(2,1)S(1)}, bf16[2048,128]{1,0:T(8,128)(2,1)S(...) custom-call(s32[5]{0:T(128)S(1)} %pad_add_fusion.ids, s32[128]{0:T(128)S(1)} %reshape.233.cols, ...), custom_call_target="tpu_custom_call" | custom-call | flops 671088640 | bytes 7864320 | tf_op jit(solution)/shard_map/middle/pallas_call | solution.py:211
  86.3 5.3 %push.1 = (bf16[3,2048,128]{2,1,0:T(8,128)(2,1)S(1)}, bf16[3,2048,128]{2,1,0:T(8,128)(2,1)}) custom-call(s32[5]{0:T(128)S(1)} %pad_add_fusion.ids, s32[128]{0:T(128)S(1)} %reshape.233.cols, bf16[2048,128]{1,0:T(8,128)(2,1)S(1)} %get-tuple-element.24.sig_ref, bf16[16,8,128,128]{3,2,1,0:T(8,128)(2,1)} %get-tuple-element.22.turned_ref), custom_call_target="tpu_custom_call" | custom-call | flops 402653184 | bytes 6291456 | tf_op jit(solution)/shard_map/push/pallas_call | solution.py:254
  91.5 1.9 collective-permute-start.12
  97.0 1.8 copy.47
  106.0 1.8 copy.53
  115.9 1.8 copy.48
  129.6 2.1 %add_convert_fusion = bf16[2048,128]{1,0:T(8,128)(2,1)} fusion(bf16[2048,128]{1,0:T(8,128)(2,1)} %collective-permute-done.14, bf16[2048,128]{1,0:T(8,128)(2,1)} %copy-done.6), kind=kLoop, calls=%fused_computation.6 | loop fusion | flops 1048576 | bytes 1572864 | tf_op jit(solution)/shard_map/convert_element_type | solution.py:447
  138.6 3.4 %collective-permute-start.19 = (f32[136,256]{1,0:T(8,128)S(1)}, f32[136,256]{1,0:T(8,128)S(1)}, u32[]{:S(2)}, u32[]{:S(2)}) collective-permute-start(f32[136,256]{1,0:T(8,128)S(1)} %bitcast_add_fusion.2), channel_id=1, source_target_pairs={{0,2},{1,3},{2,0},{3,1},{4,6},{5,7},{6,4},{7,5},{8,10},{9,11},{10,... | collective-permute-start | bytes 417800 | tf_op jit(solution)/shard_map/ppermute | solution.py:385
  142.8 7.3 %collective-permute-done.19 = f32[136,256]{1,0:T(8,128)S(1)} collective-permute-done((f32[136,256]{1,0:T(8,128)S(1)}, f32[136,256]{1,0:T(8,128)S(1)}, u32[]{:S(2)}, u32[]{:S(2)}) %collective-permute-start.19) | collective-permute-done | bytes 139296 | tf_op jit(solution)/shard_map/ppermute | solution.py:385
  152.8 2.5 %collective-permute-start.16 = (bf16[2048,128]{1,0:T(8,128)(2,1)S(1)}, bf16[2048,128]{1,0:T(8,128)(2,1)S(1)}, u32[]{:S(2)}, u32[]{:S(2)}) collective-permute-start(bf16[2048,128]{1,0:T(8,128)(2,1)S(1)} %fusion.1), channel_id=1, source_target_pairs={{0,2},{1,3},{2,6},{3,7},{4,0},{5,1},{6,4},{7,5},{8,10},{9,11},{10,... | collective-permute-start | bytes 1572872 | tf_op jit(solution)/shard_map/ppermute | solution.py:416
  155.3 4.9 %collective-permute-done.20 = f32[136,256]{1,0:T(8,128)S(1)} collective-permute-done((f32[136,256]{1,0:T(8,128)S(1)}, f32[136,256]{1,0:T(8,128)S(1)}, u32[]{:S(2)}, u32[]{:S(2)}) %collective-permute-start.20) | collective-permute-done | bytes 139296 | tf_op jit(solution)/shard_map/ppermute | solution.py:385
  160.3 2.6 %maximum_convert_fusion.places = s32[4]{0:T(128)S(1)} fusion(bf16[1]{0:T(256)(128)(2,1)} %bitcast.17, bf16[1]{0:T(256)(128)(2,1)} %bitcast.15, bf16[1]{0:T(256)(128)(2,1)} %bitcast.13, bf16[1]{0:T(256)(128)(2,1)} %bitcast.11), kind=kLoop, calls=%fused_computation.52 | loop fusion | flops 32 | bytes 24 | tf_op jit(solution)/shard_map/convert_element_type | solution.py:457
  163.0 8.0 %collective-permute-done.16 = bf16[2048,128]{1,0:T(8,128)(2,1)S(1)} collective-permute-done((bf16[2048,128]{1,0:T(8,128)(2,1)S(1)}, bf16[2048,128]{1,0:T(8,128)(2,1)S(1)}, u32[]{:S(2)}, u32[]{:S(2)}) %collective-permute-start.16) | collective-permute-done | bytes 524320 | tf_op jit(solution)/shard_map/ppermute | solution.py:416
  176.3 10.4 %collective-permute-done.17 = bf16[2048,128]{1,0:T(8,128)(2,1)S(1)} collective-permute-done((bf16[2048,128]{1,0:T(8,128)(2,1)S(1)}, bf16[2048,128]{1,0:T(8,128)(2,1)S(1)}, u32[]{:S(2)}, u32[]{:S(2)}) %collective-permute-start.17) | collective-permute-done | bytes 524320 | tf_op jit(solution)/shard_map/ppermute | solution.py:416
  (144 shorter events, 62.4 us)
Async XLA Ops:
  0.6 16.2 %collective-permute-start = (bf16[2048,128]{1,0:T(8,128)(2,1)}, bf16[2048,128]{1,0:T(8,128)(2,1)S(1)}, u32[]{:S(2)}, u32[]{:S(2)}) collective-permute-start(bf16[2048,128]{1,0:T(8,128)(2,1)} %feat_ref.3), channel_id=1, source_target_pairs={{0,2},{1,3},{2,6},{3,7},{4,0},{5,1},{6,4},{7,5},{8,10},{9,11},{10,... | collective-permute-start | bytes 1572872 | tf_op jit(solution)/shard_map/ppermute | solution.py:416
  16.9 14.0 %collective-permute-start.1 = (bf16[2048,128]{1,0:T(8,128)(2,1)S(1)}, bf16[2048,128]{1,0:T(8,128)(2,1)S(1)}, u32[]{:S(2)}, u32[]{:S(2)}) collective-permute-start(bf16[2048,128]{1,0:T(8,128)(2,1)S(1)} %collective-permute-done.refs_1_), channel_id=1, source_target_pairs={{0,2},{1,3},{2,6},{3,7},{4,0},{5,1},{6,4},{7,5},{8,10},{9,11},{10,... | collective-permute-start | bytes 1572872 | tf_op jit(solution)/shard_map/ppermute | solution.py:416
  17.8 16.6 %collective-permute-start.9 = (bf16[2048,128]{1,0:T(8,128)(2,1)}, bf16[2048,128]{1,0:T(8,128)(2,1)S(1)}, u32[]{:S(2)}, u32[]{:S(2)}) collective-permute-start(bf16[2048,128]{1,0:T(8,128)(2,1)} %feat_ref.3), channel_id=1, source_target_pairs={{0,1},{1,0},{2,3},{3,2},{4,5},{5,4},{6,7},{7,6},{8,9},{9,8},{10,11... | collective-permute-start | bytes 1572872 | tf_op jit(solution)/shard_map/ppermute | solution.py:385
  17.8 17.9 %collective-permute-start.8 = (bf16[2048,128]{1,0:T(8,128)(2,1)S(1)}, bf16[2048,128]{1,0:T(8,128)(2,1)}, u32[]{:S(2)}, u32[]{:S(2)}) collective-permute-start(bf16[2048,128]{1,0:T(8,128)(2,1)S(1)} %collective-permute-done.refs_1_), channel_id=1, source_target_pairs={{0,1},{1,0},{2,3},{3,2},{4,5},{5,4},{6,7},{7,6},{8,9},{9,8},{10,11... | collective-permute-start | bytes 1572872 | tf_op jit(solution)/shard_map/ppermute | solution.py:385
  30.9 13.1 %collective-permute-start.2 = (bf16[2048,128]{1,0:T(8,128)(2,1)S(1)}, bf16[2048,128]{1,0:T(8,128)(2,1)S(1)}, u32[]{:S(2)}, u32[]{:S(2)}) collective-permute-start(bf16[2048,128]{1,0:T(8,128)(2,1)S(1)} %collective-permute-done.1.refs_1_), channel_id=1, source_target_pairs={{0,2},{1,3},{2,6},{3,7},{4,0},{5,1},{6,4},{7,5},{8,10},{9,11},{10,... | collective-permute-start | bytes 1572872 | tf_op jit(solution)/shard_map/ppermute | solution.py:416
  31.4 41.4 %collective-permute-start.4 = (bf16[2048,128]{1,0:T(8,128)(2,1)}, bf16[2048,128]{1,0:T(8,128)(2,1)S(1)}, u32[]{:S(2)}, u32[]{:S(2)}) collective-permute-start(bf16[2048,128]{1,0:T(8,128)(2,1)} %feat_ref.3), channel_id=1, source_target_pairs={{0,8},{8,0},{16,24},{24,16},{1,9},{9,1},{17,25},{25,17},{2,10},{10... | collective-permute-start | bytes 1572872 | tf_op jit(solution)/shard_map/ppermute | solution.py:385
  32.9 39.9 %collective-permute-start.5 = (bf16[2048,128]{1,0:T(8,128)(2,1)}, bf16[2048,128]{1,0:T(8,128)(2,1)S(1)}, u32[]{:S(2)}, u32[]{:S(2)}) collective-permute-start(bf16[2048,128]{1,0:T(8,128)(2,1)} %feat_ref.3), channel_id=1, source_target_pairs={{0,16},{8,24},{16,0},{24,8},{1,17},{9,25},{17,1},{25,9},{2,18},{10... | collective-permute-start | bytes 1572872 | tf_op jit(solution)/shard_map/ppermute | solution.py:385
  35.2 37.6 %collective-permute-start.6 = (bf16[2048,128]{1,0:T(8,128)(2,1)}, bf16[2048,128]{1,0:T(8,128)(2,1)}, u32[]{:S(2)}, u32[]{:S(2)}) collective-permute-start(bf16[2048,128]{1,0:T(8,128)(2,1)} %feat_ref.3), channel_id=1, source_target_pairs={{0,24},{8,16},{16,8},{24,0},{1,25},{9,17},{17,9},{25,1},{2,26},{10... | collective-permute-start | bytes 1572872 | tf_op jit(solution)/shard_map/ppermute | solution.py:385
  35.7 33.7 %collective-permute-start.7 = (bf16[2048,128]{1,0:T(8,128)(2,1)S(1)}, bf16[2048,128]{1,0:T(8,128)(2,1)}, u32[]{:S(2)}, u32[]{:S(2)}) collective-permute-start(bf16[2048,128]{1,0:T(8,128)(2,1)S(1)} %collective-permute-done.1.refs_1_), channel_id=1, source_target_pairs={{0,1},{1,0},{2,3},{3,2},{4,5},{5,4},{6,7},{7,6},{8,9},{9,8},{10,11... | collective-permute-start | bytes 1572872 | tf_op jit(solution)/shard_map/ppermute | solution.py:385
  44.0 32.0 %collective-permute-start.3 = (bf16[2048,128]{1,0:T(8,128)(2,1)S(1)}, bf16[2048,128]{1,0:T(8,128)(2,1)S(1)}, u32[]{:S(2)}, u32[]{:S(2)}) collective-permute-start(bf16[2048,128]{1,0:T(8,128)(2,1)S(1)} %collective-permute-done.2.own_ref), channel_id=1, source_target_pairs={{0,1},{1,0},{2,3},{3,2},{4,5},{5,4},{6,7},{7,6},{8,9},{9,8},{10,11... | collective-permute-start | bytes 1572872 | tf_op jit(solution)/shard_map/ppermute | solution.py:385
  46.9 15.8 %copy-start.8 = (bf16[2048,128]{1,0:T(8,128)(2,1)S(1)}, bf16[2048,128]{1,0:T(8,128)(2,1)}, u32[]{:S(2)}) copy-start(bf16[2048,128]{1,0:T(8,128)(2,1)} %copy-done.7) | copy-start | bytes 1572868
  91.5 11.5 %collective-permute-start.12 = (bf16[1168,128]{1,0:T(8,128)(2,1)}, bf16[1168,128]{1,0:T(8,128)(2,1)}, u32[]{:S(2)}, u32[]{:S(2)}) collective-permute-start(bf16[1168,128]{1,0:T(8,128)(2,1)} %get-tuple-element.32), channel_id=1, source_target_pairs={{0,24},{8,16},{16,8},{24,0},{1,25},{9,17},{17,9},{25,1},{2,26},{10... | collective-permute-start | bytes 897032 | tf_op jit(solution)/shard_map/ppermute | solution.py:385
  93.4 15.3 %collective-permute-start.11 = (bf16[1168,128]{1,0:T(8,128)(2,1)}, bf16[1168,128]{1,0:T(8,128)(2,1)}, u32[]{:S(2)}, u32[]{:S(2)}) collective-permute-start(bf16[1168,128]{1,0:T(8,128)(2,1)} %get-tuple-element.33), channel_id=1, source_target_pairs={{0,16},{8,24},{16,0},{24,8},{1,17},{9,25},{17,1},{25,9},{2,18},{10... | collective-permute-start | bytes 897032 | tf_op jit(solution)/shard_map/ppermute | solution.py:385
  93.9 20.2 %collective-permute-start.10 = (bf16[1168,128]{1,0:T(8,128)(2,1)}, bf16[1168,128]{1,0:T(8,128)(2,1)}, u32[]{:S(2)}, u32[]{:S(2)}) collective-permute-start(bf16[1168,128]{1,0:T(8,128)(2,1)} %get-tuple-element.34), channel_id=1, source_target_pairs={{0,8},{8,0},{16,24},{24,16},{1,9},{9,1},{17,25},{25,17},{2,10},{10... | collective-permute-start | bytes 897032 | tf_op jit(solution)/shard_map/ppermute | solution.py:385
  95.9 55.5 %collective-permute-start.13 = (bf16[3,2048,128]{2,1,0:T(8,128)(2,1)}, bf16[3,2048,128]{2,1,0:T(8,128)(2,1)}, u32[]{:S(2)}, u32[]{:S(2)}) collective-permute-start(bf16[3,2048,128]{2,1,0:T(8,128)(2,1)} %get-tuple-element.28), channel_id=1, source_target_pairs={{0,1},{1,0},{2,3},{3,2},{4,5},{5,4},{6,7},{7,6},{8,9},{9,8},{10,11... | collective-permute-start | bytes 4718600 | tf_op jit(solution)/shard_map/ppermute | solution.py:385
  99.6 30.0 %collective-permute-start.14 = (bf16[2048,128]{1,0:T(8,128)(2,1)}, bf16[2048,128]{1,0:T(8,128)(2,1)}, u32[]{:S(2)}, u32[]{:S(2)}) collective-permute-start(bf16[2048,128]{1,0:T(8,128)(2,1)} %copy-done.13), channel_id=1, source_target_pairs={{0,1},{1,0},{2,3},{3,2},{4,5},{5,4},{6,7},{7,6},{8,9},{9,8},{10,11... | collective-permute-start | bytes 1572872 | tf_op jit(solution)/shard_map/ppermute | solution.py:385
  128.8 8.8 %collective-permute-start.18 = (f32[136,256]{1,0:T(8,128)}, f32[136,256]{1,0:T(8,128)}, u32[]{:S(2)}, u32[]{:S(2)}) collective-permute-start(f32[136,256]{1,0:T(8,128)} %bitcast.93), channel_id=1, source_target_pairs={{0,1},{1,0},{2,3},{3,2},{4,5},{5,4},{6,7},{7,6},{8,9},{9,8},{10,11... | collective-permute-start | bytes 417800 | tf_op jit(solution)/shard_map/ppermute | solution.py:385
  131.8 19.6 %collective-permute-start.15 = (bf16[2048,128]{1,0:T(8,128)(2,1)}, bf16[2048,128]{1,0:T(8,128)(2,1)}, u32[]{:S(2)}, u32[]{:S(2)}) collective-permute-start(bf16[2048,128]{1,0:T(8,128)(2,1)} %add_convert_fusion), channel_id=1, source_target_pairs={{0,2},{1,3},{2,6},{3,7},{4,0},{5,1},{6,4},{7,5},{8,10},{9,11},{10,... | collective-permute-start | bytes 1572872 | tf_op jit(solution)/shard_map/ppermute | solution.py:416
  138.6 24.3 %copy-start.21 = (bf16[1,128,128]{2,1,0:T(8,128)(2,1)S(1)}, bf16[1,128,128]{2,1,0:T(8,128)(2,1)}, u32[]{:S(2)}) copy-start(bf16[1,128,128]{2,1,0:T(8,128)(2,1)} %slice_bitcast_fusion.7) | copy-start | bytes 98308
  138.6 11.5 %collective-permute-start.19 = (f32[136,256]{1,0:T(8,128)S(1)}, f32[136,256]{1,0:T(8,128)S(1)}, u32[]{:S(2)}, u32[]{:S(2)}) collective-permute-start(f32[136,256]{1,0:T(8,128)S(1)} %bitcast_add_fusion.2), channel_id=1, source_target_pairs={{0,2},{1,3},{2,0},{3,1},{4,6},{5,7},{6,4},{7,5},{8,10},{9,11},{10,... | collective-permute-start | bytes 417800 | tf_op jit(solution)/shard_map/ppermute | solution.py:385
  150.2 10.0 %collective-permute-start.20 = (f32[136,256]{1,0:T(8,128)S(1)}, f32[136,256]{1,0:T(8,128)S(1)}, u32[]{:S(2)}, u32[]{:S(2)}) collective-permute-start(f32[136,256]{1,0:T(8,128)S(1)} %add.143), channel_id=1, source_target_pairs={{0,4},{1,5},{2,6},{3,7},{4,0},{5,1},{6,2},{7,3},{8,12},{9,13},{10,... | collective-permute-start | bytes 417800 | tf_op jit(solution)/shard_map/ppermute | solution.py:385
  152.8 18.2 %collective-permute-start.16 = (bf16[2048,128]{1,0:T(8,128)(2,1)S(1)}, bf16[2048,128]{1,0:T(8,128)(2,1)S(1)}, u32[]{:S(2)}, u32[]{:S(2)}) collective-permute-start(bf16[2048,128]{1,0:T(8,128)(2,1)S(1)} %fusion.1), channel_id=1, source_target_pairs={{0,2},{1,3},{2,6},{3,7},{4,0},{5,1},{6,4},{7,5},{8,10},{9,11},{10,... | collective-permute-start | bytes 1572872 | tf_op jit(solution)/shard_map/ppermute | solution.py:416
  160.2 2.7 %collective-permute-start.21 = (f32[136,256]{1,0:T(8,128)S(1)}, f32[136,256]{1,0:T(8,128)S(1)}, u32[]{:S(2)}, u32[]{:S(2)}) collective-permute-start(f32[136,256]{1,0:T(8,128)S(1)} %add_multiply_fusion), channel_id=1, source_target_pairs={{0,1},{1,0},{2,3},{3,2},{4,5},{5,4},{6,7},{7,6},{8,9},{9,8},{10,11... | collective-permute-start | bytes 417800 | tf_op jit(solution)/shard_map/ppermute | solution.py:385
  172.3 14.5 %collective-permute-start.17 = (bf16[2048,128]{1,0:T(8,128)(2,1)S(1)}, bf16[2048,128]{1,0:T(8,128)(2,1)S(1)}, u32[]{:S(2)}, u32[]{:S(2)}) collective-permute-start(bf16[2048,128]{1,0:T(8,128)(2,1)S(1)} %fusion), channel_id=1, source_target_pairs={{0,2},{1,3},{2,6},{3,7},{4,0},{5,1},{6,4},{7,5},{8,10},{9,11},{10,... | collective-permute-start | bytes 1572872 | tf_op jit(solution)/shard_map/ppermute | solution.py:416
  (20 other events, 69.7 us)

commit v2 on v1

v2 whole, which is shorter than its diff:
```python
from functools import partial

import jax
import jax.numpy as jnp
from jax import lax
from jax.experimental import pallas as pl
from jax.experimental.pallas import tpu as pltpu
from jax.sharding import PartitionSpec as P

F32 = jnp.float32
BF16 = jnp.bfloat16
BLK = 128
ROWS_PER = 4
CHUNKS = 2
VMEM = 20 * 1024 * 1024


def mm(a, b, lhs=1, rhs=0):
    return lax.dot_general(a, b, (((lhs,), (rhs,)), ((), ())), preferred_element_type=F32)


def params():
    return pltpu.CompilerParams(vmem_limit_bytes=VMEM)


def cost(flops, nbytes, trans=0):
    return pl.CostEstimate(flops=flops, bytes_accessed=nbytes, transcendentals=trans)


def prep_kernel(t_ref, plain_ref, deg_ref):
    total = jnp.zeros((BLK, BLK), F32)
    for k in range(t_ref.shape[1]):
        t = t_ref[0, k].astype(F32)
        total = total + t
        plain_ref[0, k] = t.astype(BF16)
    deg_ref[...] = jnp.broadcast_to(jnp.sum(total, axis=1, keepdims=True), (BLK, BLK))


def prep(tiles):
    g, n = tiles.shape[:2]
    tile_spec = pl.BlockSpec((1, n, BLK, BLK), lambda i: (i, 0, 0, 0))
    return pl.pallas_call(
        prep_kernel,
        grid=(g,),
        in_specs=[tile_spec],
        out_specs=[tile_spec, pl.BlockSpec((BLK, BLK), lambda i: (i, 0))],
        out_shape=[
            jax.ShapeDtypeStruct(tiles.shape, BF16),
            jax.ShapeDtypeStruct((g * BLK, BLK), F32),
        ],
        compiler_params=params(),
        cost_estimate=cost(tiles.size, tiles.size * 8),
        name="prep",
    )(tiles)


def block(ref, index):
    return ref[pl.ds(pl.multiple_of(index * BLK, BLK), BLK), :]


def pull_sum(ids, cols, tiles_ref, slabs_ref, b, g, n, step):
    core, chip = ids[0], ids[1 + step]
    own = block(slabs_ref.at[0], cols[g * n + chip * 2 + core])
    sib = block(slabs_ref.at[1], cols[g * n + chip * 2 + 1 - core])
    return mm(tiles_ref[b, core], own) + mm(tiles_ref[b, 1 - core], sib)


def lay_out(parts, slabs_ref):
    tall = parts[0].shape[0]
    for j, part in enumerate(parts):
        half, at = divmod(j, len(parts) // 2)
        slabs_ref[half, pl.ds(at * tall, tall), :] = part[...]


def pull_kernel(ids, cols, tiles_ref, *refs, n, step, first):
    if first:
        *parts, out_ref, slabs_ref = refs
    else:
        *parts, acc_ref, out_ref, slabs_ref = refs
    lay_out(parts, slabs_ref)
    for g in range(tiles_ref.shape[0]):
        rows = pl.ds(g * BLK, BLK)
        part = pull_sum(ids, cols, tiles_ref, slabs_ref, g, g, n, step)
        out_ref[rows, :] = part if first else acc_ref[rows, :] + part


def pull(ids, cols, tiles, own, sib, acc, step):
    g, n = tiles.shape[:2]
    width = own[0].shape[1]
    rows = g * BLK
    whole = pl.BlockSpec((rows, width), lambda i, ids, cols: (0, 0))
    chunk = pl.BlockSpec(own[0].shape, lambda i, ids, cols: (0, 0))
    pair = pl.BlockSpec((g, 2, BLK, BLK), lambda i, ids, cols: (0, ids[1 + step], 0, 0))
    more = () if acc is None else (acc,)
    return pl.pallas_call(
        partial(pull_kernel, n=n, step=step, first=acc is None),
        grid_spec=pltpu.PrefetchScalarGridSpec(
            num_scalar_prefetch=2,
            grid=(1,),
            in_specs=[pair] + [chunk] * (len(own) + len(sib)) + [whole] * len(more),
            out_specs=whole,
            scratch_shapes=[pltpu.VMEM((2, rows, width), BF16)],
        ),
        out_shape=jax.ShapeDtypeStruct((rows, width), F32),
        compiler_params=params(),
        cost_estimate=cost(4 * rows * BLK * width, 12 * rows * width),
        name=f"pull{step}",
    )(ids, cols, tiles, *own, *sib, *more)


def off_kernel(here_ref, asked, row, valid, off_ref, *refs, wide):
    fetched, (acc_in, deg_in, acc_ref, deg_ref) = refs[:wide], refs[wide:]
    acc_ref[...] = acc_in[...]
    deg_ref[...] = deg_in[...]
    here = here_ref[0]
    for k in range(wide):
        src = source(here, k, wide)
        mask = off_ref[0, src].astype(F32) * valid[src].astype(F32)
        at = pl.ds(pl.multiple_of(row[src] * BLK, BLK), BLK)
        acc_ref[at, :] += mm(mask.astype(BF16), fetched[k][...])
        deg_ref[at, :] += jnp.broadcast_to(jnp.sum(mask, axis=1, keepdims=True), (BLK, BLK))


def off_band(here, asked, row, valid, off_tiles, by_peer, acc, deg):
    wide = len(by_peer)
    rows, width = acc.shape

    def spec_of(k):
        return pl.BlockSpec(
            (BLK, width), lambda i, here, asked, row, valid: (asked[source(here[0], k, wide)], 0)
        )

    full = pl.BlockSpec((rows, width), lambda i, *s: (0, 0))
    offs = pl.BlockSpec(off_tiles.shape, lambda i, *s: (0, 0, 0, 0))
    return pl.pallas_call(
        partial(off_kernel, wide=wide),
        grid_spec=pltpu.PrefetchScalarGridSpec(
            num_scalar_prefetch=4,
            grid=(1,),
            in_specs=[offs] + [spec_of(k) for k in range(wide)] + [full, full],
            out_specs=[full, full],
        ),
        out_shape=[jax.ShapeDtypeStruct((rows, width), F32)] * 2,
        compiler_params=params(),
        cost_estimate=cost(2 * wide * BLK**3, 16 * rows * width),
        name="off_band",
    )(here, asked, row, valid, off_tiles, *by_peer, acc, deg)


def place(cols, tile, signal_rows, place_ref, g, core, chip, n):
    for j in range(2):
        which = core if j == 0 else 1 - core
        at = pl.ds(pl.multiple_of(cols[g * n + chip * 2 + which] * BLK, BLK), BLK)
        place_ref[j, at, :] += mm(tile(which), signal_rows, 0, 0)


def middle_kernel(
    ids, cols, tiles_ref, acc_ref, deg_ref, feat_ref, cot_ref,
    wself_ref, wneigh_ref, bias_ref, going_ref, *refs, n, steps,
):
    *parts, out_ref, gp_ref, agg_ref, sig_ref, keep_ref, send_ref, place_ref, slabs_ref = refs
    i = pl.program_id(0)

    @pl.when(i == 0)
    def _():
        place_ref[...] = jnp.zeros_like(place_ref)
        lay_out(parts, slabs_ref)

    inverse = 1.0 / (deg_ref[...] + 1.0)
    sums = [
        pull_sum(ids, cols, tiles_ref, slabs_ref, b, i * ROWS_PER + b, n, steps - 1)
        for b in range(ROWS_PER)
    ]
    gathered = acc_ref[...] + jnp.concatenate(sums, axis=0)
    aggregate = (gathered * inverse).astype(BF16)
    agg_ref[...] = aggregate
    pre = mm(feat_ref[...], wself_ref[...]) + mm(aggregate, wneigh_ref[...])
    pre = pre + bias_ref[...].astype(F32)
    slope = 0.7978845608028654
    square = pre * pre
    bent = jnp.tanh(slope * (pre + 0.044715 * (square * pre)))
    half = 0.5 * (1.0 + bent)
    out_ref[...] = (pre * half).astype(BF16)
    deriv = half + (0.5 * pre) * (1.0 - bent * bent) * (slope + (3 * 0.044715 * slope) * square)
    grad_pre = (cot_ref[...].astype(F32) * deriv).astype(BF16)
    gp_ref[...] = grad_pre
    signal = (mm(grad_pre, wneigh_ref[...], 1, 1) * inverse).astype(BF16)
    sig_ref[...] = signal
    core, chip = ids[0], ids[2]
    for b in range(ROWS_PER):
        place(
            cols, lambda which, b=b: going_ref[b, which], signal[b * BLK : (b + 1) * BLK],
            place_ref, i * ROWS_PER + b, core, chip, n,
        )

    @pl.when(i == pl.num_programs(0) - 1)
    def _():
        keep_ref[...] = place_ref[0].astype(BF16)
        send_ref[...] = place_ref[1].astype(BF16)


def middle(ids, cols, tiles, own, sib, acc, deg, features, cot, w_self, w_neigh, bias, steps):
    g, n = tiles.shape[:2]
    rows, width = features.shape
    outw = w_self.shape[1]
    tall = ROWS_PER * BLK

    def whole(r, c):
        return pl.BlockSpec((r, c), lambda i, ids, cols: (0, 0))

    def part(c):
        return pl.BlockSpec((tall, c), lambda i, ids, cols: (i, 0))

    def pair(at):
        return pl.BlockSpec((ROWS_PER, 2, BLK, BLK), lambda i, ids, cols: (i, ids[at], 0, 0))

    def shape(c, t):
        return jax.ShapeDtypeStruct((rows, c), t)

    return pl.pallas_call(
        partial(middle_kernel, n=n, steps=steps),
        grid_spec=pltpu.PrefetchScalarGridSpec(
            num_scalar_prefetch=2,
            grid=(g // ROWS_PER,),
            in_specs=[
                pair(steps), part(width), part(width), part(width), part(outw),
                whole(width, outw), whole(width, outw), whole(1, outw), pair(2),
            ]
            + [whole(*x.shape) for x in (*own, *sib)],
            out_specs=[
                part(outw), part(outw), part(width), part(width),
                whole(rows, width), whole(rows, width),
            ],
            scratch_shapes=[
                pltpu.VMEM((2, rows, width), F32),
                pltpu.VMEM((2, rows, width), BF16),
            ],
        ),
        out_shape=[
            shape(outw, BF16), shape(outw, BF16), shape(width, BF16), shape(width, BF16),
            shape(width, BF16), shape(width, BF16),
        ],
        compiler_params=params(),
        cost_estimate=cost(8 * rows * BLK * width + 6 * rows * width * outw, 30 * rows * width, rows * outw),
        name="middle",
    )(ids, cols, tiles, acc, deg, features, cot, w_self, w_neigh, bias, tiles, *own, *sib)


def push_kernel(ids, cols, sig_ref, tiles_ref, keep_ref, send_ref, place_ref, *, n, steps):
    p = pl.program_id(0)
    chip = ids[1 + lax.rem(p + 2, steps)]
    place_ref[...] = jnp.zeros_like(place_ref)
    for g in range(tiles_ref.shape[0]):
        place(
            cols, lambda which, g=g: tiles_ref[g, which], sig_ref[g * BLK : (g + 1) * BLK, :],
            place_ref, g, ids[0], chip, n,
        )
    keep_ref[0] = place_ref[0].astype(BF16)
    send_ref[0] = place_ref[1].astype(BF16)


def push(ids, cols, signal, tiles, steps):
    g, n = tiles.shape[:2]
    rows, width = signal.shape
    out = pl.BlockSpec((1, rows, width), lambda p, ids, cols: (p, 0, 0))
    return pl.pallas_call(
        partial(push_kernel, n=n, steps=steps),
        grid_spec=pltpu.PrefetchScalarGridSpec(
            num_scalar_prefetch=2,
            grid=(steps - 1,),
            in_specs=[
                pl.BlockSpec((rows, width), lambda p, ids, cols: (0, 0)),
                pl.BlockSpec(
                    (g, 2, BLK, BLK),
                    lambda p, ids, cols: (0, ids[1 + lax.rem(p + 2, steps)], 0, 0),
                ),
            ],
            out_specs=[out, out],
            scratch_shapes=[pltpu.VMEM((2, rows, width), F32)],
        ),
        out_shape=[jax.ShapeDtypeStruct((steps - 1, rows, width), BF16)] * 2,
        compiler_params=params(),
        cost_estimate=cost(4 * (steps - 1) * rows * BLK * width, 8 * (steps - 1) * rows * width),
        name="push",
    )(ids, cols, signal, tiles)


def half_rows(wide):
    step = 16 * wide
    return (BLK + 1 + step - 1) // step * step


def grads_kernel(
    ids, asked, row, valid, off_ref, sig_ref, feat_ref, agg_ref, gp_ref,
    mine_ref, other_ref, *pushed_refs, wide,
):
    here = lax.axis_index("wide")
    tall = 4 * BLK
    dself = dneigh = dbias = None
    for i in range(feat_ref.shape[0] // tall):
        rows = pl.ds(i * tall, tall)
        gp = gp_ref[rows, :]
        a = mm(feat_ref[rows, :], gp, 0, 0)
        b = mm(agg_ref[rows, :], gp, 0, 0)
        c = jnp.sum(gp.astype(F32), axis=0, keepdims=True)
        dself, dneigh, dbias = (a, b, c) if i == 0 else (dself + a, dneigh + b, dbias + c)
    first = ids[0] == 0
    mine_ref[pl.ds(0, BLK), :] = jnp.where(first, dself, dneigh)
    other_ref[pl.ds(0, BLK), :] = jnp.where(first, dneigh, dself)
    spare = mine_ref.shape[0] - BLK
    mine_ref[pl.ds(BLK, spare), :] = jnp.broadcast_to(dbias, (spare, dbias.shape[1]))
    other_ref[pl.ds(BLK, spare), :] = jnp.broadcast_to(dbias, (spare, dbias.shape[1]))
    for k in range(wide):
        peer = target(here, k, wide)
        mask = (off_ref[0, peer] * valid[peer]).astype(F32).astype(BF16)
        at = pl.ds(pl.multiple_of(row[peer] * BLK, BLK), BLK)
        ref = pushed_refs[k]
        ref[pl.ds(0, BLK), :] = mm(mask, sig_ref[at, :], 0, 0).astype(BF16)
        ref[pl.ds(BLK, 16), :] = jnp.full((16, BLK), asked[peer], jnp.int32).astype(F32).astype(BF16)


def grads(ids, asked, row, valid, off_tiles, signal, features, aggregate, grad_pre):
    wide = off_tiles.shape[1]
    rows, width = features.shape
    outw = grad_pre.shape[1]

    def whole(x):
        return pl.BlockSpec(x.shape, lambda i, *s: (0,) * len(x.shape))

    ins = (off_tiles, signal, features, aggregate, grad_pre)
    outs = [jax.ShapeDtypeStruct((half_rows(wide), outw), F32)] * 2
    outs += [jax.ShapeDtypeStruct((BLK + 16, width), BF16)] * wide
    return pl.pallas_call(
        partial(grads_kernel, wide=wide),
        grid_spec=pltpu.PrefetchScalarGridSpec(
            num_scalar_prefetch=4,
            grid=(1,),
            in_specs=[whole(x) for x in ins],
            out_specs=[whole(x) for x in outs],
        ),
        out_shape=outs,
        compiler_params=params(),
        cost_estimate=cost(8 * rows * width * width, 16 * rows * width),
        name="grads",
    )(ids, asked, row, valid, *ins)


def pack_kernel(mine_ref, come_ref, *refs, wide):
    pushed_refs, msg_refs = refs[:wide], refs[wide:]
    here = lax.axis_index("wide")
    piece = mine_ref.shape[0] // wide
    head = BLK + 16
    for k in range(wide):
        peer = target(here, k, wide)
        rows = pl.ds(pl.multiple_of(peer * piece, 16), piece)
        total = mine_ref[rows, :] + come_ref[rows, :]
        high = total.astype(BF16)
        low = (total - high.astype(F32)).astype(BF16)
        msg_refs[k][pl.ds(0, head), :] = pushed_refs[k][...]
        for j, x in enumerate((high[:, :BLK], high[:, BLK:], low[:, :BLK], low[:, BLK:])):
            msg_refs[k][pl.ds(head + j * piece, piece), :] = x


def pack(mine, come, pushed):
    wide = len(pushed)

    def whole(x):
        return pl.BlockSpec(x.shape, lambda i: (0,) * len(x.shape))

    ins = (mine, come, *pushed)
    tall = BLK + 16 + mine.shape[0] // wide * 4
    outs = [jax.ShapeDtypeStruct((tall, pushed[0].shape[1]), BF16)] * wide
    return pl.pallas_call(
        partial(pack_kernel, wide=wide),
        grid=(1,),
        in_specs=[whole(x) for x in ins],
        out_specs=[whole(x) for x in outs],
        out_shape=outs,
        compiler_params=params(),
        cost_estimate=cost(4 * mine.size, 20 * mine.size),
        name="pack",
    )(*ins)


def piece_sum_kernel(*refs):
    arrived, out_ref = refs[:-1], refs[-1]
    piece = out_ref.shape[0]
    head = BLK + 16
    for side in range(2):
        part = [
            a[pl.ds(head + side * piece, piece), :].astype(F32)
            + a[pl.ds(head + (side + 2) * piece, piece), :].astype(F32)
            for a in arrived
        ]
        out_ref[:, pl.ds(side * BLK, BLK)] = tree_sum(part)


def piece_sum(arrived):
    def whole(x):
        return pl.BlockSpec(x.shape, lambda i: (0,) * len(x.shape))

    piece = (arrived[0].shape[0] - BLK - 16) // 4
    out = jax.ShapeDtypeStruct((piece, 2 * BLK), F32)
    return pl.pallas_call(
        piece_sum_kernel,
        grid=(1,),
        in_specs=[whole(x) for x in arrived],
        out_specs=whole(out),
        out_shape=out,
        compiler_params=params(),
        cost_estimate=cost(arrived[0].size * len(arrived), 2 * arrived[0].size * len(arrived)),
        name="piece_sum",
    )(*arrived)


def half_kernel(*refs, factor):
    pieces, out_ref = refs[:-1], refs[-1]
    wide, piece = len(pieces), pieces[0].shape[0]
    here = lax.axis_index("wide")
    for k in range(wide):
        at = pl.ds(pl.multiple_of(source(here, k, wide) * piece, 16), piece)
        out_ref[at, :] = pieces[k][...] * factor


def half(pieces, factor):
    def whole(x):
        return pl.BlockSpec(x.shape, lambda i: (0, 0))

    out = jax.ShapeDtypeStruct((pieces[0].shape[0] * len(pieces), pieces[0].shape[1]), F32)
    return pl.pallas_call(
        partial(half_kernel, factor=factor),
        grid=(1,),
        in_specs=[whole(x) for x in pieces],
        out_specs=whole(out),
        out_shape=out,
        compiler_params=params(),
        cost_estimate=cost(out.size, 8 * out.size),
        name="half",
    )(*pieces)


def finish_kernel(ids, total_ref, paired_ref, self_ref, neigh_ref, bias_ref):
    first = ids[0] == 0
    total, paired = total_ref[pl.ds(0, BLK), :], paired_ref[pl.ds(0, BLK), :]
    self_ref[...] = jnp.where(first, total, paired)
    neigh_ref[...] = jnp.where(first, paired, total)
    at = pl.ds(BLK, 8)
    bias_ref[...] = jnp.where(first, total_ref[at, :], paired_ref[at, :])[:1]


def finish(ids, total, paired):
    def whole(x):
        return pl.BlockSpec(x.shape, lambda i, *s: (0, 0))

    outs = [jax.ShapeDtypeStruct((r, 2 * BLK), F32) for r in (BLK, BLK, 1)]
    return pl.pallas_call(
        finish_kernel,
        grid_spec=pltpu.PrefetchScalarGridSpec(
            num_scalar_prefetch=1,
            grid=(1,),
            in_specs=[whole(total), whole(paired)],
            out_specs=[whole(x) for x in outs],
        ),
        out_shape=outs,
        compiler_params=params(),
        cost_estimate=cost(4 * total.size, 16 * total.size),
        name="finish",
    )(ids, total, paired)


def base_kernel(gp_ref, wself_ref, keep_ref, come_ref, *refs):
    arrived, out_ref = refs[:-1], refs[-1]
    tall = 4 * BLK
    for i in range(out_ref.shape[0] // tall):
        rows = pl.ds(i * tall, tall)
        both = keep_ref[0, rows, :].astype(F32) + come_ref[0, rows, :].astype(F32)
        out_ref[rows, :] = mm(gp_ref[rows, :], wself_ref[...], 1, 1) + both
    line = lax.broadcasted_iota(jnp.int32, (16, BLK), 0)
    for a in arrived:
        index = jnp.max(jnp.where(line == 0, a[pl.ds(BLK, 16), :].astype(F32), 0.0))
        at = pl.ds(pl.multiple_of(index.astype(jnp.int32) * BLK, BLK), BLK)
        out_ref[at, :] += a[pl.ds(0, BLK), :].astype(F32)


def base(grad_pre, w_self, keeps, comes, arrived):
    last, rows, width = keeps.shape

    def whole(x):
        return pl.BlockSpec(x.shape, lambda i, *s: (0,) * x.ndim)

    slab = pl.BlockSpec((1, rows, width), lambda i: (last - 1, 0, 0))
    head = pl.BlockSpec((BLK + 16, width), lambda i: (0, 0))
    return pl.pallas_call(
        base_kernel,
        grid=(1,),
        in_specs=[whole(grad_pre), whole(w_self), slab, slab] + [head] * len(arrived),
        out_specs=pl.BlockSpec((rows, width), lambda i, *s: (0, 0)),
        out_shape=jax.ShapeDtypeStruct((rows, width), F32),
        compiler_params=params(),
        cost_estimate=cost(4 * rows * width * width, 12 * rows * width),
        name="base",
    )(grad_pre, w_self, keeps, comes, *arrived)


def joined_kernel(*refs):
    total = refs[0][...].astype(F32)
    for ref in refs[1:-1]:
        total = total + ref[...].astype(F32)
    refs[-1][...] = total.astype(BF16)


def joined(j, got, stacks, s):
    last, rows, width = stacks[0].shape
    tall = rows // CHUNKS
    part = pl.BlockSpec((None, tall, width), lambda i: (s, j, 0))
    whole = pl.BlockSpec((tall, width), lambda i: (0, 0))
    more = () if got is None else (got,)
    return pl.pallas_call(
        joined_kernel,
        grid=(1,),
        in_specs=[whole] * len(more) + [part] * len(stacks),
        out_specs=whole,
        out_shape=jax.ShapeDtypeStruct((tall, width), BF16),
        compiler_params=params(),
        cost_estimate=cost(3 * tall * width, 8 * tall * width),
        name=f"joined{s}_{j}",
    )(*more, *stacks)


def last_kernel(rest_ref, *refs):
    got, out_ref = refs[:-1], refs[-1]
    tall = got[0].shape[0]
    for j, ref in enumerate(got):
        rows = pl.ds(j * tall, tall)
        out_ref[rows, :] = rest_ref[rows, :] + ref[...].astype(F32)


def last(rest, got):
    def whole(x):
        return pl.BlockSpec(x.shape, lambda i: (0, 0))

    return pl.pallas_call(
        last_kernel,
        grid=(1,),
        in_specs=[whole(x) for x in (rest, *got)],
        out_specs=whole(rest),
        out_shape=jax.ShapeDtypeStruct(rest.shape, F32),
        compiler_params=params(),
        cost_estimate=cost(rest.size, 10 * rest.size),
        name="last",
    )(rest, *got)


def power(size):
    return size & (size - 1) == 0


def target(i, k, size):
    return i ^ k if power(size) else lax.rem(i + k, size)


def source(i, k, size):
    return i ^ k if power(size) else lax.rem(i + size - k, size)


def to_peer(x, axis, k):
    size = lax.axis_size(axis)
    return lax.ppermute(x, axis, [(i, i ^ k if power(size) else (i + k) % size) for i in range(size)])


def tree_sum(parts):
    while len(parts) > 1:
        pairs = [a + b for a, b in zip(parts[::2], parts[1::2])]
        parts = pairs + parts[len(pairs) * 2 :]
    return parts[0]


def shards(
    features,
    band_tiles,
    band_cols,
    off_tiles,
    req_block,
    req_row,
    req_valid,
    weight_self,
    weight_neigh,
    bias_term,
    cotangent,
):
    row_count, width = features.shape
    n = lax.axis_size("narrow")
    wide = lax.axis_size("wide")
    steps = n // 2
    fold = [0] + list(range(1, steps, 2)) + list(range(2, steps, 2))[::-1]
    after = {a: b for a, b in zip(fold, fold[1:] + fold[:1])}

    def onward(x):
        return lax.ppermute(x, "narrow", [(i, after[i // 2] * 2 + i % 2) for i in range(n)])

    def swap(x):
        return to_peer(x, "narrow", 1)

    me = lax.axis_index("narrow")
    here = lax.axis_index("wide")
    chips = jnp.array(
        [[fold[(fold.index(z) - s) % steps] for s in range(steps)] for z in range(steps)], jnp.int32
    )[me // 2]
    ids = jnp.concatenate([(me % 2)[None].astype(jnp.int32), chips])
    cols = band_cols.reshape(-1)
    asked, row, valid = req_block[0], req_row[0], req_valid[0]
    def tie(*xs):
        return lax.optimization_barrier(xs)

    def cut(x):
        tall = row_count // CHUNKS
        return [lax.slice_in_dim(x, j * tall, (j + 1) * tall) for j in range(CHUNKS)]

    slabs, pairs = [cut(features)], []
    by_peer = [features] + [to_peer(features, "wide", k) for k in range(1, wide)]
    tiles, degree = prep(band_tiles)
    acc = None
    for s in range(1, steps):
        following = [onward(x) for x in slabs[-1]]
        pairs.append([swap(x) for x in slabs[-1]])
        if s == 1:
            following[1], tiles, degree = tie(following[1], tiles, degree)
        else:
            acc = pull(ids, cols, tiles, slabs[s - 2], pairs[s - 2], acc, s - 2)
            following[1], acc = tie(following[1], acc)
        if s == steps - 1:
            following[0], *by_peer = tie(following[0], *by_peer)
            acc = pull(ids, cols, tiles, slabs[-1], pairs[-1], acc, s - 1)
            acc, degree = off_band(
                here[None], asked, row, valid, off_tiles, by_peer, acc, degree
            )
            following[0], acc, degree = tie(following[0], acc, degree)
        slabs.append(following)
    pairs.append([swap(x) for x in slabs[-1]])
    layer_out, grad_pre, aggregate, signal, keep, send = middle(
        ids, cols, tiles, slabs[-1], pairs[-1], acc, degree, features, cotangent,
        weight_self, weight_neigh, bias_term.reshape(1, -1), steps,
    )

    come = swap(send)
    mine, other, *pushed = grads(ids, asked, row, valid, off_tiles, signal, features, aggregate, grad_pre)
    come, mine, other, *pushed = tie(come, mine, other, *pushed)
    first = (keep[None], come[None])
    going = [joined(j, None, first, 0) for j in range(CHUNKS)]
    *going, signal = tie(*going, signal)
    got = [onward(x) for x in going]
    keeps, sends = push(ids, cols, signal, tiles, steps)
    comes = swap(sends)
    packed = pack(mine, swap(other), pushed)
    arrived = [packed[0]] + [to_peer(packed[k], "wide", k) for k in range(1, wide)]
    got[0], keeps, comes, *packed = tie(got[0], keeps, comes, *packed)
    rest = total = None
    for s in range(steps - 2):
        going = [joined(j, got[j], (keeps, comes), s) for j in range(CHUNKS)]
        got = [onward(x) for x in going]
        if s == 0:
            total = piece_sum(arrived)
            rest = base(grad_pre, weight_self, keeps, comes, arrived)
            got[0], total, rest = tie(got[0], total, rest)
    if power(steps):
        k = 1
        while k < steps:
            total = total + to_peer(total, "narrow", 2 * k)
            k *= 2
    else:
        total = lax.psum(total, "narrow", axis_index_groups=[list(range(c, n, 2)) for c in (0, 1)])
    pieces = [total] + [to_peer(total, "wide", k) for k in range(1, wide)]
    whole = half(pieces, (wide * n * row_count) ** (-0.5))
    grad_self, grad_neigh, grad_bias = finish(ids, whole, swap(whole))
    got[-1], grad_self, grad_neigh, grad_bias = tie(got[-1], grad_self, grad_neigh, grad_bias)
    grad_features = last(rest, got)
    return layer_out, grad_features, grad_self, grad_neigh, grad_bias.reshape(-1)


def solution(mesh):
    both = ("wide", "narrow")
    placed = (
        P(both, None),
        P(both, None, None, None),
        P(both, None),
        P(both, None, None, None),
        P(both, None),
        P(both, None),
        P(both, None),
        P(),
        P(),
        P(),
        P(both, None),
    )
    return jax.shard_map(
        shards,
        mesh=mesh,
        in_specs=placed,
        out_specs=(P(both, None), P(both, None), P(), P(), P()),
        check_vma=False,
    )
```

time: 190 us -> 116 us (0.61); the launches traced: 188 us -> 116 us
  waiting for transfers between devices: 65.6 us -> 31.5 us
  local copies, waits for them, and re-layouts: 45.9 us -> 16.7 us
  starting transfers between devices: 20 us -> 43.7 us
  other arithmetic: 16.5 us -> 0.09 us
  Pallas kernels: 38.7 us -> 23 us
    ppermute x6 -> x12, waiting for transfers between devices: 52.4 us -> 19.5 us  [onward(): lax.ppermute(x, 'narrow', [(i, after[i // 2] * 2 + i % 2) for i in range(...]
    ppermute x6 -> x12, starting transfers between devices: 7.3 us -> 24.3 us  [onward(): lax.ppermute(x, 'narrow', [(i, after[i // 2] * 2 + i % 2) for i in range(...]
    slice x15 -> x1, local copies, waits for them, and re-layouts: 12.3 us -> 1.07 us  [cut(): lax.slice_in_dim(x, j * tall, (j + 1) * tall)]
    pallas_call x1, Pallas kernels: 12 us -> 1.95 us  [prep(): pl.pallas_call(prep_kernel, grid=(g,), in_specs=[tile_spec], out_specs=[t...]
    convert_element_type x8 -> x0, other arithmetic: 9.43 us -> none  [the longest x2 2.65 us: shards(): (got.astype(F32) + (keeps[s].astype(F32) + come[s].astype(F32))).astype(B...]
    ppermute x16 -> x23, starting transfers between devices: 12.7 us -> 19.4 us  [to_peer(): lax.ppermute(x, axis, [(i, i ^ k if power(size) else (i + k) % size) for...]
    add x11 -> x0, other arithmetic: 6.08 us -> none  [the longest x4 3.87 us: grads_of(): g = (g[:, 0] + g[:, 1]).transpose(0, 2, 1, 3).reshape(2, BLK, 2 * BLK)]
    pallas_call x3, Pallas kernels: 9.96 us -> 5.44 us  [pull(): pl.pallas_call(partial(pull_kernel, n=n, step=step, first=acc is None), g...]
  transfers between devices with their start and end apart: 22 -> 35, of which waited for: 8 -> 17; matrix products, arithmetic and copies ran while one was open for 28% -> 1% of each run, Pallas kernels for 13% -> 11%
where the time goes in v2:
time: 116 us
  starting transfers between devices  43.7 us (38%)
  waiting for transfers between devices  31.5 us (27%)
  Pallas kernels  23 us (20%)
  local copies, waits for them, and re-layouts  16.7 us (14%)
    ppermute x12, starting transfers between devices, onward(): lax.ppermute(x, 'narrow', [(i, after[i // 2] * 2 + i % 2) for i in range(...  24.3 us
    ppermute x12, waiting for transfers between devices, onward(): lax.ppermute(x, 'narrow', [(i, after[i // 2] * 2 + i % 2) for i in range(...  19.5 us
    ppermute x23, starting transfers between devices, to_peer(): lax.ppermute(x, axis, [(i, i ^ k if power(size) else (i + k) % size) for...  19.4 us
    unnamed x43, local copies, waits for them, and re-layouts  14.8 us
    ppermute x23, waiting for transfers between devices, to_peer(): lax.ppermute(x, axis, [(i, i ^ k if power(size) else (i + k) % size) for...  12 us
    pallas_call x1, Pallas kernels, middle(): pl.pallas_call(partial(middle_kernel, n=n, steps=steps), grid_spec=pltpu....  6.21 us
    pallas_call x3, Pallas kernels, pull(): pl.pallas_call(partial(pull_kernel, n=n, step=step, first=acc is None), g...  5.44 us
    pallas_call x1, Pallas kernels, push(): pl.pallas_call(partial(push_kernel, n=n, steps=steps), grid_spec=pltpu.Pr...  2.97 us
  transfers between devices with their start and end apart: 35, of which 17 were waited for; matrix products, arithmetic and copies ran while one was open for 1% of the time, Pallas kernels for 11%

profile of v2, /device:TPU:0, one launch (start us, length us, event | category | flops | bytes accessed | tf_op | source)
XLA Modules:
  0.0 115.9 jit_solution(17358070962433104253)
XLA Ops:
  1.7 3.1 %collective-permute-start.1 = (bf16[1024,128]{1,0:T(8,128)(2,1)S(1)}, bf16[1024,128]{1,0:T(8,128)(2,1)S(1)}, u32[]{:S(2)}, u32[]{:S(2)}) collective-permute-start(bf16[1024,128]{1,0:T(8,128)(2,1)S(1)} %get-tuple-element.125.refs_0_), channel_id=1, source_target_pairs={{0,2},{1,3},{2,6},{3,7},{4,0},{5,1},{6,4},{7,5},{8,10},{9,11},{10,... | collective-permute-start | bytes 786440 | tf_op jit(solution)/shard_map/ppermute | solution.py:599
  4.8 2.6 %collective-permute-start = (bf16[1024,128]{1,0:T(8,128)(2,1)S(1)}, bf16[1024,128]{1,0:T(8,128)(2,1)}, u32[]{:S(2)}, u32[]{:S(2)}) collective-permute-start(bf16[1024,128]{1,0:T(8,128)(2,1)S(1)} %get-tuple-element.126.refs_1_), channel_id=1, source_target_pairs={{0,2},{1,3},{2,6},{3,7},{4,0},{5,1},{6,4},{7,5},{8,10},{9,11},{10,... | collective-permute-start | bytes 786440 | tf_op jit(solution)/shard_map/ppermute | solution.py:599
  7.9 2.4 %collective-permute-start.6 = (bf16[2048,128]{1,0:T(8,128)(2,1)}, bf16[2048,128]{1,0:T(8,128)(2,1)}, u32[]{:S(2)}, u32[]{:S(2)}) collective-permute-start(bf16[2048,128]{1,0:T(8,128)(2,1)} %feat_ref.3), channel_id=1, source_target_pairs={{0,24},{8,16},{16,8},{24,0},{1,25},{9,17},{17,9},{25,1},{2,26},{10... | collective-permute-start | bytes 1572872 | tf_op jit(solution)/shard_map/ppermute | solution.py:568
  10.3 3.4 %copy-done.4 = s32[16,8,128,128]{3,2,1,0:T(8,128)S(1)} copy-done((s32[16,8,128,128]{3,2,1,0:T(8,128)S(1)}, s32[16,8,128,128]{3,2,1,0:T(8,128)}, u32[]{:S(2)}) %copy-start.4) | copy-done | bytes 8388632
  13.7 2.0 %prep.1 = (bf16[16,8,128,128]{3,2,1,0:T(8,128)(2,1)S(1)}, f32[2048,128]{1,0:T(8,128)S(1)}) custom-call(s32[16,8,128,128]{3,2,1,0:T(8,128)S(1)} %copy-done.4), custom_call_target="tpu_custom_call" | custom-call | flops 2097152 | bytes 16777216 | tf_op jit(solution)/shard_map/prep/pallas_call | solution.py:42
  15.7 2.0 %copy-done = bf16[16,8,128,128]{3,2,1,0:T(8,128)(2,1)} copy-done((bf16[16,8,128,128]{3,2,1,0:T(8,128)(2,1)}, bf16[16,8,128,128]{3,2,1,0:T(8,128)(2,1)S(1)}, u32[]{:S(2)}) %copy-start) | copy-done | bytes 4194328
  17.8 1.6 %collective-permute-start.5 = (bf16[2048,128]{1,0:T(8,128)(2,1)S(1)}, bf16[2048,128]{1,0:T(8,128)(2,1)}, u32[]{:S(2)}, u32[]{:S(2)}) collective-permute-start(bf16[2048,128]{1,0:T(8,128)(2,1)S(1)} %copy-done.5), channel_id=1, source_target_pairs={{0,16},{8,24},{16,0},{24,8},{1,17},{9,25},{17,1},{25,9},{2,18},{10... | collective-permute-start | bytes 1572872 | tf_op jit(solution)/shard_map/ppermute | solution.py:568
  21.5 3.5 %collective-permute-start.2 = (bf16[1024,128]{1,0:T(8,128)(2,1)S(1)}, bf16[1024,128]{1,0:T(8,128)(2,1)}, u32[]{:S(2)}, u32[]{:S(2)}) collective-permute-start(bf16[1024,128]{1,0:T(8,128)(2,1)S(1)} %collective-permute-done.1.refs_0_), channel_id=1, source_target_pairs={{0,2},{1,3},{2,6},{3,7},{4,0},{5,1},{6,4},{7,5},{8,10},{9,11},{10,... | collective-permute-start | bytes 786440 | tf_op jit(solution)/shard_map/ppermute | solution.py:599
  27.2 3.4 %collective-permute-done.7.refs_1_ = bf16[1024,128]{1,0:T(8,128)(2,1)} collective-permute-done((bf16[1024,128]{1,0:T(8,128)(2,1)}, bf16[1024,128]{1,0:T(8,128)(2,1)}, u32[]{:S(2)}, u32[]{:S(2)}) %collective-permute-start.7) | collective-permute-done | bytes 262176 | tf_op jit(solution)/shard_map/ppermute | solution.py:599
  31.5 2.2 %copy-done.1 = bf16[16,8,128,128]{3,2,1,0:T(8,128)(2,1)S(1)} copy-done((bf16[16,8,128,128]{3,2,1,0:T(8,128)(2,1)S(1)}, bf16[16,8,128,128]{3,2,1,0:T(8,128)(2,1)}, u32[]{:S(2)}) %copy-start.1) | copy-done | bytes 4194328
  37.5 3.4 %collective-permute-start.12 = (bf16[1024,128]{1,0:T(8,128)(2,1)}, bf16[1024,128]{1,0:T(8,128)(2,1)S(1)}, u32[]{:S(2)}, u32[]{:S(2)}) collective-permute-start(bf16[1024,128]{1,0:T(8,128)(2,1)} %collective-permute-done.7.refs_1_), channel_id=1, source_target_pairs={{0,2},{1,3},{2,6},{3,7},{4,0},{5,1},{6,4},{7,5},{8,10},{9,11},{10,... | collective-permute-start | bytes 786440 | tf_op jit(solution)/shard_map/ppermute | solution.py:599
  41.4 2.2 %copy-done.2 = bf16[16,8,128,128]{3,2,1,0:T(8,128)(2,1)S(1)} copy-done((bf16[16,8,128,128]{3,2,1,0:T(8,128)(2,1)S(1)}, bf16[16,8,128,128]{3,2,1,0:T(8,128)(2,1)}, u32[]{:S(2)}) %copy-start.2) | copy-done | bytes 4194328
  44.6 2.1 %pull1.1.refs_4_ = f32[2048,128]{1,0:T(8,128)S(1)} custom-call(s32[5]{0:T(128)S(1)} %pad_add_fusion.ids, s32[128]{0:T(128)S(1)} %reshape.19.cols, bf16[16,8,128,128]{3,2,1,0:T(8,128)(2,1)S(1)} %copy-done.2, bf16[1024,128]{1,0:T(8,128)(2,1)S(1)} %collective-permute-done.1.refs_0_, bf16[1024,128]{1,0:T(8,128)(2,1)} %collective-permute-done.refs_1_, ...), custom_call_target="tpu_custom_call" | custom-call | flops 134217728 | bytes 3145728 | tf_op jit(solution)/shard_map/pull1/pallas_call | solution.py:95
  47.0 5.2 %collective-permute-done.12.refs_1_ = bf16[1024,128]{1,0:T(8,128)(2,1)S(1)} collective-permute-done((bf16[1024,128]{1,0:T(8,128)(2,1)}, bf16[1024,128]{1,0:T(8,128)(2,1)S(1)}, u32[]{:S(2)}, u32[]{:S(2)}) %collective-permute-start.12) | collective-permute-done | bytes 262176 | tf_op jit(solution)/shard_map/ppermute | solution.py:599
  52.2 2.3 %pull2.1.refs_4_ = f32[2048,128]{1,0:T(8,128)S(1)} custom-call(s32[5]{0:T(128)S(1)} %pad_add_fusion.ids, s32[128]{0:T(128)S(1)} %reshape.19.cols, bf16[16,8,128,128]{3,2,1,0:T(8,128)(2,1)S(1)} %copy-done.2, bf16[1024,128]{1,0:T(8,128)(2,1)} %collective-permute-done.2.refs_0_, bf16[1024,128]{1,0:T(8,128)(2,1)} %collective-permute-done.7.refs_1_, ...), custom_call_target="tpu_custom_call" | custom-call | flops 134217728 | bytes 3145728 | tf_op jit(solution)/shard_map/pull2/pallas_call | solution.py:95
  54.6 2.0 %off_band.1 = (f32[2048,128]{1,0:T(8,128)S(1)}, f32[2048,128]{1,0:T(8,128)S(1)}) custom-call(s32[1]{0:T(128)} %bitcast.2.here_ref, s32[4]{0:T(128)S(1)} %bitcast.14, s32[4]{0:T(128)S(1)} %bitcast.16, s32[4]{0:T(128)S(1)} %bitcast.18, s32[1,4,128,128]{3,2,1,0:T(8,128)S(1)} %copy-done.6, bf16[2048,128]{1,0:T(8,128)(2,1)S(1)} %copy-done.5, ...), custom_call_target="tpu_custom_call" | custom-call | flops 16777216 | bytes 4194304 | tf_op jit(solution)/shard_map/off_band/pallas_call | solution.py:135
  58.3 6.2 %middle.1 = (bf16[2048,256]{1,0:T(8,128)(2,1)}, bf16[2048,256]{1,0:T(8,128)(2,1)S(1)}, bf16[2048,128]{1,0:T(8,128)(2,1)S(1)}, bf16[2048,128]{1,0:T(8,128)(2,1)S(...) custom-call(s32[5]{0:T(128)S(1)} %pad_add_fusion.ids, s32[128]{0:T(128)S(1)} %reshape.19.cols, ...), custom_call_target="tpu_custom_call" | custom-call | flops 671088640 | bytes 7864320 | tf_op jit(solution)/shard_map/middle/pallas_call | solution.py:220
  66.6 3.0 %push.1 = (bf16[3,2048,128]{2,1,0:T(8,128)(2,1)S(1)}, bf16[3,2048,128]{2,1,0:T(8,128)(2,1)S(1)}) custom-call(s32[5]{0:T(128)S(1)} %pad_add_fusion.ids, s32[128]{0:T(128)S(1)} %reshape.19.cols, bf16[2048,128]{1,0:T(8,128)(2,1)S(1)} %get-tuple-element.98.sig_ref, bf16[16,8,128,128]{3,2,1,0:T(8,128)(2,1)S(1)} %copy-done.3), custom_call_target="tpu_custom_call" | custom-call | flops 402653184 | bytes 6291456 | tf_op jit(solution)/shard_map/push/pallas_call | solution.py:266
  70.9 3.3 %collective-permute-start.26 = (bf16[1024,128]{1,0:T(8,128)(2,1)S(1)}, bf16[1024,128]{1,0:T(8,128)(2,1)S(1)}, u32[]{:S(2)}, u32[]{:S(2)}) collective-permute-start(bf16[1024,128]{1,0:T(8,128)(2,1)S(1)} %joined0_1.2), channel_id=1, source_target_pairs={{0,2},{1,3},{2,6},{3,7},{4,0},{5,1},{6,4},{7,5},{8,10},{9,11},{10,... | collective-permute-start | bytes 786440 | tf_op jit(solution)/shard_map/ppermute | solution.py:599
  74.2 5.8 %collective-permute-done.18.refs_0_ = bf16[1024,128]{1,0:T(8,128)(2,1)S(1)} collective-permute-done((bf16[1024,128]{1,0:T(8,128)(2,1)S(1)}, bf16[1024,128]{1,0:T(8,128)(2,1)S(1)}, u32[]{:S(2)}, u32[]{:S(2)}) %collective-permute-start.18) | collective-permute-done | bytes 262176 | tf_op jit(solution)/shard_map/ppermute | solution.py:599
  81.0 4.7 %collective-permute-done.26.refs_0_ = bf16[1024,128]{1,0:T(8,128)(2,1)S(1)} collective-permute-done((bf16[1024,128]{1,0:T(8,128)(2,1)S(1)}, bf16[1024,128]{1,0:T(8,128)(2,1)S(1)}, u32[]{:S(2)}, u32[]{:S(2)}) %collective-permute-start.26) | collective-permute-done | bytes 262176 | tf_op jit(solution)/shard_map/ppermute | solution.py:599
  94.5 3.5 %collective-permute-start.29 = (f32[48,256]{1,0:T(8,128)S(1)}, f32[48,256]{1,0:T(8,128)S(1)}, u32[]{:S(2)}, u32[]{:S(2)}) collective-permute-start(f32[48,256]{1,0:T(8,128)S(1)} %piece_sum.1), channel_id=1, source_target_pairs={{0,2},{1,3},{2,0},{3,1},{4,6},{5,7},{6,4},{7,5},{8,10},{9,11},{10,... | collective-permute-start | bytes 147464 | tf_op jit(solution)/shard_map/ppermute | solution.py:568
  97.9 2.1 %collective-permute-done.29 = f32[48,256]{1,0:T(8,128)S(1)} collective-permute-done((f32[48,256]{1,0:T(8,128)S(1)}, f32[48,256]{1,0:T(8,128)S(1)}, u32[]{:S(2)}, u32[]{:S(2)}) %collective-permute-start.29) | collective-permute-done | bytes 49184 | tf_op jit(solution)/shard_map/ppermute | solution.py:568
  102.4 3.0 %collective-permute-start.25 = (bf16[1024,128]{1,0:T(8,128)(2,1)S(1)}, bf16[1024,128]{1,0:T(8,128)(2,1)S(1)}, u32[]{:S(2)}, u32[]{:S(2)}) collective-permute-start(bf16[1024,128]{1,0:T(8,128)(2,1)S(1)} %joined1_0.1), channel_id=1, source_target_pairs={{0,2},{1,3},{2,6},{3,7},{4,0},{5,1},{6,4},{7,5},{8,10},{9,11},{10,... | collective-permute-start | bytes 786440 | tf_op jit(solution)/shard_map/ppermute | solution.py:599
  (116 shorter events, 40.4 us)
Async XLA Ops:
  1.7 16.0 %collective-permute-start.1 = (bf16[1024,128]{1,0:T(8,128)(2,1)S(1)}, bf16[1024,128]{1,0:T(8,128)(2,1)S(1)}, u32[]{:S(2)}, u32[]{:S(2)}) collective-permute-start(bf16[1024,128]{1,0:T(8,128)(2,1)S(1)} %get-tuple-element.125.refs_0_), channel_id=1, source_target_pairs={{0,2},{1,3},{2,6},{3,7},{4,0},{5,1},{6,4},{7,5},{8,10},{9,11},{10,... | collective-permute-start | bytes 786440 | tf_op jit(solution)/shard_map/ppermute | solution.py:599
  4.8 13.0 %collective-permute-start = (bf16[1024,128]{1,0:T(8,128)(2,1)S(1)}, bf16[1024,128]{1,0:T(8,128)(2,1)}, u32[]{:S(2)}, u32[]{:S(2)}) collective-permute-start(bf16[1024,128]{1,0:T(8,128)(2,1)S(1)} %get-tuple-element.126.refs_1_), channel_id=1, source_target_pairs={{0,2},{1,3},{2,6},{3,7},{4,0},{5,1},{6,4},{7,5},{8,10},{9,11},{10,... | collective-permute-start | bytes 786440 | tf_op jit(solution)/shard_map/ppermute | solution.py:599
  7.4 12.0 %collective-permute-start.8 = (bf16[1024,128]{1,0:T(8,128)(2,1)S(1)}, bf16[1024,128]{1,0:T(8,128)(2,1)S(1)}, u32[]{:S(2)}, u32[]{:S(2)}) collective-permute-start(bf16[1024,128]{1,0:T(8,128)(2,1)S(1)} %get-tuple-element.125.refs_0_), channel_id=1, source_target_pairs={{0,1},{1,0},{2,3},{3,2},{4,5},{5,4},{6,7},{7,6},{8,9},{9,8},{10,11... | collective-permute-start | bytes 786440 | tf_op jit(solution)/shard_map/ppermute | solution.py:568
  7.4 13.4 %collective-permute-start.9 = (bf16[1024,128]{1,0:T(8,128)(2,1)S(1)}, bf16[1024,128]{1,0:T(8,128)(2,1)S(1)}, u32[]{:S(2)}, u32[]{:S(2)}) collective-permute-start(bf16[1024,128]{1,0:T(8,128)(2,1)S(1)} %get-tuple-element.126.refs_1_), channel_id=1, source_target_pairs={{0,1},{1,0},{2,3},{3,2},{4,5},{5,4},{6,7},{7,6},{8,9},{9,8},{10,11... | collective-permute-start | bytes 786440 | tf_op jit(solution)/shard_map/ppermute | solution.py:568
  7.9 29.7 %collective-permute-start.6 = (bf16[2048,128]{1,0:T(8,128)(2,1)}, bf16[2048,128]{1,0:T(8,128)(2,1)}, u32[]{:S(2)}, u32[]{:S(2)}) collective-permute-start(bf16[2048,128]{1,0:T(8,128)(2,1)} %feat_ref.3), channel_id=1, source_target_pairs={{0,24},{8,16},{16,8},{24,0},{1,25},{9,17},{17,9},{25,1},{2,26},{10... | collective-permute-start | bytes 1572872 | tf_op jit(solution)/shard_map/ppermute | solution.py:568
  17.7 7.3 %collective-permute-start.13 = (bf16[1024,128]{1,0:T(8,128)(2,1)S(1)}, bf16[1024,128]{1,0:T(8,128)(2,1)S(1)}, u32[]{:S(2)}, u32[]{:S(2)}) collective-permute-start(bf16[1024,128]{1,0:T(8,128)(2,1)S(1)} %collective-permute-done.1.refs_0_), channel_id=1, source_target_pairs={{0,1},{1,0},{2,3},{3,2},{4,5},{5,4},{6,7},{7,6},{8,9},{9,8},{10,11... | collective-permute-start | bytes 786440 | tf_op jit(solution)/shard_map/ppermute | solution.py:568
  17.8 23.1 %collective-permute-start.5 = (bf16[2048,128]{1,0:T(8,128)(2,1)S(1)}, bf16[2048,128]{1,0:T(8,128)(2,1)}, u32[]{:S(2)}, u32[]{:S(2)}) collective-permute-start(bf16[2048,128]{1,0:T(8,128)(2,1)S(1)} %copy-done.5), channel_id=1, source_target_pairs={{0,16},{8,24},{16,0},{24,8},{1,17},{9,25},{17,1},{25,9},{2,18},{10... | collective-permute-start | bytes 1572872 | tf_op jit(solution)/shard_map/ppermute | solution.py:568
  20.1 10.5 %collective-permute-start.7 = (bf16[1024,128]{1,0:T(8,128)(2,1)}, bf16[1024,128]{1,0:T(8,128)(2,1)}, u32[]{:S(2)}, u32[]{:S(2)}) collective-permute-start(bf16[1024,128]{1,0:T(8,128)(2,1)} %collective-permute-done.refs_1_), channel_id=1, source_target_pairs={{0,2},{1,3},{2,6},{3,7},{4,0},{5,1},{6,4},{7,5},{8,10},{9,11},{10,... | collective-permute-start | bytes 786440 | tf_op jit(solution)/shard_map/ppermute | solution.py:599
  21.5 15.2 %collective-permute-start.2 = (bf16[1024,128]{1,0:T(8,128)(2,1)S(1)}, bf16[1024,128]{1,0:T(8,128)(2,1)}, u32[]{:S(2)}, u32[]{:S(2)}) collective-permute-start(bf16[1024,128]{1,0:T(8,128)(2,1)S(1)} %collective-permute-done.1.refs_0_), channel_id=1, source_target_pairs={{0,2},{1,3},{2,6},{3,7},{4,0},{5,1},{6,4},{7,5},{8,10},{9,11},{10,... | collective-permute-start | bytes 786440 | tf_op jit(solution)/shard_map/ppermute | solution.py:599
  25.7 21.1 %collective-permute-start.4 = (bf16[2048,128]{1,0:T(8,128)(2,1)S(1)}, bf16[2048,128]{1,0:T(8,128)(2,1)}, u32[]{:S(2)}, u32[]{:S(2)}) collective-permute-start(bf16[2048,128]{1,0:T(8,128)(2,1)S(1)} %copy-done.5), channel_id=1, source_target_pairs={{0,8},{8,0},{16,24},{24,16},{1,9},{9,1},{17,25},{25,17},{2,10},{10... | collective-permute-start | bytes 1572872 | tf_op jit(solution)/shard_map/ppermute | solution.py:568
  30.6 10.4 %collective-permute-start.14 = (bf16[1024,128]{1,0:T(8,128)(2,1)}, bf16[1024,128]{1,0:T(8,128)(2,1)}, u32[]{:S(2)}, u32[]{:S(2)}) collective-permute-start(bf16[1024,128]{1,0:T(8,128)(2,1)} %collective-permute-done.refs_1_), channel_id=1, source_target_pairs={{0,1},{1,0},{2,3},{3,2},{4,5},{5,4},{6,7},{7,6},{8,9},{9,8},{10,11... | collective-permute-start | bytes 786440 | tf_op jit(solution)/shard_map/ppermute | solution.py:568
  36.7 10.3 %collective-permute-start.3 = (bf16[1024,128]{1,0:T(8,128)(2,1)}, bf16[1024,128]{1,0:T(8,128)(2,1)S(1)}, u32[]{:S(2)}, u32[]{:S(2)}) collective-permute-start(bf16[1024,128]{1,0:T(8,128)(2,1)} %collective-permute-done.2.refs_0_), channel_id=1, source_target_pairs={{0,2},{1,3},{2,6},{3,7},{4,0},{5,1},{6,4},{7,5},{8,10},{9,11},{10,... | collective-permute-start | bytes 786440 | tf_op jit(solution)/shard_map/ppermute | solution.py:599
  37.5 14.7 %collective-permute-start.12 = (bf16[1024,128]{1,0:T(8,128)(2,1)}, bf16[1024,128]{1,0:T(8,128)(2,1)S(1)}, u32[]{:S(2)}, u32[]{:S(2)}) collective-permute-start(bf16[1024,128]{1,0:T(8,128)(2,1)} %collective-permute-done.7.refs_1_), channel_id=1, source_target_pairs={{0,2},{1,3},{2,6},{3,7},{4,0},{5,1},{6,4},{7,5},{8,10},{9,11},{10,... | collective-permute-start | bytes 786440 | tf_op jit(solution)/shard_map/ppermute | solution.py:599
  40.9 11.3 %collective-permute-start.10 = (bf16[1024,128]{1,0:T(8,128)(2,1)}, bf16[1024,128]{1,0:T(8,128)(2,1)}, u32[]{:S(2)}, u32[]{:S(2)}) collective-permute-start(bf16[1024,128]{1,0:T(8,128)(2,1)} %collective-permute-done.2.refs_0_), channel_id=1, source_target_pairs={{0,1},{1,0},{2,3},{3,2},{4,5},{5,4},{6,7},{7,6},{8,9},{9,8},{10,11... | collective-permute-start | bytes 786440 | tf_op jit(solution)/shard_map/ppermute | solution.py:568
  40.9 11.3 %collective-permute-start.11 = (bf16[1024,128]{1,0:T(8,128)(2,1)}, bf16[1024,128]{1,0:T(8,128)(2,1)}, u32[]{:S(2)}, u32[]{:S(2)}) collective-permute-start(bf16[1024,128]{1,0:T(8,128)(2,1)} %collective-permute-done.7.refs_1_), channel_id=1, source_target_pairs={{0,1},{1,0},{2,3},{3,2},{4,5},{5,4},{6,7},{7,6},{8,9},{9,8},{10,11... | collective-permute-start | bytes 786440 | tf_op jit(solution)/shard_map/ppermute | solution.py:568
  69.5 10.5 %collective-permute-start.19 = (bf16[3,2048,128]{2,1,0:T(8,128)(2,1)S(1)}, bf16[3,2048,128]{2,1,0:T(8,128)(2,1)S(1)}, u32[]{:S(2)}, u32[]{:S(2)}) collective-permute-start(bf16[3,2048,128]{2,1,0:T(8,128)(2,1)S(1)} %get-tuple-element.100), channel_id=1, source_target_pairs={{0,1},{1,0},{2,3},{3,2},{4,5},{5,4},{6,7},{7,6},{8,9},{9,8},{10,11... | collective-permute-start | bytes 4718600 | tf_op jit(solution)/shard_map/ppermute | solution.py:568
  70.0 10.1 %collective-permute-start.18 = (bf16[1024,128]{1,0:T(8,128)(2,1)S(1)}, bf16[1024,128]{1,0:T(8,128)(2,1)S(1)}, u32[]{:S(2)}, u32[]{:S(2)}) collective-permute-start(bf16[1024,128]{1,0:T(8,128)(2,1)S(1)} %joined0_0.2), channel_id=1, source_target_pairs={{0,2},{1,3},{2,6},{3,7},{4,0},{5,1},{6,4},{7,5},{8,10},{9,11},{10,... | collective-permute-start | bytes 786440 | tf_op jit(solution)/shard_map/ppermute | solution.py:599
  70.9 14.8 %collective-permute-start.26 = (bf16[1024,128]{1,0:T(8,128)(2,1)S(1)}, bf16[1024,128]{1,0:T(8,128)(2,1)S(1)}, u32[]{:S(2)}, u32[]{:S(2)}) collective-permute-start(bf16[1024,128]{1,0:T(8,128)(2,1)S(1)} %joined0_1.2), channel_id=1, source_target_pairs={{0,2},{1,3},{2,6},{3,7},{4,0},{5,1},{6,4},{7,5},{8,10},{9,11},{10,... | collective-permute-start | bytes 786440 | tf_op jit(solution)/shard_map/ppermute | solution.py:599
  80.1 14.4 %collective-permute-start.21 = (bf16[1024,128]{1,0:T(8,128)(2,1)S(1)}, bf16[1024,128]{1,0:T(8,128)(2,1)S(1)}, u32[]{:S(2)}, u32[]{:S(2)}) collective-permute-start(bf16[1024,128]{1,0:T(8,128)(2,1)S(1)} %joined0_0.3), channel_id=1, source_target_pairs={{0,2},{1,3},{2,6},{3,7},{4,0},{5,1},{6,4},{7,5},{8,10},{9,11},{10,... | collective-permute-start | bytes 786440 | tf_op jit(solution)/shard_map/ppermute | solution.py:599
  85.7 15.1 %collective-permute-start.27 = (bf16[1024,128]{1,0:T(8,128)(2,1)S(1)}, bf16[1024,128]{1,0:T(8,128)(2,1)S(1)}, u32[]{:S(2)}, u32[]{:S(2)}) collective-permute-start(bf16[1024,128]{1,0:T(8,128)(2,1)S(1)} %joined0_1.3), channel_id=1, source_target_pairs={{0,2},{1,3},{2,6},{3,7},{4,0},{5,1},{6,4},{7,5},{8,10},{9,11},{10,... | collective-permute-start | bytes 786440 | tf_op jit(solution)/shard_map/ppermute | solution.py:599
  94.5 5.5 %collective-permute-start.29 = (f32[48,256]{1,0:T(8,128)S(1)}, f32[48,256]{1,0:T(8,128)S(1)}, u32[]{:S(2)}, u32[]{:S(2)}) collective-permute-start(f32[48,256]{1,0:T(8,128)S(1)} %piece_sum.1), channel_id=1, source_target_pairs={{0,2},{1,3},{2,0},{3,1},{4,6},{5,7},{6,4},{7,5},{8,10},{9,11},{10,... | collective-permute-start | bytes 147464 | tf_op jit(solution)/shard_map/ppermute | solution.py:568
  100.0 5.6 %collective-permute-start.30 = (f32[48,256]{1,0:T(8,128)S(1)}, f32[48,256]{1,0:T(8,128)S(1)}, u32[]{:S(2)}, u32[]{:S(2)}) collective-permute-start(f32[48,256]{1,0:T(8,128)S(1)} %add.16), channel_id=1, source_target_pairs={{0,4},{1,5},{2,6},{3,7},{4,0},{5,1},{6,2},{7,3},{8,12},{9,13},{10,... | collective-permute-start | bytes 147464 | tf_op jit(solution)/shard_map/ppermute | solution.py:568
  101.0 13.9 %collective-permute-start.28 = (bf16[1024,128]{1,0:T(8,128)(2,1)S(1)}, bf16[1024,128]{1,0:T(8,128)(2,1)S(1)}, u32[]{:S(2)}, u32[]{:S(2)}) collective-permute-start(bf16[1024,128]{1,0:T(8,128)(2,1)S(1)} %joined1_1.1), channel_id=1, source_target_pairs={{0,2},{1,3},{2,6},{3,7},{4,0},{5,1},{6,4},{7,5},{8,10},{9,11},{10,... | collective-permute-start | bytes 786440 | tf_op jit(solution)/shard_map/ppermute | solution.py:599
  102.4 12.5 %collective-permute-start.25 = (bf16[1024,128]{1,0:T(8,128)(2,1)S(1)}, bf16[1024,128]{1,0:T(8,128)(2,1)S(1)}, u32[]{:S(2)}, u32[]{:S(2)}) collective-permute-start(bf16[1024,128]{1,0:T(8,128)(2,1)S(1)} %joined1_0.1), channel_id=1, source_target_pairs={{0,2},{1,3},{2,6},{3,7},{4,0},{5,1},{6,4},{7,5},{8,10},{9,11},{10,... | collective-permute-start | bytes 786440 | tf_op jit(solution)/shard_map/ppermute | solution.py:599
  (32 other events, 128.3 us)

commit v3 on v2

v3 whole, which is shorter than its diff:
```python
from functools import partial

import jax
import jax.numpy as jnp
from jax import lax
from jax.experimental import pallas as pl
from jax.experimental.pallas import tpu as pltpu
from jax.sharding import PartitionSpec as P

F32 = jnp.float32
BF16 = jnp.bfloat16
BLK = 128
ROWS_PER = 4
CHUNKS = 1
PARTS = 2
VMEM = 28 * 1024 * 1024


def mm(a, b, lhs=1, rhs=0):
    return lax.dot_general(a, b, (((lhs,), (rhs,)), ((), ())), preferred_element_type=F32)


def params():
    return pltpu.CompilerParams(vmem_limit_bytes=VMEM)


def cost(flops, nbytes, trans=0):
    return pl.CostEstimate(flops=flops, bytes_accessed=nbytes, transcendentals=trans)


def block(ref, index):
    return ref[pl.ds(pl.multiple_of(index * BLK, BLK), BLK), :]


def tile_reads(tiles_ref, buffer, sems, chip):
    count = buffer.shape[0] // ROWS_PER
    reads = []
    for q in range(count):
        rows = pl.ds(q * ROWS_PER, ROWS_PER)
        reads.append(
            pltpu.make_async_copy(
                tiles_ref.at[rows, pl.ds(chip * 2, 2)], buffer.at[rows], sems.at[q]
            )
        )
    for r in reads:
        r.start()
    return reads


def pair_sum(ids, cols, pair, slabs_ref, g, n, chip, base=0):
    core = ids[0]
    own = block(slabs_ref.at[0], cols[g * n + chip * 2 + core])
    sib = block(slabs_ref.at[1], cols[g * n + chip * 2 + 1 - core])
    mine, other = pair[g, base + core].astype(F32), pair[g, base + 1 - core].astype(F32)
    return mm(mine.astype(BF16), own) + mm(other.astype(BF16), sib), mine + other


def lay_out(parts, slabs_ref):
    tall = parts[0].shape[0]
    for j, part in enumerate(parts):
        half, at = divmod(j, len(parts) // 2)
        slabs_ref[half, pl.ds(at * tall, tall), :] = part[...]


def spec(x):
    return pl.BlockSpec(x.shape, lambda *i: (0,) * len(x.shape))


def in_hbm():
    return pl.BlockSpec(memory_space=pltpu.HBM)


def halve_kernel(t_ref, out_ref):
    out_ref[...] = t_ref[...].astype(F32).astype(BF16)


def halve(tiles):
    g, n = tiles.shape[:2]
    one = pl.BlockSpec((1, n, BLK, BLK), lambda i: (i, 0, 0, 0))
    return pl.pallas_call(
        halve_kernel,
        grid=(g,),
        in_specs=[one],
        out_specs=one,
        out_shape=jax.ShapeDtypeStruct(tiles.shape, BF16),
        compiler_params=params(),
        cost_estimate=cost(tiles.size, 6 * tiles.size),
        name="halve",
    )(tiles)


def pull_kernel(ids, cols, *refs, n, step, chunks, wide):
    refs = list(refs)
    if wide:
        row, valid = refs[:2]
        refs = refs[2:]
    tiles_ref, parts = refs[0], refs[1 : 1 + 2 * chunks]
    refs = refs[1 + 2 * chunks :]
    if step:
        acc_in, counts_in = refs[:2]
        refs = refs[2:]
    if wide:
        off_ref, fetched = refs[0], refs[1 : 1 + wide]
        refs = refs[1 + wide :]
        here = lax.axis_index("wide")
    acc_ref, counts_ref, slabs_ref, pair, sems = refs[:5]
    chip = ids[1 + step]
    reads = tile_reads(tiles_ref, pair, sems, chip)
    lay_out(parts, slabs_ref)
    for q, r in enumerate(reads):
        r.wait()
        for g in range(q * ROWS_PER, (q + 1) * ROWS_PER):
            rows = pl.ds(g * BLK, BLK)
            part, count = pair_sum(ids, cols, pair, slabs_ref, g, n, chip)
            acc_ref[rows, :] = acc_in[rows, :] + part if step else part
            counts_ref[rows, :] = counts_in[rows, :] + count if step else count
    if wide:
        for k in range(wide):
            src = target(here, k, wide)
            mask = (off_ref[0, src] * valid[src]).astype(F32)
            at = pl.ds(pl.multiple_of(row[src] * BLK, BLK), BLK)
            acc_ref[at, :] += mm(mask.astype(BF16), fetched[k][...])
            counts_ref[at, :] += mask


def pull(ids, cols, tiles, own, sib, sums, step, off=()):
    g, n = tiles.shape[:2]
    width = own[0].shape[1]
    rows = g * BLK
    wide = 0
    scalars, ins = [], [*own, *sib, *sums]
    specs = [in_hbm()] + [spec(x) for x in ins]
    if off:
        *scalars, off_tiles, fetched = off
        wide = len(fetched)
        ins += [off_tiles, *fetched]
        specs += [spec(x) for x in (off_tiles, *fetched)]
    out = jax.ShapeDtypeStruct((rows, width), F32)
    return pl.pallas_call(
        partial(pull_kernel, n=n, step=step, chunks=len(own), wide=wide),
        grid_spec=pltpu.PrefetchScalarGridSpec(
            num_scalar_prefetch=2 + len(scalars),
            grid=(1,),
            in_specs=specs,
            out_specs=[spec(out)] * 2,
            scratch_shapes=[
                pltpu.VMEM((2, rows, width), BF16),
                pltpu.VMEM((g, 2, BLK, BLK), jnp.int32),
                pltpu.SemaphoreType.DMA((g // ROWS_PER,)),
            ],
        ),
        out_shape=[out] * 2,
        compiler_params=params(),
        cost_estimate=cost(4 * rows * BLK * width, 12 * rows * width),
        name=f"pull{step}",
    )(ids, cols, *scalars, tiles, *ins)


def serve_kernel(*refs, wide):
    asked, feat_ref, outs = refs[:wide], refs[wide], refs[wide + 1 :]
    here = lax.axis_index("wide")
    for k in range(wide):
        outs[k][...] = block(feat_ref, asked[k][here])


def serve(asked, features):
    wide = len(asked)
    out = jax.ShapeDtypeStruct((BLK, features.shape[1]), features.dtype)
    return pl.pallas_call(
        partial(serve_kernel, wide=wide),
        grid_spec=pltpu.PrefetchScalarGridSpec(
            num_scalar_prefetch=wide,
            grid=(1,),
            in_specs=[spec(features)],
            out_specs=[spec(out)] * wide,
        ),
        out_shape=[out] * wide,
        compiler_params=params(),
        cost_estimate=cost(0, 4 * features.size),
        name="serve",
    )(*asked, features)


def place(cols, tiles_ref, signal_rows, place_ref, g, core, chip, n):
    for j in range(2):
        which = core if j == 0 else 1 - core
        at = pl.ds(pl.multiple_of(cols[g * n + chip * 2 + which] * BLK, BLK), BLK)
        place_ref[j, at, :] += mm(tiles_ref[g, chip * 2 + which], signal_rows, 0, 0)


def middle_kernel(
    ids, cols, tiles_ref, cot_ref, acc_ref, counts_ref, feat_ref, wself_ref, wneigh_ref, bias_ref,
    *refs, n, steps, chunks,
):
    parts, refs = refs[: 2 * chunks], refs[2 * chunks :]
    out_hbm, gp_ref, agg_ref, sig_ref, keep_ref, send_ref = refs[:6]
    place_ref, slabs_ref, out, out_sems = refs[6:]
    core, last, first = ids[0], ids[steps], ids[2]
    tall = ROWS_PER * BLK
    count = feat_ref.shape[0] // tall

    def rows_of(q):
        return pl.ds(q * tall, tall)

    writes = [
        pltpu.make_async_copy(out.at[rows_of(q)], out_hbm.at[rows_of(q)], out_sems.at[q])
        for q in range(count)
    ]
    place_ref[...] = jnp.zeros_like(place_ref)
    lay_out(parts, slabs_ref)
    ones = jnp.ones((BLK, BLK), BF16)
    slope = 0.7978845608028654
    for q in range(count):
        rows = rows_of(q)
        both = [
            pair_sum(ids, cols, tiles_ref, slabs_ref, g, n, last, last * 2)
            for g in range(q * ROWS_PER, (q + 1) * ROWS_PER)
        ]
        gathered = acc_ref[rows, :] + jnp.concatenate([b[0] for b in both], axis=0)
        counts = counts_ref[rows, :] + jnp.concatenate([b[1] for b in both], axis=0)
        inverse = 1.0 / (mm(counts.astype(BF16), ones) + 1.0)
        aggregate = (gathered * inverse).astype(BF16)
        agg_ref[rows, :] = aggregate
        pre = mm(feat_ref[rows, :], wself_ref[...]) + mm(aggregate, wneigh_ref[...])
        pre = pre + bias_ref[...].astype(F32)
        square = pre * pre
        bent = jnp.tanh(slope * (pre + 0.044715 * (square * pre)))
        half = 0.5 * (1.0 + bent)
        out[rows, :] = (pre * half).astype(BF16)
        writes[q].start()
        deriv = half + (0.5 * pre) * (1.0 - bent * bent) * (
            slope + (3 * 0.044715 * slope) * square
        )
        grad_pre = (cot_ref[rows, :].astype(F32) * deriv).astype(BF16)
        gp_ref[rows, :] = grad_pre
        signal = (mm(grad_pre, wneigh_ref[...], 1, 1) * inverse).astype(BF16)
        sig_ref[rows, :] = signal
        for b in range(ROWS_PER):
            rows_b = signal[b * BLK : (b + 1) * BLK]
            place(cols, tiles_ref, rows_b, place_ref, q * ROWS_PER + b, core, first, n)
    keep_ref[...] = place_ref[0].astype(BF16)
    send_ref[...] = place_ref[1].astype(BF16)
    for w in writes:
        w.wait()


def middle(ids, cols, tiles, cot, sums, features, w_self, w_neigh, bias, own, sib, steps):
    g, n = tiles.shape[:2]
    rows, width = features.shape
    outw = w_self.shape[1]
    count = g // ROWS_PER

    def shape(c):
        return jax.ShapeDtypeStruct((rows, c), BF16)

    ins = (*sums, features, w_self, w_neigh, bias, *own, *sib)
    outs = [shape(outw), shape(outw), shape(width), shape(width), shape(width), shape(width)]
    return pl.pallas_call(
        partial(middle_kernel, n=n, steps=steps, chunks=len(own)),
        grid_spec=pltpu.PrefetchScalarGridSpec(
            num_scalar_prefetch=2,
            grid=(1,),
            in_specs=[spec(x) for x in (tiles, cot, *ins)],
            out_specs=[in_hbm()] + [spec(x) for x in outs[1:]],
            scratch_shapes=[
                pltpu.VMEM((2, rows, width), F32),
                pltpu.VMEM((2, rows, width), BF16),
                pltpu.VMEM((rows, outw), BF16),
                pltpu.SemaphoreType.DMA((count,)),
            ],
        ),
        out_shape=outs,
        compiler_params=params(),
        cost_estimate=cost(
            8 * rows * BLK * width + 6 * rows * width * outw, 30 * rows * width, rows * outw
        ),
        name="middle",
    )(ids, cols, tiles, cot, *ins)


def push_kernel(ids, cols, tiles_ref, sig_ref, keep_ref, *refs, n, which):
    *send_refs, place_ref = refs
    parts = len(send_refs) // len(which)
    tall = send_refs[0].shape[0]
    for p, s in enumerate(which):
        place_ref[...] = jnp.zeros_like(place_ref)
        for g in range(tiles_ref.shape[0]):
            rows = sig_ref[g * BLK : (g + 1) * BLK, :]
            place(cols, tiles_ref, rows, place_ref, g, ids[0], ids[1 + s], n)
        keep_ref[p] = place_ref[0].astype(BF16)
        for j in range(parts):
            send_refs[p * parts + j][...] = place_ref[1, pl.ds(j * tall, tall), :].astype(BF16)


def push(ids, cols, signal, tiles, which):
    g, n = tiles.shape[:2]
    rows, width = signal.shape
    count = len(which)
    outs = [jax.ShapeDtypeStruct((count, rows, width), BF16)]
    outs += [jax.ShapeDtypeStruct((rows // PARTS, width), BF16)] * (count * PARTS)
    keeps, *sends = pl.pallas_call(
        partial(push_kernel, n=n, which=which),
        grid_spec=pltpu.PrefetchScalarGridSpec(
            num_scalar_prefetch=2,
            grid=(1,),
            in_specs=[spec(tiles), spec(signal)],
            out_specs=[spec(x) for x in outs],
            scratch_shapes=[pltpu.VMEM((2, rows, width), F32)],
        ),
        out_shape=outs,
        compiler_params=params(),
        cost_estimate=cost(4 * count * rows * BLK * width, 8 * count * rows * width),
        name="push",
    )(ids, cols, tiles, signal)
    return keeps, sends


def half_rows(wide):
    step = 16 * wide
    return (BLK + 1 + step - 1) // step * step


def grads_kernel(
    ids, asked, row, valid, off_ref, sig_ref, feat_ref, agg_ref, gp_ref,
    mine_ref, other_ref, *pushed_refs, wide,
):
    here = lax.axis_index("wide")
    tall = 4 * BLK
    dself = dneigh = dbias = None
    for i in range(feat_ref.shape[0] // tall):
        rows = pl.ds(i * tall, tall)
        gp = gp_ref[rows, :]
        a = mm(feat_ref[rows, :], gp, 0, 0)
        b = mm(agg_ref[rows, :], gp, 0, 0)
        c = jnp.sum(gp.astype(F32), axis=0, keepdims=True)
        dself, dneigh, dbias = (a, b, c) if i == 0 else (dself + a, dneigh + b, dbias + c)
    first = ids[0] == 0
    mine_ref[pl.ds(0, BLK), :] = jnp.where(first, dself, dneigh)
    other_ref[pl.ds(0, BLK), :] = jnp.where(first, dneigh, dself)
    spare = mine_ref.shape[0] - BLK
    mine_ref[pl.ds(BLK, spare), :] = jnp.broadcast_to(dbias, (spare, dbias.shape[1]))
    other_ref[pl.ds(BLK, spare), :] = jnp.broadcast_to(dbias, (spare, dbias.shape[1]))
    for k in range(wide):
        peer = target(here, k, wide)
        mask = (off_ref[0, peer] * valid[peer]).astype(F32).astype(BF16)
        at = pl.ds(pl.multiple_of(row[peer] * BLK, BLK), BLK)
        ref = pushed_refs[k]
        ref[pl.ds(0, BLK), :] = mm(mask, sig_ref[at, :], 0, 0).astype(BF16)
        ref[pl.ds(BLK, 16), :] = jnp.full((16, BLK), asked[peer], jnp.int32).astype(F32).astype(BF16)


def grads(ids, asked, row, valid, off_tiles, signal, features, aggregate, grad_pre):
    wide = off_tiles.shape[1]
    rows, width = features.shape
    outw = grad_pre.shape[1]

    def whole(x):
        return pl.BlockSpec(x.shape, lambda i, *s: (0,) * len(x.shape))

    ins = (off_tiles, signal, features, aggregate, grad_pre)
    outs = [jax.ShapeDtypeStruct((half_rows(wide), outw), F32)] * 2
    outs += [jax.ShapeDtypeStruct((BLK + 16, width), BF16)] * wide
    return pl.pallas_call(
        partial(grads_kernel, wide=wide),
        grid_spec=pltpu.PrefetchScalarGridSpec(
            num_scalar_prefetch=4,
            grid=(1,),
            in_specs=[whole(x) for x in ins],
            out_specs=[whole(x) for x in outs],
        ),
        out_shape=outs,
        compiler_params=params(),
        cost_estimate=cost(8 * rows * width * width, 16 * rows * width),
        name="grads",
    )(ids, asked, row, valid, *ins)


def pack_kernel(mine_ref, come_ref, *refs, wide):
    pushed_refs, msg_refs = refs[:wide], refs[wide:]
    here = lax.axis_index("wide")
    piece = mine_ref.shape[0] // wide
    head = BLK + 16
    for k in range(wide):
        peer = target(here, k, wide)
        rows = pl.ds(pl.multiple_of(peer * piece, 16), piece)
        total = mine_ref[rows, :] + come_ref[rows, :]
        high = total.astype(BF16)
        low = (total - high.astype(F32)).astype(BF16)
        msg_refs[k][pl.ds(0, head), :] = pushed_refs[k][...]
        for j, x in enumerate((high[:, :BLK], high[:, BLK:], low[:, :BLK], low[:, BLK:])):
            msg_refs[k][pl.ds(head + j * piece, piece), :] = x


def pack(mine, come, pushed):
    wide = len(pushed)

    def whole(x):
        return pl.BlockSpec(x.shape, lambda i: (0,) * len(x.shape))

    ins = (mine, come, *pushed)
    tall = BLK + 16 + mine.shape[0] // wide * 4
    outs = [jax.ShapeDtypeStruct((tall, pushed[0].shape[1]), BF16)] * wide
    return pl.pallas_call(
        partial(pack_kernel, wide=wide),
        grid=(1,),
        in_specs=[whole(x) for x in ins],
        out_specs=[whole(x) for x in outs],
        out_shape=outs,
        compiler_params=params(),
        cost_estimate=cost(4 * mine.size, 20 * mine.size),
        name="pack",
    )(*ins)


def piece_sum_kernel(*refs):
    arrived, out_ref = refs[:-1], refs[-1]
    piece = out_ref.shape[0]
    head = BLK + 16
    for side in range(2):
        part = [
            a[pl.ds(head + side * piece, piece), :].astype(F32)
            + a[pl.ds(head + (side + 2) * piece, piece), :].astype(F32)
            for a in arrived
        ]
        out_ref[:, pl.ds(side * BLK, BLK)] = tree_sum(part)


def piece_sum(arrived):
    def whole(x):
        return pl.BlockSpec(x.shape, lambda i: (0,) * len(x.shape))

    piece = (arrived[0].shape[0] - BLK - 16) // 4
    out = jax.ShapeDtypeStruct((piece, 2 * BLK), F32)
    return pl.pallas_call(
        piece_sum_kernel,
        grid=(1,),
        in_specs=[whole(x) for x in arrived],
        out_specs=whole(out),
        out_shape=out,
        compiler_params=params(),
        cost_estimate=cost(arrived[0].size * len(arrived), 2 * arrived[0].size * len(arrived)),
        name="piece_sum",
    )(*arrived)


def half_kernel(*refs, factor):
    pieces, out_ref = refs[:-1], refs[-1]
    wide, piece = len(pieces), pieces[0].shape[0]
    here = lax.axis_index("wide")
    for k in range(wide):
        at = pl.ds(pl.multiple_of(source(here, k, wide) * piece, 16), piece)
        out_ref[at, :] = pieces[k][...] * factor


def half(pieces, factor):
    def whole(x):
        return pl.BlockSpec(x.shape, lambda i: (0, 0))

    out = jax.ShapeDtypeStruct((pieces[0].shape[0] * len(pieces), pieces[0].shape[1]), F32)
    return pl.pallas_call(
        partial(half_kernel, factor=factor),
        grid=(1,),
        in_specs=[whole(x) for x in pieces],
        out_specs=whole(out),
        out_shape=out,
        compiler_params=params(),
        cost_estimate=cost(out.size, 8 * out.size),
        name="half",
    )(*pieces)


def finish_kernel(ids, total_ref, paired_ref, self_ref, neigh_ref, bias_ref):
    first = ids[0] == 0
    total, paired = total_ref[pl.ds(0, BLK), :], paired_ref[pl.ds(0, BLK), :]
    self_ref[...] = jnp.where(first, total, paired)
    neigh_ref[...] = jnp.where(first, paired, total)
    at = pl.ds(BLK, 8)
    bias_ref[...] = jnp.where(first, total_ref[at, :], paired_ref[at, :])[:1]


def finish(ids, total, paired):
    def whole(x):
        return pl.BlockSpec(x.shape, lambda i, *s: (0, 0))

    outs = [jax.ShapeDtypeStruct((r, 2 * BLK), F32) for r in (BLK, BLK, 1)]
    return pl.pallas_call(
        finish_kernel,
        grid_spec=pltpu.PrefetchScalarGridSpec(
            num_scalar_prefetch=1,
            grid=(1,),
            in_specs=[whole(total), whole(paired)],
            out_specs=[whole(x) for x in outs],
        ),
        out_shape=outs,
        compiler_params=params(),
        cost_estimate=cost(4 * total.size, 16 * total.size),
        name="finish",
    )(ids, total, paired)


def base_kernel(gp_ref, wself_ref, keep_ref, *refs, parts):
    come, arrived, out_ref = refs[:parts], refs[parts:-1], refs[-1]
    tall = 4 * BLK
    for i in range(out_ref.shape[0] // tall):
        rows = pl.ds(i * tall, tall)
        out_ref[rows, :] = mm(gp_ref[rows, :], wself_ref[...], 1, 1) + keep_ref[rows, :].astype(F32)
    tall = come[0].shape[0]
    for j, part in enumerate(come):
        out_ref[pl.ds(j * tall, tall), :] += part[...].astype(F32)
    line = lax.broadcasted_iota(jnp.int32, (16, BLK), 0)
    for a in arrived:
        index = jnp.max(jnp.where(line == 0, a[pl.ds(BLK, 16), :].astype(F32), 0.0))
        at = pl.ds(pl.multiple_of(index.astype(jnp.int32) * BLK, BLK), BLK)
        out_ref[at, :] += a[pl.ds(0, BLK), :].astype(F32)


def base(grad_pre, w_self, keeps, come, arrived):
    count, rows, width = keeps.shape
    slab = pl.BlockSpec((None, rows, width), lambda i: (count - 1, 0, 0))
    head = pl.BlockSpec((BLK + 16, width), lambda i: (0, 0))
    out = jax.ShapeDtypeStruct((rows, width), F32)
    return pl.pallas_call(
        partial(base_kernel, parts=len(come)),
        grid=(1,),
        in_specs=[spec(grad_pre), spec(w_self), slab]
        + [spec(x) for x in come]
        + [head] * len(arrived),
        out_specs=spec(out),
        out_shape=out,
        compiler_params=params(),
        cost_estimate=cost(4 * rows * width * width, 12 * rows * width),
        name="base",
    )(grad_pre, w_self, keeps, *come, *arrived)


def joined_kernel(*refs, more):
    out_ref = refs[-1]
    keep_ref, parts = refs[more], refs[more + 1 : -1]
    tall = parts[0].shape[0]
    for j, part in enumerate(parts):
        rows = pl.ds(j * tall, tall)
        total = keep_ref[rows, :].astype(F32) + part[...].astype(F32)
        if more:
            total = total + refs[0][rows, :].astype(F32)
        out_ref[rows, :] = total.astype(BF16)


def joined(got, keeps, come, s):
    _, rows, width = keeps.shape
    keep = pl.BlockSpec((None, rows, width), lambda i: (s, 0, 0))
    more = () if got is None else (got,)
    out = jax.ShapeDtypeStruct((rows, width), BF16)
    return pl.pallas_call(
        partial(joined_kernel, more=len(more)),
        grid=(1,),
        in_specs=[spec(x) for x in more] + [keep] + [spec(x) for x in come],
        out_specs=spec(out),
        out_shape=out,
        compiler_params=params(),
        cost_estimate=cost(3 * rows * width, 8 * rows * width),
        name=f"joined{s}",
    )(*more, keeps, *come)


def last_kernel(rest_ref, *refs):
    got, out_ref = refs[:-1], refs[-1]
    tall = got[0].shape[0]
    for j, ref in enumerate(got):
        rows = pl.ds(j * tall, tall)
        out_ref[rows, :] = rest_ref[rows, :] + ref[...].astype(F32)


def last(rest, got):
    def whole(x):
        return pl.BlockSpec(x.shape, lambda i: (0, 0))

    return pl.pallas_call(
        last_kernel,
        grid=(1,),
        in_specs=[whole(x) for x in (rest, *got)],
        out_specs=whole(rest),
        out_shape=jax.ShapeDtypeStruct(rest.shape, F32),
        compiler_params=params(),
        cost_estimate=cost(rest.size, 10 * rest.size),
        name="last",
    )(rest, *got)


def power(size):
    return size & (size - 1) == 0


def target(i, k, size):
    return i ^ k if power(size) else lax.rem(i + k, size)


def source(i, k, size):
    return i ^ k if power(size) else lax.rem(i + size - k, size)


def to_peer(x, axis, k):
    size = lax.axis_size(axis)
    return lax.ppermute(x, axis, [(i, i ^ k if power(size) else (i + k) % size) for i in range(size)])


def back_to(x, axis, k):
    size = lax.axis_size(axis)
    return to_peer(x, axis, k if power(size) else size - k)


def tree_sum(parts):
    while len(parts) > 1:
        pairs = [a + b for a, b in zip(parts[::2], parts[1::2])]
        parts = pairs + parts[len(pairs) * 2 :]
    return parts[0]


def shards(
    features,
    band_tiles,
    band_cols,
    off_tiles,
    req_block,
    req_row,
    req_valid,
    weight_self,
    weight_neigh,
    bias_term,
    cotangent,
):
    row_count, width = features.shape
    n = lax.axis_size("narrow")
    wide = lax.axis_size("wide")
    steps = n // 2
    fold = [0] + list(range(1, steps, 2)) + list(range(2, steps, 2))[::-1]
    after = {a: b for a, b in zip(fold, fold[1:] + fold[:1])}

    def onward(x):
        return lax.ppermute(x, "narrow", [(i, after[i // 2] * 2 + i % 2) for i in range(n)])

    def swap(x):
        return to_peer(x, "narrow", 1)

    me = lax.axis_index("narrow")
    here = lax.axis_index("wide")
    chips = jnp.array(
        [[fold[(fold.index(z) - s) % steps] for s in range(steps)] for z in range(steps)], jnp.int32
    )[me // 2]
    ids = jnp.concatenate([(me % 2)[None].astype(jnp.int32), chips])
    cols = band_cols.reshape(-1)
    asked, row, valid = req_block[0], req_row[0], req_valid[0]
    def tie(*xs):
        return lax.optimization_barrier(xs)

    def cut(x):
        tall = row_count // CHUNKS
        return [x] if CHUNKS == 1 else [lax.slice_in_dim(x, j * tall, (j + 1) * tall) for j in range(CHUNKS)]

    tiles = band_tiles
    slabs, pairs = [cut(features)], []
    asked_of_me = [asked] + [to_peer(asked, "wide", k) for k in range(1, wide)]
    sums = ()
    for s in range(1, steps):
        following = [onward(x) for x in slabs[-1]]
        pairs.append([swap(x) for x in slabs[-1]])
        off = (row, valid, off_tiles, fetched) if s == steps - 1 else ()
        sums = pull(ids, cols, tiles, slabs[-1], pairs[-1], sums, s - 1, off)
        following[-1], *sums = tie(following[-1], *sums)
        if s == 1:
            following[-1], *asked_of_me = tie(following[-1], *asked_of_me)
            served = serve(asked_of_me, features)
            fetched = [served[0]] + [back_to(served[k], "wide", k) for k in range(1, wide)]
        elif s == 2:
            following[-1], *fetched = tie(following[-1], *fetched)
        slabs.append(following)
        if s == steps - 2:
            halved = halve(tiles)
            halved, *sums = tie(halved, *sums)
    pairs.append([swap(x) for x in slabs[-1]])
    layer_out, grad_pre, aggregate, signal, keep, send = middle(
        ids, cols, halved, cotangent, sums, features, weight_self, weight_neigh,
        bias_term.reshape(1, -1), slabs[-1], pairs[-1], steps,
    )

    come = swap(send)
    keep2, send2 = push(ids, cols, signal, halved, (2 % steps,))
    mine, other, *pushed = grads(
        ids, asked, row, valid, off_tiles, signal, features, aggregate, grad_pre
    )
    come, mine, other, keep2, *more = tie(come, mine, other, keep2, *send2, *pushed)
    send2, pushed = more[: len(send2)], more[len(send2) :]
    got = onward(joined(None, keep[None], [come], 0))
    come2 = [swap(x) for x in send2]
    packed = pack(mine, swap(other), pushed)
    arrived = [packed[0]] + [to_peer(packed[k], "wide", k) for k in range(1, wide)]
    total = piece_sum(arrived)
    if not power(steps):
        total = lax.psum(total, "narrow", axis_index_groups=[list(range(c, n, 2)) for c in (0, 1)])
    later = tuple((s + 3) % steps for s in range(steps - 2))
    k = 1
    for s in range(steps - 2):
        if power(steps) and k < steps:
            total = total + to_peer(total, "narrow", 2 * k)
            k *= 2
        got, total = tie(got, total)
        if s == 0:
            got, signal = tie(got, signal)
            going = joined(got, keep2, come2, 0)
            keeps, sends = push(ids, cols, signal, halved, later)
            comes = [swap(x) for x in sends]
            rest = base(grad_pre, weight_self, keeps, comes[-PARTS:], arrived)
        else:
            if s == 1:
                got, rest = tie(got, rest)
            going = joined(got, keeps, comes[(s - 1) * PARTS : s * PARTS], s - 1)
        got = onward(going)
    while power(steps) and k < steps:
        total = total + to_peer(total, "narrow", 2 * k)
        k *= 2
    pieces = [total] + [to_peer(total, "wide", k) for k in range(1, wide)]
    whole = half(pieces, (wide * n * row_count) ** (-0.5))
    grad_self, grad_neigh, grad_bias = finish(ids, whole, swap(whole))
    got, grad_self, grad_neigh, grad_bias = tie(got, grad_self, grad_neigh, grad_bias)
    grad_features = last(rest, [got])
    return layer_out, grad_features, grad_self, grad_neigh, grad_bias.reshape(-1)


def solution(mesh):
    both = ("wide", "narrow")
    placed = (
        P(both, None),
        P(both, None, None, None),
        P(both, None),
        P(both, None, None, None),
        P(both, None),
        P(both, None),
        P(both, None),
        P(),
        P(),
        P(),
        P(both, None),
    )
    return jax.shard_map(
        shards,
        mesh=mesh,
        in_specs=placed,
        out_specs=(P(both, None), P(both, None), P(), P(), P()),
        check_vma=False,
    )
```

time: 116 us -> 108 us (0.931)
  waiting for transfers between devices: 31.5 us -> 49.8 us
  starting transfers between devices: 43.7 us -> 31.8 us
  local copies, waits for them, and re-layouts: 16.7 us -> 6.02 us
  Pallas kernels: 23 us -> 19.4 us
    ppermute x12 -> x6, starting transfers between devices: 24.3 us -> 9.47 us  [onward(): lax.ppermute(x, 'narrow', [(i, after[i // 2] * 2 + i % 2) for i in range(...]
    ppermute x23 -> x27, waiting for transfers between devices: 12 us -> 24.2 us  [to_peer(): lax.ppermute(x, axis, [(i, i ^ k if power(size) else (i + k) % size) for...]
    unnamed x43 -> x25, local copies, waits for them, and re-layouts: 14.8 us -> 5.24 us
    ppermute x12 -> x6, waiting for transfers between devices: 19.5 us -> 25.6 us  [onward(): lax.ppermute(x, 'narrow', [(i, after[i // 2] * 2 + i % 2) for i in range(...]
    pallas_call x14 -> x12, Pallas kernels: 19.5 us -> 15.8 us  [the longest x1 5.45 us: middle(): pl.pallas_call(partial(middle_kernel, n=n, steps=steps, chunks=len(own)),...]
    ppermute x23 -> x27, starting transfers between devices: 19.4 us -> 22.4 us  [to_peer(): lax.ppermute(x, axis, [(i, i ^ k if power(size) else (i + k) % size) for...]
  transfers between devices with their start and end apart: 35 -> 33, of which waited for: 17 -> 16; matrix products, arithmetic and copies ran while one was open for 1% -> 2% of each run, Pallas kernels for 11% -> 11%
where the time goes in v3:
time: 108 us
  waiting for transfers between devices  49.8 us (46%)
  starting transfers between devices  31.8 us (29%)
  Pallas kernels  19.4 us (18%)
  local copies, waits for them, and re-layouts  6.02 us (6%)
    ppermute x6, waiting for transfers between devices, onward(): lax.ppermute(x, 'narrow', [(i, after[i // 2] * 2 + i % 2) for i in range(...  25.6 us
    ppermute x27, waiting for transfers between devices, to_peer(): lax.ppermute(x, axis, [(i, i ^ k if power(size) else (i + k) % size) for...  24.2 us
    ppermute x27, starting transfers between devices, to_peer(): lax.ppermute(x, axis, [(i, i ^ k if power(size) else (i + k) % size) for...  22.4 us
    ppermute x6, starting transfers between devices, onward(): lax.ppermute(x, 'narrow', [(i, after[i // 2] * 2 + i % 2) for i in range(...  9.47 us
    pallas_call x1, Pallas kernels, middle(): pl.pallas_call(partial(middle_kernel, n=n, steps=steps, chunks=len(own)),...  5.45 us
    unnamed x25, local copies, waits for them, and re-layouts  5.24 us
    pallas_call x3, Pallas kernels, pull(): pl.pallas_call(partial(pull_kernel, n=n, step=step, chunks=len(own), wide...  5.21 us
    pallas_call x2, Pallas kernels, push(): pl.pallas_call(partial(push_kernel, n=n, which=which), grid_spec=pltpu.Pr...  2.99 us
  transfers between devices with their start and end apart: 33, of which 16 were waited for; matrix products, arithmetic and copies ran while one was open for 2% of the time, Pallas kernels for 11%

profile of v3, /device:TPU:0, one launch (start us, length us, event | category | flops | bytes accessed | tf_op | source)
XLA Modules:
  0.0 108.1 jit_solution(18079488132159513478)
XLA Ops:
  1.2 2.6 %collective-permute-start = (bf16[2048,128]{1,0:T(8,128)(2,1)}, bf16[2048,128]{1,0:T(8,128)(2,1)S(1)}, u32[]{:S(2)}, u32[]{:S(2)}) collective-permute-start(bf16[2048,128]{1,0:T(8,128)(2,1)} %feat_ref.3), channel_id=1, source_target_pairs={{0,2},{1,3},{2,6},{3,7},{4,0},{5,1},{6,4},{7,5},{8,10},{9,11},{10,... | collective-permute-start | bytes 1572872 | tf_op jit(solution)/shard_map/ppermute | solution.py:639
  3.8 2.4 %collective-permute-start.4 = (s32[4]{0:T(128)}, s32[4]{0:T(128)S(1)}, u32[]{:S(2)}, u32[]{:S(2)}) collective-permute-start(s32[4]{0:T(128)} %bitcast.13), channel_id=1, source_target_pairs={{0,24},{8,16},{16,8},{24,0},{1,25},{9,17},{17,9},{25,1},{2,26},{10... | collective-permute-start | bytes 56 | tf_op jit(solution)/shard_map/ppermute | solution.py:603
  8.9 3.4 %copy-done = s32[16,8,128,128]{3,2,1,0:T(8,128)S(1)} copy-done((s32[16,8,128,128]{3,2,1,0:T(8,128)S(1)}, s32[16,8,128,128]{3,2,1,0:T(8,128)}, u32[]{:S(2)}) %copy-start) | copy-done | bytes 8388632
  13.3 1.7 %pull0.1 = (f32[2048,128]{1,0:T(8,128)S(1)}, f32[2048,128]{1,0:T(8,128)S(1)}) custom-call(s32[5]{0:T(128)S(1)} %pad_add_fusion.ids, s32[128]{0:T(128)S(1)} %reshape.19.cols, s32[16,8,128,128]{3,2,1,0:T(8,128)S(1)} %copy-done, bf16[2048,128]{1,0:T(8,128)(2,1)S(1)} %copy-done.2, bf16[2048,128]{1,0:T(8,128)(2,1)S(1)} %collective-permute-done.1.refs_2_), custom_call_target="tpu_custom_call" | custom-call | flops 134217728 | bytes 3145728 | tf_op jit(solution)/shard_map/pull0/pallas_call | solution.py:139
  15.0 2.5 %collective-permute-done.refs_1_ = bf16[2048,128]{1,0:T(8,128)(2,1)S(1)} collective-permute-done((bf16[2048,128]{1,0:T(8,128)(2,1)}, bf16[2048,128]{1,0:T(8,128)(2,1)S(1)}, u32[]{:S(2)}, u32[]{:S(2)}) %collective-permute-start) | collective-permute-done | bytes 524320 | tf_op jit(solution)/shard_map/ppermute | solution.py:639
  19.2 1.6 %collective-permute-start.7 = (bf16[128,128]{1,0:T(8,128)(2,1)S(1)}, bf16[128,128]{1,0:T(8,128)(2,1)S(1)}, u32[]{:S(2)}, u32[]{:S(2)}) collective-permute-start(bf16[128,128]{1,0:T(8,128)(2,1)S(1)} %get-tuple-element.103), channel_id=1, source_target_pairs={{0,8},{8,0},{16,24},{24,16},{1,9},{9,1},{17,25},{25,17},{2,10},{10... | collective-permute-start | bytes 98312 | tf_op jit(solution)/shard_map/ppermute | solution.py:603
  22.8 1.7 %pull1.1 = (f32[2048,128]{1,0:T(8,128)S(1)}, f32[2048,128]{1,0:T(8,128)S(1)}) custom-call(s32[5]{0:T(128)S(1)} %pad_add_fusion.ids, s32[128]{0:T(128)S(1)} %reshape.19.cols, s32[16,8,128,128]{3,2,1,0:T(8,128)S(1)} %copy-done.1, bf16[2048,128]{1,0:T(8,128)(2,1)S(1)} %collective-permute-done.refs_1_, bf16[2048,128]{1,0:T(8,128)(2,1)S(1)} %collective-permute-done.6.refs_2_, ...), custom_call_target="tpu_custom_call" | custom-call | flops 134217728 | bytes 3145728 | tf_op jit(solution)/shard_map/pull1/pallas_call | solution.py:139
  24.6 8.3 %collective-permute-done.5.refs_3_ = bf16[2048,128]{1,0:T(8,128)(2,1)S(1)} collective-permute-done((bf16[2048,128]{1,0:T(8,128)(2,1)S(1)}, bf16[2048,128]{1,0:T(8,128)(2,1)S(1)}, u32[]{:S(2)}, u32[]{:S(2)}) %collective-permute-start.5) | collective-permute-done | bytes 524320 | tf_op jit(solution)/shard_map/ppermute | solution.py:639
  34.9 1.8 %pull2.1 = (f32[2048,128]{1,0:T(8,128)S(1)}, f32[2048,128]{1,0:T(8,128)S(1)}) custom-call(s32[5]{0:T(128)S(1)} %pad_add_fusion.ids, s32[128]{0:T(128)S(1)} %reshape.19.cols, s32[4]{0:T(128)S(1)} %bitcast.9, s32[4]{0:T(128)S(1)} %bitcast.11, s32[16,8,128,128]{3,2,1,0:T(8,128)S(1)} %copy-done.1, bf16[2048,128]{1,0:T(8,128)(2,1)S(1)} %collective-permute-done.5.refs_3_, ...), custom_call_target="tpu_custom_call" | custom-call | flops 134217728 | bytes 3145728 | tf_op jit(solution)/shard_map/pull2/pallas_call | solution.py:139
  36.7 11.5 %collective-permute-done.10.refs_0_ = bf16[2048,128]{1,0:T(8,128)(2,1)S(1)} collective-permute-done((bf16[2048,128]{1,0:T(8,128)(2,1)S(1)}, bf16[2048,128]{1,0:T(8,128)(2,1)S(1)}, u32[]{:S(2)}, u32[]{:S(2)}) %collective-permute-start.10) | collective-permute-done | bytes 524320 | tf_op jit(solution)/shard_map/ppermute | solution.py:639
  48.2 1.9 %collective-permute-done.12.refs_1_ = bf16[2048,128]{1,0:T(8,128)(2,1)S(1)} collective-permute-done((bf16[2048,128]{1,0:T(8,128)(2,1)S(1)}, bf16[2048,128]{1,0:T(8,128)(2,1)S(1)}, u32[]{:S(2)}, u32[]{:S(2)}) %collective-permute-start.12) | collective-permute-done | bytes 524320 | tf_op jit(solution)/shard_map/ppermute | solution.py:603
  50.1 5.5 %middle.1 = (bf16[2048,256]{1,0:T(8,128)(2,1)}, bf16[2048,256]{1,0:T(8,128)(2,1)S(1)}, bf16[2048,128]{1,0:T(8,128)(2,1)S(1)}, bf16[2048,128]{1,0:T(8,128)(2,1)S(...) custom-call(s32[5]{0:T(128)S(1)} %pad_add_fusion.ids, s32[128]{0:T(128)S(1)} %reshape.19.cols, ...), custom_call_target="tpu_custom_call" | custom-call | flops 671088640 | bytes 7864320 | tf_op jit(solution)/shard_map/middle/pallas_call | solution.py:258
  60.7 1.6 %collective-permute-start.16 = (bf16[336,128]{1,0:T(8,128)(2,1)S(1)}, bf16[336,128]{1,0:T(8,128)(2,1)S(1)}, u32[]{:S(2)}, u32[]{:S(2)}) collective-permute-start(bf16[336,128]{1,0:T(8,128)(2,1)S(1)} %get-tuple-element.141), channel_id=1, source_target_pairs={{0,8},{8,0},{16,24},{24,16},{1,9},{9,1},{17,25},{25,17},{2,10},{10... | collective-permute-start | bytes 258056 | tf_op jit(solution)/shard_map/ppermute | solution.py:603
  63.8 1.6 %collective-permute-done.16.refs_1_.refs_3_ = bf16[336,128]{1,0:T(8,128)(2,1)S(1)} collective-permute-done((bf16[336,128]{1,0:T(8,128)(2,1)S(1)}, bf16[336,128]{1,0:T(8,128)(2,1)S(1)}, u32[]{:S(2)}, u32[]{:S(2)}) %collective-permute-start.16) | collective-permute-done | bytes 86048 | tf_op jit(solution)/shard_map/ppermute | solution.py:603
  65.3 2.4 %collective-permute-start.18 = (bf16[336,128]{1,0:T(8,128)(2,1)S(1)}, bf16[336,128]{1,0:T(8,128)(2,1)S(1)}, u32[]{:S(2)}, u32[]{:S(2)}) collective-permute-start(bf16[336,128]{1,0:T(8,128)(2,1)S(1)} %get-tuple-element.143), channel_id=1, source_target_pairs={{0,24},{8,16},{16,8},{24,0},{1,25},{9,17},{17,9},{25,1},{2,26},{10... | collective-permute-start | bytes 258056 | tf_op jit(solution)/shard_map/ppermute | solution.py:603
  67.8 2.9 %collective-permute-done.18.refs_3_.refs_5_ = bf16[336,128]{1,0:T(8,128)(2,1)S(1)} collective-permute-done((bf16[336,128]{1,0:T(8,128)(2,1)S(1)}, bf16[336,128]{1,0:T(8,128)(2,1)S(1)}, u32[]{:S(2)}, u32[]{:S(2)}) %collective-permute-start.18) | collective-permute-done | bytes 86048 | tf_op jit(solution)/shard_map/ppermute | solution.py:603
  70.7 3.4 %collective-permute-start.19 = (f32[48,256]{1,0:T(8,128)S(1)}, f32[48,256]{1,0:T(8,128)S(1)}, u32[]{:S(2)}, u32[]{:S(2)}) collective-permute-start(f32[48,256]{1,0:T(8,128)S(1)} %piece_sum.1), channel_id=1, source_target_pairs={{0,2},{1,3},{2,0},{3,1},{4,6},{5,7},{6,4},{7,5},{8,10},{9,11},{10,... | collective-permute-start | bytes 147464 | tf_op jit(solution)/shard_map/ppermute | solution.py:603
  74.2 2.1 %collective-permute-done.19 = f32[48,256]{1,0:T(8,128)S(1)} collective-permute-done((f32[48,256]{1,0:T(8,128)S(1)}, f32[48,256]{1,0:T(8,128)S(1)}, u32[]{:S(2)}, u32[]{:S(2)}) %collective-permute-start.19) | collective-permute-done | bytes 49184 | tf_op jit(solution)/shard_map/ppermute | solution.py:603
  76.5 2.3 %collective-permute-start.22 = (bf16[2048,128]{1,0:T(8,128)(2,1)S(1)}, bf16[2048,128]{1,0:T(8,128)(2,1)S(1)}, u32[]{:S(2)}, u32[]{:S(2)}) collective-permute-start(bf16[2048,128]{1,0:T(8,128)(2,1)S(1)} %joined0.4), channel_id=1, source_target_pairs={{0,2},{1,3},{2,6},{3,7},{4,0},{5,1},{6,4},{7,5},{8,10},{9,11},{10,... | collective-permute-start | bytes 1572872 | tf_op jit(solution)/shard_map/ppermute | solution.py:639
  79.5 1.7 %push.3 = (bf16[2,2048,128]{2,1,0:T(8,128)(2,1)S(1)}, bf16[1024,128]{1,0:T(8,128)(2,1)S(1)}, bf16[1024,128]{1,0:T(8,128)(2,1)S(1)}, bf16[1024,128]{1,0:T(8,128)(2,1)S(1)}, bf16[1024,128]{1,0:T(8,128)(2,1)S(1)}) custom-call(s32[5]{0:T(128)S(1)} %pad_add_fusion.ids, s32[128]{0:T(128)S(1)} %reshape.19.cols, bf16[16,8,128,128]{3,2,1,0:T(8,128)(2,1)S(1)} %halve.1.tiles_ref, ...), custom_call_target="tpu_custom_call" | custom-call | flops 268435456 | bytes 4194304 | tf_op jit(solution)/shard_map/push/pallas_call | solution.py:301
  81.9 8.5 %collective-permute-done.23 = f32[48,256]{1,0:T(8,128)S(1)} collective-permute-done((f32[48,256]{1,0:T(8,128)S(1)}, f32[48,256]{1,0:T(8,128)S(1)}, u32[]{:S(2)}, u32[]{:S(2)}) %collective-permute-start.23) | collective-permute-done | bytes 49184 | tf_op jit(solution)/shard_map/ppermute | solution.py:603
  92.1 1.8 %collective-permute-start.28 = (bf16[2048,128]{1,0:T(8,128)(2,1)S(1)}, bf16[2048,128]{1,0:T(8,128)(2,1)S(1)}, u32[]{:S(2)}, u32[]{:S(2)}) collective-permute-start(bf16[2048,128]{1,0:T(8,128)(2,1)S(1)} %joined0.5), channel_id=1, source_target_pairs={{0,2},{1,3},{2,6},{3,7},{4,0},{5,1},{6,4},{7,5},{8,10},{9,11},{10,... | collective-permute-start | bytes 1572872 | tf_op jit(solution)/shard_map/ppermute | solution.py:639
  93.9 2.5 %collective-permute-start.31 = (f32[48,256]{1,0:T(8,128)S(1)}, f32[48,256]{1,0:T(8,128)S(1)}, u32[]{:S(2)}, u32[]{:S(2)}) collective-permute-start(f32[48,256]{1,0:T(8,128)S(1)} %add.17.refs_0_), channel_id=1, source_target_pairs={{0,24},{8,16},{16,8},{24,0},{1,25},{9,17},{17,9},{25,1},{2,26},{10... | collective-permute-start | bytes 147464 | tf_op jit(solution)/shard_map/ppermute | solution.py:603
  103.7 3.3 %collective-permute-done.28.refs_0_ = bf16[2048,128]{1,0:T(8,128)(2,1)S(1)} collective-permute-done((bf16[2048,128]{1,0:T(8,128)(2,1)S(1)}, bf16[2048,128]{1,0:T(8,128)(2,1)S(1)}, u32[]{:S(2)}, u32[]{:S(2)}) %collective-permute-start.28) | collective-permute-done | bytes 524320 | tf_op jit(solution)/shard_map/ppermute | solution.py:639
  (91 shorter events, 28.2 us)
Async XLA Ops:
  0.6 8.3 %collective-permute-start.1 = (bf16[2048,128]{1,0:T(8,128)(2,1)}, bf16[2048,128]{1,0:T(8,128)(2,1)S(1)}, u32[]{:S(2)}, u32[]{:S(2)}) collective-permute-start(bf16[2048,128]{1,0:T(8,128)(2,1)} %feat_ref.3), channel_id=1, source_target_pairs={{0,1},{1,0},{2,3},{3,2},{4,5},{5,4},{6,7},{7,6},{8,9},{9,8},{10,11... | collective-permute-start | bytes 1572872 | tf_op jit(solution)/shard_map/ppermute | solution.py:603
  1.2 16.4 %collective-permute-start = (bf16[2048,128]{1,0:T(8,128)(2,1)}, bf16[2048,128]{1,0:T(8,128)(2,1)S(1)}, u32[]{:S(2)}, u32[]{:S(2)}) collective-permute-start(bf16[2048,128]{1,0:T(8,128)(2,1)} %feat_ref.3), channel_id=1, source_target_pairs={{0,2},{1,3},{2,6},{3,7},{4,0},{5,1},{6,4},{7,5},{8,10},{9,11},{10,... | collective-permute-start | bytes 1572872 | tf_op jit(solution)/shard_map/ppermute | solution.py:639
  3.8 13.8 %collective-permute-start.4 = (s32[4]{0:T(128)}, s32[4]{0:T(128)S(1)}, u32[]{:S(2)}, u32[]{:S(2)}) collective-permute-start(s32[4]{0:T(128)} %bitcast.13), channel_id=1, source_target_pairs={{0,24},{8,16},{16,8},{24,0},{1,25},{9,17},{17,9},{25,1},{2,26},{10... | collective-permute-start | bytes 56 | tf_op jit(solution)/shard_map/ppermute | solution.py:603
  6.2 11.3 %collective-permute-start.3 = (s32[4]{0:T(128)}, s32[4]{0:T(128)S(1)}, u32[]{:S(2)}, u32[]{:S(2)}) collective-permute-start(s32[4]{0:T(128)} %bitcast.14), channel_id=1, source_target_pairs={{0,16},{8,24},{16,0},{24,8},{1,17},{9,25},{17,1},{25,9},{2,18},{10... | collective-permute-start | bytes 56 | tf_op jit(solution)/shard_map/ppermute | solution.py:603
  6.8 10.8 %collective-permute-start.2 = (s32[4]{0:T(128)}, s32[4]{0:T(128)S(1)}, u32[]{:S(2)}, u32[]{:S(2)}) collective-permute-start(s32[4]{0:T(128)} %bitcast.15), channel_id=1, source_target_pairs={{0,8},{8,0},{16,24},{24,16},{1,9},{9,1},{17,25},{25,17},{2,10},{10... | collective-permute-start | bytes 56 | tf_op jit(solution)/shard_map/ppermute | solution.py:603
  17.6 5.2 %collective-permute-start.6 = (bf16[2048,128]{1,0:T(8,128)(2,1)S(1)}, bf16[2048,128]{1,0:T(8,128)(2,1)S(1)}, u32[]{:S(2)}, u32[]{:S(2)}) collective-permute-start(bf16[2048,128]{1,0:T(8,128)(2,1)S(1)} %collective-permute-done.refs_1_), channel_id=1, source_target_pairs={{0,1},{1,0},{2,3},{3,2},{4,5},{5,4},{6,7},{7,6},{8,9},{9,8},{10,11... | collective-permute-start | bytes 1572872 | tf_op jit(solution)/shard_map/ppermute | solution.py:603
  17.6 15.2 %collective-permute-start.5 = (bf16[2048,128]{1,0:T(8,128)(2,1)S(1)}, bf16[2048,128]{1,0:T(8,128)(2,1)S(1)}, u32[]{:S(2)}, u32[]{:S(2)}) collective-permute-start(bf16[2048,128]{1,0:T(8,128)(2,1)S(1)} %collective-permute-done.refs_1_), channel_id=1, source_target_pairs={{0,2},{1,3},{2,6},{3,7},{4,0},{5,1},{6,4},{7,5},{8,10},{9,11},{10,... | collective-permute-start | bytes 1572872 | tf_op jit(solution)/shard_map/ppermute | solution.py:639
  19.2 13.6 %collective-permute-start.7 = (bf16[128,128]{1,0:T(8,128)(2,1)S(1)}, bf16[128,128]{1,0:T(8,128)(2,1)S(1)}, u32[]{:S(2)}, u32[]{:S(2)}) collective-permute-start(bf16[128,128]{1,0:T(8,128)(2,1)S(1)} %get-tuple-element.103), channel_id=1, source_target_pairs={{0,8},{8,0},{16,24},{24,16},{1,9},{9,1},{17,25},{25,17},{2,10},{10... | collective-permute-start | bytes 98312 | tf_op jit(solution)/shard_map/ppermute | solution.py:603
  20.8 12.1 %collective-permute-start.8 = (bf16[128,128]{1,0:T(8,128)(2,1)S(1)}, bf16[128,128]{1,0:T(8,128)(2,1)S(1)}, u32[]{:S(2)}, u32[]{:S(2)}) collective-permute-start(bf16[128,128]{1,0:T(8,128)(2,1)S(1)} %get-tuple-element.104), channel_id=1, source_target_pairs={{0,16},{8,24},{16,0},{24,8},{1,17},{9,25},{17,1},{25,9},{2,18},{10... | collective-permute-start | bytes 98312 | tf_op jit(solution)/shard_map/ppermute | solution.py:603
  22.3 10.6 %collective-permute-start.9 = (bf16[128,128]{1,0:T(8,128)(2,1)S(1)}, bf16[128,128]{1,0:T(8,128)(2,1)S(1)}, u32[]{:S(2)}, u32[]{:S(2)}) collective-permute-start(bf16[128,128]{1,0:T(8,128)(2,1)S(1)} %get-tuple-element.105), channel_id=1, source_target_pairs={{0,24},{8,16},{16,8},{24,0},{1,25},{9,17},{17,9},{25,1},{2,26},{10... | collective-permute-start | bytes 98312 | tf_op jit(solution)/shard_map/ppermute | solution.py:603
  33.0 15.2 %collective-permute-start.10 = (bf16[2048,128]{1,0:T(8,128)(2,1)S(1)}, bf16[2048,128]{1,0:T(8,128)(2,1)S(1)}, u32[]{:S(2)}, u32[]{:S(2)}) collective-permute-start(bf16[2048,128]{1,0:T(8,128)(2,1)S(1)} %collective-permute-done.5.refs_3_), channel_id=1, source_target_pairs={{0,2},{1,3},{2,6},{3,7},{4,0},{5,1},{6,4},{7,5},{8,10},{9,11},{10,... | collective-permute-start | bytes 1572872 | tf_op jit(solution)/shard_map/ppermute | solution.py:639
  58.3 18.0 %collective-permute-start.14 = (bf16[2048,128]{1,0:T(8,128)(2,1)S(1)}, bf16[2048,128]{1,0:T(8,128)(2,1)S(1)}, u32[]{:S(2)}, u32[]{:S(2)}) collective-permute-start(bf16[2048,128]{1,0:T(8,128)(2,1)S(1)} %joined0.3), channel_id=1, source_target_pairs={{0,2},{1,3},{2,6},{3,7},{4,0},{5,1},{6,4},{7,5},{8,10},{9,11},{10,... | collective-permute-start | bytes 1572872 | tf_op jit(solution)/shard_map/ppermute | solution.py:639
  59.3 17.0 %collective-permute-start.20 = (bf16[1024,128]{1,0:T(8,128)(2,1)S(1)}, bf16[1024,128]{1,0:T(8,128)(2,1)S(1)}, u32[]{:S(2)}, u32[]{:S(2)}) collective-permute-start(bf16[1024,128]{1,0:T(8,128)(2,1)S(1)} %get-tuple-element.147), channel_id=1, source_target_pairs={{0,1},{1,0},{2,3},{3,2},{4,5},{5,4},{6,7},{7,6},{8,9},{9,8},{10,11... | collective-permute-start | bytes 786440 | tf_op jit(solution)/shard_map/ppermute | solution.py:603
  59.7 16.6 %collective-permute-start.21 = (bf16[1024,128]{1,0:T(8,128)(2,1)S(1)}, bf16[1024,128]{1,0:T(8,128)(2,1)S(1)}, u32[]{:S(2)}, u32[]{:S(2)}) collective-permute-start(bf16[1024,128]{1,0:T(8,128)(2,1)S(1)} %get-tuple-element.148), channel_id=1, source_target_pairs={{0,1},{1,0},{2,3},{3,2},{4,5},{5,4},{6,7},{7,6},{8,9},{9,8},{10,11... | collective-permute-start | bytes 786440 | tf_op jit(solution)/shard_map/ppermute | solution.py:603
  62.2 5.5 %collective-permute-start.17 = (bf16[336,128]{1,0:T(8,128)(2,1)S(1)}, bf16[336,128]{1,0:T(8,128)(2,1)S(1)}, u32[]{:S(2)}, u32[]{:S(2)}) collective-permute-start(bf16[336,128]{1,0:T(8,128)(2,1)S(1)} %get-tuple-element.142), channel_id=1, source_target_pairs={{0,16},{8,24},{16,0},{24,8},{1,17},{9,25},{17,1},{25,9},{2,18},{10... | collective-permute-start | bytes 258056 | tf_op jit(solution)/shard_map/ppermute | solution.py:603
  65.3 5.4 %collective-permute-start.18 = (bf16[336,128]{1,0:T(8,128)(2,1)S(1)}, bf16[336,128]{1,0:T(8,128)(2,1)S(1)}, u32[]{:S(2)}, u32[]{:S(2)}) collective-permute-start(bf16[336,128]{1,0:T(8,128)(2,1)S(1)} %get-tuple-element.143), channel_id=1, source_target_pairs={{0,24},{8,16},{16,8},{24,0},{1,25},{9,17},{17,9},{25,1},{2,26},{10... | collective-permute-start | bytes 258056 | tf_op jit(solution)/shard_map/ppermute | solution.py:603
  70.7 5.5 %collective-permute-start.19 = (f32[48,256]{1,0:T(8,128)S(1)}, f32[48,256]{1,0:T(8,128)S(1)}, u32[]{:S(2)}, u32[]{:S(2)}) collective-permute-start(f32[48,256]{1,0:T(8,128)S(1)} %piece_sum.1), channel_id=1, source_target_pairs={{0,2},{1,3},{2,0},{3,1},{4,6},{5,7},{6,4},{7,5},{8,10},{9,11},{10,... | collective-permute-start | bytes 147464 | tf_op jit(solution)/shard_map/ppermute | solution.py:603
  76.5 14.4 %collective-permute-start.22 = (bf16[2048,128]{1,0:T(8,128)(2,1)S(1)}, bf16[2048,128]{1,0:T(8,128)(2,1)S(1)}, u32[]{:S(2)}, u32[]{:S(2)}) collective-permute-start(bf16[2048,128]{1,0:T(8,128)(2,1)S(1)} %joined0.4), channel_id=1, source_target_pairs={{0,2},{1,3},{2,6},{3,7},{4,0},{5,1},{6,4},{7,5},{8,10},{9,11},{10,... | collective-permute-start | bytes 1572872 | tf_op jit(solution)/shard_map/ppermute | solution.py:639
  78.7 11.6 %collective-permute-start.23 = (f32[48,256]{1,0:T(8,128)S(1)}, f32[48,256]{1,0:T(8,128)S(1)}, u32[]{:S(2)}, u32[]{:S(2)}) collective-permute-start(f32[48,256]{1,0:T(8,128)S(1)} %add.16), channel_id=1, source_target_pairs={{0,4},{1,5},{2,6},{3,7},{4,0},{5,1},{6,2},{7,3},{8,12},{9,13},{10,... | collective-permute-start | bytes 147464 | tf_op jit(solution)/shard_map/ppermute | solution.py:603
  81.2 9.2 %collective-permute-start.24 = (bf16[1024,128]{1,0:T(8,128)(2,1)S(1)}, bf16[1024,128]{1,0:T(8,128)(2,1)S(1)}, u32[]{:S(2)}, u32[]{:S(2)}) collective-permute-start(bf16[1024,128]{1,0:T(8,128)(2,1)S(1)} %get-tuple-element.153), channel_id=1, source_target_pairs={{0,1},{1,0},{2,3},{3,2},{4,5},{5,4},{6,7},{7,6},{8,9},{9,8},{10,11... | collective-permute-start | bytes 786440 | tf_op jit(solution)/shard_map/ppermute | solution.py:603
  81.3 9.1 %collective-permute-start.25 = (bf16[1024,128]{1,0:T(8,128)(2,1)S(1)}, bf16[1024,128]{1,0:T(8,128)(2,1)S(1)}, u32[]{:S(2)}, u32[]{:S(2)}) collective-permute-start(bf16[1024,128]{1,0:T(8,128)(2,1)S(1)} %get-tuple-element.154), channel_id=1, source_target_pairs={{0,1},{1,0},{2,3},{3,2},{4,5},{5,4},{6,7},{7,6},{8,9},{9,8},{10,11... | collective-permute-start | bytes 786440 | tf_op jit(solution)/shard_map/ppermute | solution.py:603
  81.8 9.1 %collective-permute-start.26 = (bf16[1024,128]{1,0:T(8,128)(2,1)S(1)}, bf16[1024,128]{1,0:T(8,128)(2,1)S(1)}, u32[]{:S(2)}, u32[]{:S(2)}) collective-permute-start(bf16[1024,128]{1,0:T(8,128)(2,1)S(1)} %get-tuple-element.157), channel_id=1, source_target_pairs={{0,1},{1,0},{2,3},{3,2},{4,5},{5,4},{6,7},{7,6},{8,9},{9,8},{10,11... | collective-permute-start | bytes 786440 | tf_op jit(solution)/shard_map/ppermute | solution.py:603
  92.1 14.9 %collective-permute-start.28 = (bf16[2048,128]{1,0:T(8,128)(2,1)S(1)}, bf16[2048,128]{1,0:T(8,128)(2,1)S(1)}, u32[]{:S(2)}, u32[]{:S(2)}) collective-permute-start(bf16[2048,128]{1,0:T(8,128)(2,1)S(1)} %joined0.5), channel_id=1, source_target_pairs={{0,2},{1,3},{2,6},{3,7},{4,0},{5,1},{6,4},{7,5},{8,10},{9,11},{10,... | collective-permute-start | bytes 1572872 | tf_op jit(solution)/shard_map/ppermute | solution.py:639
  93.9 5.0 %collective-permute-start.31 = (f32[48,256]{1,0:T(8,128)S(1)}, f32[48,256]{1,0:T(8,128)S(1)}, u32[]{:S(2)}, u32[]{:S(2)}) collective-permute-start(f32[48,256]{1,0:T(8,128)S(1)} %add.17.refs_0_), channel_id=1, source_target_pairs={{0,24},{8,16},{16,8},{24,0},{1,25},{9,17},{17,9},{25,1},{2,26},{10... | collective-permute-start | bytes 147464 | tf_op jit(solution)/shard_map/ppermute | solution.py:603
  (21 other events, 162.7 us)

commit v4 on v3

--- a/solution.py
+++ b/solution.py
@@ -11,7 +11,7 @@
 BF16 = jnp.bfloat16
 BLK = 128
 ROWS_PER = 4
-CHUNKS = 1
+CHUNKS = 2
 PARTS = 2
 VMEM = 28 * 1024 * 1024
 
@@ -26,6 +26,23 @@
 
 def cost(flops, nbytes, trans=0):
     return pl.CostEstimate(flops=flops, bytes_accessed=nbytes, transcendentals=trans)
+
+
+def fold_of(steps):
+    return [0] + list(range(1, steps, 2)) + list(range(2, steps, 2))[::-1]
+
+
+class Place:
+    def __init__(self, n):
+        me = lax.axis_index("narrow")
+        self.core, self.chip, self.steps = lax.rem(me, 2), lax.div(me, 2), n // 2
+
+    def at(self, s):
+        fold = fold_of(self.steps)
+        found = jnp.int32(0)
+        for z in range(self.steps):
+            found = jnp.where(self.chip == z, fold[(fold.index(z) - s) % self.steps], found)
+        return found
 
 
 def block(ref, index):
@@ -47,19 +64,19 @@
     return reads
 
 
-def pair_sum(ids, cols, pair, slabs_ref, g, n, chip, base=0):
-    core = ids[0]
-    own = block(slabs_ref.at[0], cols[g * n + chip * 2 + core])
-    sib = block(slabs_ref.at[1], cols[g * n + chip * 2 + 1 - core])
+def pair_sum(core, cols, pair, slabs_ref, g, n, chip, base=0):
+    own = block(slabs_ref.at[0], cols[chip * 2 + core, g])
+    sib = block(slabs_ref.at[1], cols[chip * 2 + 1 - core, g])
     mine, other = pair[g, base + core].astype(F32), pair[g, base + 1 - core].astype(F32)
     return mm(mine.astype(BF16), own) + mm(other.astype(BF16), sib), mine + other
 
 
 def lay_out(parts, slabs_ref):
-    tall = parts[0].shape[0]
-    for j, part in enumerate(parts):
-        half, at = divmod(j, len(parts) // 2)
-        slabs_ref[half, pl.ds(at * tall, tall), :] = part[...]
+    at = 0
+    for part in parts:
+        half, row = divmod(at, slabs_ref.shape[1])
+        slabs_ref[half, pl.ds(row, part.shape[0]), :] = part[...]
+        at += part.shape[0]
 
 
 def spec(x):
@@ -89,13 +106,13 @@
     )(tiles)
 
 
-def pull_kernel(ids, cols, *refs, n, step, chunks, wide):
+def pull_kernel(cols, *refs, n, step, chunks, wide):
     refs = list(refs)
     if wide:
         row, valid = refs[:2]
         refs = refs[2:]
-    tiles_ref, parts = refs[0], refs[1 : 1 + 2 * chunks]
-    refs = refs[1 + 2 * chunks :]
+    tiles_ref, parts = refs[0], refs[1 : 1 + chunks]
+    refs = refs[1 + chunks :]
     if step:
         acc_in, counts_in = refs[:2]
         refs = refs[2:]
@@ -104,14 +121,15 @@
         refs = refs[1 + wide :]
         here = lax.axis_index("wide")
     acc_ref, counts_ref, slabs_ref, pair, sems = refs[:5]
-    chip = ids[1 + step]
+    here_now = Place(n)
+    core, chip = here_now.core, here_now.at(step)
     reads = tile_reads(tiles_ref, pair, sems, chip)
     lay_out(parts, slabs_ref)
     for q, r in enumerate(reads):
         r.wait()
         for g in range(q * ROWS_PER, (q + 1) * ROWS_PER):
             rows = pl.ds(g * BLK, BLK)
-            part, count = pair_sum(ids, cols, pair, slabs_ref, g, n, chip)
+            part, count = pair_sum(core, cols, pair, slabs_ref, g, n, chip)
             acc_ref[rows, :] = acc_in[rows, :] + part if step else part
             counts_ref[rows, :] = counts_in[rows, :] + count if step else count
     if wide:
@@ -123,7 +141,7 @@
             counts_ref[at, :] += mask
 
 
-def pull(ids, cols, tiles, own, sib, sums, step, off=()):
+def pull(cols, tiles, own, sib, sums, step, off=()):
     g, n = tiles.shape[:2]
     width = own[0].shape[1]
     rows = g * BLK
@@ -137,9 +155,9 @@
         specs += [spec(x) for x in (off_tiles, *fetched)]
     out = jax.ShapeDtypeStruct((rows, width), F32)
     return pl.pallas_call(
-        partial(pull_kernel, n=n, step=step, chunks=len(own), wide=wide),
+        partial(pull_kernel, n=n, step=step, chunks=len(own) + len(sib), wide=wide),
         grid_spec=pltpu.PrefetchScalarGridSpec(
-            num_scalar_prefetch=2 + len(scalars),
+            num_scalar_prefetch=1 + len(scalars),
             grid=(1,),
             in_specs=specs,
             out_specs=[spec(out)] * 2,
@@ -153,7 +171,7 @@
         compiler_params=params(),
         cost_estimate=cost(4 * rows * BLK * width, 12 * rows * width),
         name=f"pull{step}",
-    )(ids, cols, *scalars, tiles, *ins)
+    )(cols, *scalars, tiles, *ins)
 
 
 def serve_kernel(*refs, wide):
@@ -184,18 +202,19 @@
 def place(cols, tiles_ref, signal_rows, place_ref, g, core, chip, n):
     for j in range(2):
         which = core if j == 0 else 1 - core
-        at = pl.ds(pl.multiple_of(cols[g * n + chip * 2 + which] * BLK, BLK), BLK)
+        at = pl.ds(pl.multiple_of(cols[chip * 2 + which, g] * BLK, BLK), BLK)
         place_ref[j, at, :] += mm(tiles_ref[g, chip * 2 + which], signal_rows, 0, 0)
 
 
 def middle_kernel(
-    ids, cols, tiles_ref, cot_ref, acc_ref, counts_ref, feat_ref, wself_ref, wneigh_ref, bias_ref,
+    cols, tiles_ref, cot_ref, acc_ref, counts_ref, feat_ref, wself_ref, wneigh_ref, bias_ref,
     *refs, n, steps, chunks,
 ):
     parts, refs = refs[: 2 * chunks], refs[2 * chunks :]
     out_hbm, gp_ref, agg_ref, sig_ref, keep_ref, send_ref = refs[:6]
     place_ref, slabs_ref, out, out_sems = refs[6:]
-    core, last, first = ids[0], ids[steps], ids[2]
+    place_now = Place(n)
+    core, last, first = place_now.core, place_now.at(steps - 1), place_now.at(1)
     tall = ROWS_PER * BLK
     count = feat_ref.shape[0] // tall
 
@@ -213,7 +232,7 @@
     for q in range(count):
         rows = rows_of(q)
         both = [
-            pair_sum(ids, cols, tiles_ref, slabs_ref, g, n, last, last * 2)
+            pair_sum(core, cols, tiles_ref, slabs_ref, g, n, last, last * 2)
             for g in range(q * ROWS_PER, (q + 1) * ROWS_PER)
         ]
         gathered = acc_ref[rows, :] + jnp.concatenate([b[0] for b in both], axis=0)
@@ -244,7 +263,7 @@
         w.wait()
 
 
-def middle(ids, cols, tiles, cot, sums, features, w_self, w_neigh, bias, own, sib, steps):
+def middle(cols, tiles, cot, sums, features, w_self, w_neigh, bias, own, sib, steps):
     g, n = tiles.shape[:2]
     rows, width = features.shape
     outw = w_self.shape[1]
@@ -258,7 +277,7 @@
     return pl.pallas_call(
         partial(middle_kernel, n=n, steps=steps, chunks=len(own)),
         grid_spec=pltpu.PrefetchScalarGridSpec(
-            num_scalar_prefetch=2,
+            num_scalar_prefetch=1,
             grid=(1,),
             in_specs=[spec(x) for x in (tiles, cot, *ins)],
             out_specs=[in_hbm()] + [spec(x) for x in outs[1:]],
@@ -275,24 +294,25 @@
             8 * rows * BLK * width + 6 * rows * width * outw, 30 * rows * width, rows * outw
         ),
         name="middle",
-    )(ids, cols, tiles, cot, *ins)
-
-
-def push_kernel(ids, cols, tiles_ref, sig_ref, keep_ref, *refs, n, which):
+    )(cols, tiles, cot, *ins)
+
+
+def push_kernel(cols, tiles_ref, sig_ref, keep_ref, *refs, n, which):
     *send_refs, place_ref = refs
+    now = Place(n)
     parts = len(send_refs) // len(which)
     tall = send_refs[0].shape[0]
     for p, s in enumerate(which):
         place_ref[...] = jnp.zeros_like(place_ref)
         for g in range(tiles_ref.shape[0]):
             rows = sig_ref[g * BLK : (g + 1) * BLK, :]
-            place(cols, tiles_ref, rows, place_ref, g, ids[0], ids[1 + s], n)
+            place(cols, tiles_ref, rows, place_ref, g, now.core, now.at(s), n)
         keep_ref[p] = place_ref[0].astype(BF16)
         for j in range(parts):
             send_refs[p * parts + j][...] = place_ref[1, pl.ds(j * tall, tall), :].astype(BF16)
 
 
-def push(ids, cols, signal, tiles, which):
+def push(cols, signal, tiles, which):
     g, n = tiles.shape[:2]
     rows, width = signal.shape
     count = len(which)
@@ -301,7 +321,7 @@
     keeps, *sends = pl.pallas_call(
         partial(push_kernel, n=n, which=which),
         grid_spec=pltpu.PrefetchScalarGridSpec(
-            num_scalar_prefetch=2,
+            num_scalar_prefetch=1,
             grid=(1,),
             in_specs=[spec(tiles), spec(signal)],
             out_specs=[spec(x) for x in outs],
@@ -311,7 +331,7 @@
         compiler_params=params(),
         cost_estimate=cost(4 * count * rows * BLK * width, 8 * count * rows * width),
         name="push",
-    )(ids, cols, tiles, signal)
+    )(cols, tiles, signal)
     return keeps, sends
 
 
@@ -321,7 +341,7 @@
 
 
 def grads_kernel(
-    ids, asked, row, valid, off_ref, sig_ref, feat_ref, agg_ref, gp_ref,
+    asked, row, valid, off_ref, sig_ref, feat_ref, agg_ref, gp_ref,
     mine_ref, other_ref, *pushed_refs, wide,
 ):
     here = lax.axis_index("wide")
@@ -334,7 +354,7 @@
         b = mm(agg_ref[rows, :], gp, 0, 0)
         c = jnp.sum(gp.astype(F32), axis=0, keepdims=True)
         dself, dneigh, dbias = (a, b, c) if i == 0 else (dself + a, dneigh + b, dbias + c)
-    first = ids[0] == 0
+    first = lax.rem(lax.axis_index("narrow"), 2) == 0
     mine_ref[pl.ds(0, BLK), :] = jnp.where(first, dself, dneigh)
     other_ref[pl.ds(0, BLK), :] = jnp.where(first, dneigh, dself)
     spare = mine_ref.shape[0] - BLK
@@ -349,7 +369,7 @@
         ref[pl.ds(BLK, 16), :] = jnp.full((16, BLK), asked[peer], jnp.int32).astype(F32).astype(BF16)
 
 
-def grads(ids, asked, row, valid, off_tiles, signal, features, aggregate, grad_pre):
+def grads(asked, row, valid, off_tiles, signal, features, aggregate, grad_pre):
     wide = off_tiles.shape[1]
     rows, width = features.shape
     outw = grad_pre.shape[1]
@@ -363,7 +383,7 @@
     return pl.pallas_call(
         partial(grads_kernel, wide=wide),
         grid_spec=pltpu.PrefetchScalarGridSpec(
-            num_scalar_prefetch=4,
+            num_scalar_prefetch=3,
             grid=(1,),
             in_specs=[whole(x) for x in ins],
             out_specs=[whole(x) for x in outs],
@@ -372,7 +392,7 @@
         compiler_params=params(),
         cost_estimate=cost(8 * rows * width * width, 16 * rows * width),
         name="grads",
-    )(ids, asked, row, valid, *ins)
+    )(asked, row, valid, *ins)
 
 
 def pack_kernel(mine_ref, come_ref, *refs, wide):
@@ -469,8 +489,8 @@
     )(*pieces)
 
 
-def finish_kernel(ids, total_ref, paired_ref, self_ref, neigh_ref, bias_ref):
-    first = ids[0] == 0
+def finish_kernel(total_ref, paired_ref, self_ref, neigh_ref, bias_ref):
+    first = lax.rem(lax.axis_index("narrow"), 2) == 0
     total, paired = total_ref[pl.ds(0, BLK), :], paired_ref[pl.ds(0, BLK), :]
     self_ref[...] = jnp.where(first, total, paired)
     neigh_ref[...] = jnp.where(first, paired, total)
@@ -478,24 +498,21 @@
     bias_ref[...] = jnp.where(first, total_ref[at, :], paired_ref[at, :])[:1]
 
 
-def finish(ids, total, paired):
+def finish(total, paired):
     def whole(x):
         return pl.BlockSpec(x.shape, lambda i, *s: (0, 0))
 
     outs = [jax.ShapeDtypeStruct((r, 2 * BLK), F32) for r in (BLK, BLK, 1)]
     return pl.pallas_call(
         finish_kernel,
-        grid_spec=pltpu.PrefetchScalarGridSpec(
-            num_scalar_prefetch=1,
-            grid=(1,),
-            in_specs=[whole(total), whole(paired)],
-            out_specs=[whole(x) for x in outs],
-        ),
+        grid=(1,),
+        in_specs=[whole(total), whole(paired)],
+        out_specs=[whole(x) for x in outs],
         out_shape=outs,
         compiler_params=params(),
         cost_estimate=cost(4 * total.size, 16 * total.size),
         name="finish",
-    )(ids, total, paired)
+    )(total, paired)
 
 
 def base_kernel(gp_ref, wself_ref, keep_ref, *refs, parts):
@@ -632,7 +649,7 @@
     n = lax.axis_size("narrow")
     wide = lax.axis_size("wide")
     steps = n // 2
-    fold = [0] + list(range(1, steps, 2)) + list(range(2, steps, 2))[::-1]
+    fold = fold_of(steps)
     after = {a: b for a, b in zip(fold, fold[1:] + fold[:1])}
 
     def onward(x):
@@ -641,13 +658,7 @@
     def swap(x):
         return to_peer(x, "narrow", 1)
 
-    me = lax.axis_index("narrow")
-    here = lax.axis_index("wide")
-    chips = jnp.array(
-        [[fold[(fold.index(z) - s) % steps] for s in range(steps)] for z in range(steps)], jnp.int32
-    )[me // 2]
-    ids = jnp.concatenate([(me % 2)[None].astype(jnp.int32), chips])
-    cols = band_cols.reshape(-1)
+    cols = band_cols.T
     asked, row, valid = req_block[0], req_row[0], req_valid[0]
     def tie(*xs):
         return lax.optimization_barrier(xs)
@@ -662,10 +673,11 @@
     sums = ()
     for s in range(1, steps):
         following = [onward(x) for x in slabs[-1]]
-        pairs.append([swap(x) for x in slabs[-1]])
+        pairs.append([swap(features)] if s == 1 else [swap(x) for x in slabs[-1]])
         off = (row, valid, off_tiles, fetched) if s == steps - 1 else ()
-        sums = pull(ids, cols, tiles, slabs[-1], pairs[-1], sums, s - 1, off)
-        following[-1], *sums = tie(following[-1], *sums)
+        sums = pull(cols, tiles, slabs[-1], pairs[-1], sums, s - 1, off)
+        at = 0 if s == 1 else -1
+        following[at], *sums = tie(following[at], *sums)
         if s == 1:
             following[-1], *asked_of_me = tie(following[-1], *asked_of_me)
             served = serve(asked_of_me, features)
@@ -676,16 +688,18 @@
         if s == steps - 2:
             halved = halve(tiles)
             halved, *sums = tie(halved, *sums)
-    pairs.append([swap(x) for x in slabs[-1]])
+    early = [swap(x) for x in slabs[-1][:-1]]
+    slabs[-1][-1], *early = tie(slabs[-1][-1], *early)
+    pairs.append([*early, swap(slabs[-1][-1])])
     layer_out, grad_pre, aggregate, signal, keep, send = middle(
-        ids, cols, halved, cotangent, sums, features, weight_self, weight_neigh,
+        cols, halved, cotangent, sums, features, weight_self, weight_neigh,
         bias_term.reshape(1, -1), slabs[-1], pairs[-1], steps,
     )
 
     come = swap(send)
-    keep2, send2 = push(ids, cols, signal, halved, (2 % steps,))
+    keep2, send2 = push(cols, signal, halved, (2 % steps,))
     mine, other, *pushed = grads(
-        ids, asked, row, valid, off_tiles, signal, features, aggregate, grad_pre
+        asked, row, valid, off_tiles, signal, features, aggregate, grad_pre
     )
     come, mine, other, keep2, *more = tie(come, mine, other, keep2, *send2, *pushed)
     send2, pushed = more[: len(send2)], more[len(send2) :]
@@ -706,7 +720,7 @@
         if s == 0:
             got, signal = tie(got, signal)
             going = joined(got, keep2, come2, 0)
-            keeps, sends = push(ids, cols, signal, halved, later)
+            keeps, sends = push(cols, signal, halved, later)
             comes = [swap(x) for x in sends]
             rest = base(grad_pre, weight_self, keeps, comes[-PARTS:], arrived)
         else:
@@ -719,7 +733,7 @@
         k *= 2
     pieces = [total] + [to_peer(total, "wide", k) for k in range(1, wide)]
     whole = half(pieces, (wide * n * row_count) ** (-0.5))
-    grad_self, grad_neigh, grad_bias = finish(ids, whole, swap(whole))
+    grad_self, grad_neigh, grad_bias = finish(whole, swap(whole))
     got, grad_self, grad_neigh, grad_bias = tie(got, grad_self, grad_neigh, grad_bias)
     grad_features = last(rest, [got])
     return layer_out, grad_features, grad_self, grad_neigh, grad_bias.reshape(-1)

time: 108 us -> 104 us (0.963)
  waiting for transfers between devices: 49.8 us -> 42.9 us
  starting transfers between devices: 31.8 us -> 35.5 us
    ppermute x6 -> x9, waiting for transfers between devices: 25.6 us -> 9.87 us  [onward(): lax.ppermute(x, 'narrow', [(i, after[i // 2] * 2 + i % 2) for i in range(...]
    ppermute x27 -> x30, waiting for transfers between devices: 24.2 us -> 33 us  [to_peer(): lax.ppermute(x, axis, [(i, i ^ k if power(size) else (i + k) % size) for...]
    ppermute x6 -> x9, starting transfers between devices: 9.47 us -> 17.8 us  [onward(): lax.ppermute(x, 'narrow', [(i, after[i // 2] * 2 + i % 2) for i in range(...]
    ppermute x27 -> x30, starting transfers between devices: 22.4 us -> 17.7 us  [to_peer(): lax.ppermute(x, axis, [(i, i ^ k if power(size) else (i + k) % size) for...]
    unnamed x25 -> x24, local copies, waits for them, and re-layouts: 5.24 us -> 4.12 us
  transfers between devices with their start and end apart: 33 -> 39, of which waited for: 16 -> 18; matrix products, arithmetic and copies ran while one was open for 2% -> 1% of each run, Pallas kernels for 11% -> 12%
where the time goes in v4:
time: 104 us
  waiting for transfers between devices  42.9 us (41%)
  starting transfers between devices  35.5 us (34%)
  Pallas kernels  19.1 us (18%)
  local copies, waits for them, and re-layouts  5.19 us (5%)
    ppermute x30, waiting for transfers between devices, to_peer(): lax.ppermute(x, axis, [(i, i ^ k if power(size) else (i + k) % size) for...  33 us
    ppermute x9, starting transfers between devices, onward(): lax.ppermute(x, 'narrow', [(i, after[i // 2] * 2 + i % 2) for i in range(...  17.8 us
    ppermute x30, starting transfers between devices, to_peer(): lax.ppermute(x, axis, [(i, i ^ k if power(size) else (i + k) % size) for...  17.7 us
    ppermute x9, waiting for transfers between devices, onward(): lax.ppermute(x, 'narrow', [(i, after[i // 2] * 2 + i % 2) for i in range(...  9.87 us
    pallas_call x3, Pallas kernels, pull(): pl.pallas_call(partial(pull_kernel, n=n, step=step, chunks=len(own) + len...  5.4 us
    pallas_call x1, Pallas kernels, middle(): pl.pallas_call(partial(middle_kernel, n=n, steps=steps, chunks=len(own)),...  5.35 us
    unnamed x24, local copies, waits for them, and re-layouts  4.12 us
    pallas_call x2, Pallas kernels, push(): pl.pallas_call(partial(push_kernel, n=n, which=which), grid_spec=pltpu.Pr...  3.2 us
  transfers between devices with their start and end apart: 39, of which 18 were waited for; matrix products, arithmetic and copies ran while one was open for 1% of the time, Pallas kernels for 12%

profile of v4, /device:TPU:0, one launch (start us, length us, event | category | flops | bytes accessed | tf_op | source)
XLA Modules:
  0.0 103.7 jit_solution(14760749224904075173)
XLA Ops:
  2.2 2.6 %collective-permute-start.5 = (bf16[1024,128]{1,0:T(8,128)(2,1)S(1)}, bf16[1024,128]{1,0:T(8,128)(2,1)S(1)}, u32[]{:S(2)}, u32[]{:S(2)}) collective-permute-start(bf16[1024,128]{1,0:T(8,128)(2,1)S(1)} %get-tuple-element.171.refs_1_), channel_id=1, source_target_pairs={{0,2},{1,3},{2,6},{3,7},{4,0},{5,1},{6,4},{7,5},{8,10},{9,11},{10,... | collective-permute-start | bytes 786440 | tf_op jit(solution)/shard_map/ppermute | solution.py:656
  4.9 2.6 %collective-permute-start = (bf16[1024,128]{1,0:T(8,128)(2,1)S(1)}, bf16[1024,128]{1,0:T(8,128)(2,1)S(1)}, u32[]{:S(2)}, u32[]{:S(2)}) collective-permute-start(bf16[1024,128]{1,0:T(8,128)(2,1)S(1)} %get-tuple-element.172.refs_2_), channel_id=1, source_target_pairs={{0,2},{1,3},{2,6},{3,7},{4,0},{5,1},{6,4},{7,5},{8,10},{9,11},{10,... | collective-permute-start | bytes 786440 | tf_op jit(solution)/shard_map/ppermute | solution.py:656
  7.5 3.4 %copy-done = s32[16,8,128,128]{3,2,1,0:T(8,128)S(1)} copy-done((s32[16,8,128,128]{3,2,1,0:T(8,128)S(1)}, s32[16,8,128,128]{3,2,1,0:T(8,128)}, u32[]{:S(2)}) %copy-start) | copy-done | bytes 8388632
  11.5 1.8 %pull0.1 = (f32[2048,128]{1,0:T(8,128)S(1)}, f32[2048,128]{1,0:T(8,128)S(1)}) custom-call(s32[8,16]{1,0:T(8,128)S(1)} %bitcast.7, s32[16,8,128,128]{3,2,1,0:T(8,128)S(1)} %copy-done, bf16[1024,128]{1,0:T(8,128)(2,1)S(1)} %get-tuple-element.171.refs_1_, bf16[1024,128]{1,0:T(8,128)(2,1)S(1)} %get-tuple-element.172.refs_2_, ...), custom_call_target="tpu_custom_call" | custom-call | flops 134217728 | bytes 3145728 | tf_op jit(solution)/shard_map/pull0/pallas_call | solution.py:157
  14.1 2.4 %collective-permute-start.3 = (s32[4]{0:T(128)S(1)}, s32[4]{0:T(128)S(1)}, u32[]{:S(2)}, u32[]{:S(2)}) collective-permute-start(s32[4]{0:T(128)S(1)} %bitcast.17), channel_id=1, source_target_pairs={{0,24},{8,16},{16,8},{24,0},{1,25},{9,17},{17,9},{25,1},{2,26},{10... | collective-permute-start | bytes 56 | tf_op jit(solution)/shard_map/ppermute | solution.py:620
  18.5 1.5 %collective-permute-done.2.refs_2_ = s32[4]{0:T(128)S(1)} collective-permute-done((s32[4]{0:T(128)S(1)}, s32[4]{0:T(128)S(1)}, u32[]{:S(2)}, u32[]{:S(2)}) %collective-permute-start.2) | collective-permute-done | bytes 48 | tf_op jit(solution)/shard_map/ppermute | solution.py:620
  21.1 3.4 %collective-permute-start.4 = (bf16[1024,128]{1,0:T(8,128)(2,1)S(1)}, bf16[1024,128]{1,0:T(8,128)(2,1)S(1)}, u32[]{:S(2)}, u32[]{:S(2)}) collective-permute-start(bf16[1024,128]{1,0:T(8,128)(2,1)S(1)} %collective-permute-done.refs_2_), channel_id=1, source_target_pairs={{0,2},{1,3},{2,6},{3,7},{4,0},{5,1},{6,4},{7,5},{8,10},{9,11},{10,... | collective-permute-start | bytes 786440 | tf_op jit(solution)/shard_map/ppermute | solution.py:656
  25.5 2.0 %collective-permute-start.9 = (bf16[128,128]{1,0:T(8,128)(2,1)S(1)}, bf16[128,128]{1,0:T(8,128)(2,1)S(1)}, u32[]{:S(2)}, u32[]{:S(2)}) collective-permute-start(bf16[128,128]{1,0:T(8,128)(2,1)S(1)} %get-tuple-element.105), channel_id=1, source_target_pairs={{0,8},{8,0},{16,24},{24,16},{1,9},{9,1},{17,25},{25,17},{2,10},{10... | collective-permute-start | bytes 98312 | tf_op jit(solution)/shard_map/ppermute | solution.py:620
  29.1 1.8 %pull1.1 = (f32[2048,128]{1,0:T(8,128)S(1)}, f32[2048,128]{1,0:T(8,128)S(1)}) custom-call(s32[8,16]{1,0:T(8,128)S(1)} %bitcast.8, s32[16,8,128,128]{3,2,1,0:T(8,128)S(1)} %copy-done.1, bf16[1024,128]{1,0:T(8,128)(2,1)S(1)} %collective-permute-done.5.refs_1_, bf16[1024,128]{1,0:T(8,128)(2,1)S(1)} %collective-permute-done.refs_2_, ...), custom_call_target="tpu_custom_call" | custom-call | flops 134217728 | bytes 3145728 | tf_op jit(solution)/shard_map/pull1/pallas_call | solution.py:157
  31.7 2.1 %collective-permute-done.11.refs_13_ = bf16[128,128]{1,0:T(8,128)(2,1)S(1)} collective-permute-done((bf16[128,128]{1,0:T(8,128)(2,1)S(1)}, bf16[128,128]{1,0:T(8,128)(2,1)S(1)}, u32[]{:S(2)}, u32[]{:S(2)}) %collective-permute-start.11) | collective-permute-done | bytes 32800 | tf_op jit(solution)/shard_map/ppermute | solution.py:620
  34.3 3.4 %collective-permute-start.12 = (bf16[1024,128]{1,0:T(8,128)(2,1)S(1)}, bf16[1024,128]{1,0:T(8,128)(2,1)S(1)}, u32[]{:S(2)}, u32[]{:S(2)}) collective-permute-start(bf16[1024,128]{1,0:T(8,128)(2,1)S(1)} %collective-permute-done.4.refs_4_), channel_id=1, source_target_pairs={{0,2},{1,3},{2,6},{3,7},{4,0},{5,1},{6,4},{7,5},{8,10},{9,11},{10,... | collective-permute-start | bytes 786440 | tf_op jit(solution)/shard_map/ppermute | solution.py:656
  38.4 1.8 %pull2.1 = (f32[2048,128]{1,0:T(8,128)S(1)}, f32[2048,128]{1,0:T(8,128)S(1)}) custom-call(s32[8,16]{1,0:T(8,128)S(1)} %bitcast.9, s32[4]{0:T(128)S(1)} %bitcast.13, s32[4]{0:T(128)S(1)} %bitcast.15, s32[16,8,128,128]{3,2,1,0:T(8,128)S(1)} %copy-done.1, bf16[1024,128]{1,0:T(8,128)(2,1)S(1)} %collective-permute-done.13.refs_3_, ...), custom_call_target="tpu_custom_call" | custom-call | flops 134217728 | bytes 3145728 | tf_op jit(solution)/shard_map/pull2/pallas_call | solution.py:157
  40.3 3.2 %collective-permute-done.12.refs_1_ = bf16[1024,128]{1,0:T(8,128)(2,1)S(1)} collective-permute-done((bf16[1024,128]{1,0:T(8,128)(2,1)S(1)}, bf16[1024,128]{1,0:T(8,128)(2,1)S(1)}, u32[]{:S(2)}, u32[]{:S(2)}) %collective-permute-start.12) | collective-permute-done | bytes 262176 | tf_op jit(solution)/shard_map/ppermute | solution.py:656
  45.0 5.4 %middle.1 = (bf16[2048,256]{1,0:T(8,128)(2,1)}, bf16[2048,256]{1,0:T(8,128)(2,1)S(1)}, bf16[2048,128]{1,0:T(8,128)(2,1)S(1)}, bf16[2048,128]{1,0:T(8,128)(2,1)S(...) custom-call(s32[8,16]{1,0:T(8,128)S(1)} %bitcast.10, bf16[16,8,128,128]{3,2,1,0:T(8,128)(2,1)S(1)} %halve.1.tiles_ref, ...), custom_call_target="tpu_custom_call" | custom-call | flops 671088640 | bytes 7864320 | tf_op jit(solution)/shard_map/middle/pallas_call | solution.py:277
  53.1 2.5 %collective-permute-start.20 = (bf16[2048,128]{1,0:T(8,128)(2,1)S(1)}, bf16[2048,128]{1,0:T(8,128)(2,1)S(1)}, u32[]{:S(2)}, u32[]{:S(2)}) collective-permute-start(bf16[2048,128]{1,0:T(8,128)(2,1)S(1)} %joined0.3), channel_id=1, source_target_pairs={{0,2},{1,3},{2,6},{3,7},{4,0},{5,1},{6,4},{7,5},{8,10},{9,11},{10,... | collective-permute-start | bytes 1572872 | tf_op jit(solution)/shard_map/ppermute | solution.py:656
  57.9 3.9 %collective-permute-done.22.refs_1_.refs_3_ = bf16[336,128]{1,0:T(8,128)(2,1)S(1)} collective-permute-done((bf16[336,128]{1,0:T(8,128)(2,1)S(1)}, bf16[336,128]{1,0:T(8,128)(2,1)S(1)}, u32[]{:S(2)}, u32[]{:S(2)}) %collective-permute-start.22) | collective-permute-done | bytes 86048 | tf_op jit(solution)/shard_map/ppermute | solution.py:620
  62.0 5.1 %collective-permute-done.24.refs_3_.refs_5_ = bf16[336,128]{1,0:T(8,128)(2,1)S(1)} collective-permute-done((bf16[336,128]{1,0:T(8,128)(2,1)S(1)}, bf16[336,128]{1,0:T(8,128)(2,1)S(1)}, u32[]{:S(2)}, u32[]{:S(2)}) %collective-permute-start.24) | collective-permute-done | bytes 86048 | tf_op jit(solution)/shard_map/ppermute | solution.py:620
  68.5 2.9 %collective-permute-done.25 = f32[48,256]{1,0:T(8,128)S(1)} collective-permute-done((f32[48,256]{1,0:T(8,128)S(1)}, f32[48,256]{1,0:T(8,128)S(1)}, u32[]{:S(2)}, u32[]{:S(2)}) %collective-permute-start.25) | collective-permute-done | bytes 49184 | tf_op jit(solution)/shard_map/ppermute | solution.py:620
  73.0 1.7 %collective-permute-start.29 = (f32[48,256]{1,0:T(8,128)S(1)}, f32[48,256]{1,0:T(8,128)S(1)}, u32[]{:S(2)}, u32[]{:S(2)}) collective-permute-start(f32[48,256]{1,0:T(8,128)S(1)} %add.6), channel_id=1, source_target_pairs={{0,4},{1,5},{2,6},{3,7},{4,0},{5,1},{6,2},{7,3},{8,12},{9,13},{10,... | collective-permute-start | bytes 147464 | tf_op jit(solution)/shard_map/ppermute | solution.py:620
  74.8 1.9 %push.3 = (bf16[2,2048,128]{2,1,0:T(8,128)(2,1)S(1)}, bf16[1024,128]{1,0:T(8,128)(2,1)S(1)}, bf16[1024,128]{1,0:T(8,128)(2,1)S(1)}, bf16[1024,128]{1,0:T(8,128)(2,1)S(1)}, bf16[1024,128]{1,0:T(8,128)(2,1)S(1)}) custom-call(s32[8,16]{1,0:T(8,128)S(1)} %bitcast.12, bf16[16,8,128,128]{3,2,1,0:T(8,128)(2,1)S(1)} %halve.1.tiles_ref, ...), custom_call_target="tpu_custom_call" | custom-call | flops 268435456 | bytes 4194304 | tf_op jit(solution)/shard_map/push/pallas_call | solution.py:321
  77.3 8.7 %collective-permute-done.29 = f32[48,256]{1,0:T(8,128)S(1)} collective-permute-done((f32[48,256]{1,0:T(8,128)S(1)}, f32[48,256]{1,0:T(8,128)S(1)}, u32[]{:S(2)}, u32[]{:S(2)}) %collective-permute-start.29) | collective-permute-done | bytes 49184 | tf_op jit(solution)/shard_map/ppermute | solution.py:620
  89.7 2.1 %collective-permute-start.35 = (f32[48,256]{1,0:T(8,128)S(1)}, f32[48,256]{1,0:T(8,128)S(1)}, u32[]{:S(2)}, u32[]{:S(2)}) collective-permute-start(f32[48,256]{1,0:T(8,128)S(1)} %add.7.refs_0_), channel_id=1, source_target_pairs={{0,8},{8,0},{16,24},{24,16},{1,9},{9,1},{17,25},{25,17},{2,10},{10... | collective-permute-start | bytes 147464 | tf_op jit(solution)/shard_map/ppermute | solution.py:620
  91.8 1.6 %collective-permute-done.37.refs_3_ = f32[48,256]{1,0:T(8,128)S(1)} collective-permute-done((f32[48,256]{1,0:T(8,128)S(1)}, f32[48,256]{1,0:T(8,128)S(1)}, u32[]{:S(2)}, u32[]{:S(2)}) %collective-permute-start.37) | collective-permute-done | bytes 49184 | tf_op jit(solution)/shard_map/ppermute | solution.py:620
  96.2 6.5 %collective-permute-done.34.refs_0_ = bf16[2048,128]{1,0:T(8,128)(2,1)S(1)} collective-permute-done((bf16[2048,128]{1,0:T(8,128)(2,1)S(1)}, bf16[2048,128]{1,0:T(8,128)(2,1)S(1)}, u32[]{:S(2)}, u32[]{:S(2)}) %collective-permute-start.34) | collective-permute-done | bytes 524320 | tf_op jit(solution)/shard_map/ppermute | solution.py:656
  (100 shorter events, 28.4 us)
Async XLA Ops:
  0.7 6.8 %collective-permute-start.6 = (bf16[2048,128]{1,0:T(8,128)(2,1)}, bf16[2048,128]{1,0:T(8,128)(2,1)S(1)}, u32[]{:S(2)}, u32[]{:S(2)}) collective-permute-start(bf16[2048,128]{1,0:T(8,128)(2,1)} %feat_ref.3), channel_id=1, source_target_pairs={{0,1},{1,0},{2,3},{3,2},{4,5},{5,4},{6,7},{7,6},{8,9},{9,8},{10,11... | collective-permute-start | bytes 1572872 | tf_op jit(solution)/shard_map/ppermute | solution.py:620
  2.2 11.1 %collective-permute-start.5 = (bf16[1024,128]{1,0:T(8,128)(2,1)S(1)}, bf16[1024,128]{1,0:T(8,128)(2,1)S(1)}, u32[]{:S(2)}, u32[]{:S(2)}) collective-permute-start(bf16[1024,128]{1,0:T(8,128)(2,1)S(1)} %get-tuple-element.171.refs_1_), channel_id=1, source_target_pairs={{0,2},{1,3},{2,6},{3,7},{4,0},{5,1},{6,4},{7,5},{8,10},{9,11},{10,... | collective-permute-start | bytes 786440 | tf_op jit(solution)/shard_map/ppermute | solution.py:656
  4.9 15.7 %collective-permute-start = (bf16[1024,128]{1,0:T(8,128)(2,1)S(1)}, bf16[1024,128]{1,0:T(8,128)(2,1)S(1)}, u32[]{:S(2)}, u32[]{:S(2)}) collective-permute-start(bf16[1024,128]{1,0:T(8,128)(2,1)S(1)} %get-tuple-element.172.refs_2_), channel_id=1, source_target_pairs={{0,2},{1,3},{2,6},{3,7},{4,0},{5,1},{6,4},{7,5},{8,10},{9,11},{10,... | collective-permute-start | bytes 786440 | tf_op jit(solution)/shard_map/ppermute | solution.py:656
  13.3 11.2 %collective-permute-start.13 = (bf16[1024,128]{1,0:T(8,128)(2,1)S(1)}, bf16[1024,128]{1,0:T(8,128)(2,1)S(1)}, u32[]{:S(2)}, u32[]{:S(2)}) collective-permute-start(bf16[1024,128]{1,0:T(8,128)(2,1)S(1)} %collective-permute-done.5.refs_1_), channel_id=1, source_target_pairs={{0,2},{1,3},{2,6},{3,7},{4,0},{5,1},{6,4},{7,5},{8,10},{9,11},{10,... | collective-permute-start | bytes 786440 | tf_op jit(solution)/shard_map/ppermute | solution.py:656
  20.6 6.9 %collective-permute-start.8 = (bf16[1024,128]{1,0:T(8,128)(2,1)S(1)}, bf16[1024,128]{1,0:T(8,128)(2,1)S(1)}, u32[]{:S(2)}, u32[]{:S(2)}) collective-permute-start(bf16[1024,128]{1,0:T(8,128)(2,1)S(1)} %collective-permute-done.refs_2_), channel_id=1, source_target_pairs={{0,1},{1,0},{2,3},{3,2},{4,5},{5,4},{6,7},{7,6},{8,9},{9,8},{10,11... | collective-permute-start | bytes 786440 | tf_op jit(solution)/shard_map/ppermute | solution.py:620
  20.6 8.4 %collective-permute-start.7 = (bf16[1024,128]{1,0:T(8,128)(2,1)S(1)}, bf16[1024,128]{1,0:T(8,128)(2,1)S(1)}, u32[]{:S(2)}, u32[]{:S(2)}) collective-permute-start(bf16[1024,128]{1,0:T(8,128)(2,1)S(1)} %collective-permute-done.5.refs_1_), channel_id=1, source_target_pairs={{0,1},{1,0},{2,3},{3,2},{4,5},{5,4},{6,7},{7,6},{8,9},{9,8},{10,11... | collective-permute-start | bytes 786440 | tf_op jit(solution)/shard_map/ppermute | solution.py:620
  21.1 10.1 %collective-permute-start.4 = (bf16[1024,128]{1,0:T(8,128)(2,1)S(1)}, bf16[1024,128]{1,0:T(8,128)(2,1)S(1)}, u32[]{:S(2)}, u32[]{:S(2)}) collective-permute-start(bf16[1024,128]{1,0:T(8,128)(2,1)S(1)} %collective-permute-done.refs_2_), channel_id=1, source_target_pairs={{0,2},{1,3},{2,6},{3,7},{4,0},{5,1},{6,4},{7,5},{8,10},{9,11},{10,... | collective-permute-start | bytes 786440 | tf_op jit(solution)/shard_map/ppermute | solution.py:656
  24.5 13.2 %collective-permute-start.16 = (bf16[1024,128]{1,0:T(8,128)(2,1)S(1)}, bf16[1024,128]{1,0:T(8,128)(2,1)S(1)}, u32[]{:S(2)}, u32[]{:S(2)}) collective-permute-start(bf16[1024,128]{1,0:T(8,128)(2,1)S(1)} %collective-permute-done.13.refs_3_), channel_id=1, source_target_pairs={{0,2},{1,3},{2,6},{3,7},{4,0},{5,1},{6,4},{7,5},{8,10},{9,11},{10,... | collective-permute-start | bytes 786440 | tf_op jit(solution)/shard_map/ppermute | solution.py:656
  25.5 5.7 %collective-permute-start.9 = (bf16[128,128]{1,0:T(8,128)(2,1)S(1)}, bf16[128,128]{1,0:T(8,128)(2,1)S(1)}, u32[]{:S(2)}, u32[]{:S(2)}) collective-permute-start(bf16[128,128]{1,0:T(8,128)(2,1)S(1)} %get-tuple-element.105), channel_id=1, source_target_pairs={{0,8},{8,0},{16,24},{24,16},{1,9},{9,1},{17,25},{25,17},{2,10},{10... | collective-permute-start | bytes 98312 | tf_op jit(solution)/shard_map/ppermute | solution.py:620
  29.0 4.8 %collective-permute-start.11 = (bf16[128,128]{1,0:T(8,128)(2,1)S(1)}, bf16[128,128]{1,0:T(8,128)(2,1)S(1)}, u32[]{:S(2)}, u32[]{:S(2)}) collective-permute-start(bf16[128,128]{1,0:T(8,128)(2,1)S(1)} %get-tuple-element.107), channel_id=1, source_target_pairs={{0,24},{8,16},{16,8},{24,0},{1,25},{9,17},{17,9},{25,1},{2,26},{10... | collective-permute-start | bytes 98312 | tf_op jit(solution)/shard_map/ppermute | solution.py:620
  34.3 9.1 %collective-permute-start.12 = (bf16[1024,128]{1,0:T(8,128)(2,1)S(1)}, bf16[1024,128]{1,0:T(8,128)(2,1)S(1)}, u32[]{:S(2)}, u32[]{:S(2)}) collective-permute-start(bf16[1024,128]{1,0:T(8,128)(2,1)S(1)} %collective-permute-done.4.refs_4_), channel_id=1, source_target_pairs={{0,2},{1,3},{2,6},{3,7},{4,0},{5,1},{6,4},{7,5},{8,10},{9,11},{10,... | collective-permute-start | bytes 786440 | tf_op jit(solution)/shard_map/ppermute | solution.py:656
  37.7 5.7 %collective-permute-start.17 = (bf16[1024,128]{1,0:T(8,128)(2,1)S(1)}, bf16[1024,128]{1,0:T(8,128)(2,1)S(1)}, u32[]{:S(2)}, u32[]{:S(2)}) collective-permute-start(bf16[1024,128]{1,0:T(8,128)(2,1)S(1)} %collective-permute-done.16.refs_0_), channel_id=1, source_target_pairs={{0,1},{1,0},{2,3},{3,2},{4,5},{5,4},{6,7},{7,6},{8,9},{9,8},{10,11... | collective-permute-start | bytes 786440 | tf_op jit(solution)/shard_map/ppermute | solution.py:620
  53.1 18.3 %collective-permute-start.20 = (bf16[2048,128]{1,0:T(8,128)(2,1)S(1)}, bf16[2048,128]{1,0:T(8,128)(2,1)S(1)}, u32[]{:S(2)}, u32[]{:S(2)}) collective-permute-start(bf16[2048,128]{1,0:T(8,128)(2,1)S(1)} %joined0.3), channel_id=1, source_target_pairs={{0,2},{1,3},{2,6},{3,7},{4,0},{5,1},{6,4},{7,5},{8,10},{9,11},{10,... | collective-permute-start | bytes 1572872 | tf_op jit(solution)/shard_map/ppermute | solution.py:656
  55.8 15.6 %collective-permute-start.26 = (bf16[1024,128]{1,0:T(8,128)(2,1)S(1)}, bf16[1024,128]{1,0:T(8,128)(2,1)S(1)}, u32[]{:S(2)}, u32[]{:S(2)}) collective-permute-start(bf16[1024,128]{1,0:T(8,128)(2,1)S(1)} %get-tuple-element.151), channel_id=1, source_target_pairs={{0,1},{1,0},{2,3},{3,2},{4,5},{5,4},{6,7},{7,6},{8,9},{9,8},{10,11... | collective-permute-start | bytes 786440 | tf_op jit(solution)/shard_map/ppermute | solution.py:620
  56.1 15.2 %collective-permute-start.27 = (bf16[1024,128]{1,0:T(8,128)(2,1)S(1)}, bf16[1024,128]{1,0:T(8,128)(2,1)S(1)}, u32[]{:S(2)}, u32[]{:S(2)}) collective-permute-start(bf16[1024,128]{1,0:T(8,128)(2,1)S(1)} %get-tuple-element.152), channel_id=1, source_target_pairs={{0,1},{1,0},{2,3},{3,2},{4,5},{5,4},{6,7},{7,6},{8,9},{9,8},{10,11... | collective-permute-start | bytes 786440 | tf_op jit(solution)/shard_map/ppermute | solution.py:620
  57.4 4.7 %collective-permute-start.23 = (bf16[336,128]{1,0:T(8,128)(2,1)S(1)}, bf16[336,128]{1,0:T(8,128)(2,1)S(1)}, u32[]{:S(2)}, u32[]{:S(2)}) collective-permute-start(bf16[336,128]{1,0:T(8,128)(2,1)S(1)} %get-tuple-element.146), channel_id=1, source_target_pairs={{0,16},{8,24},{16,0},{24,8},{1,17},{9,25},{17,1},{25,9},{2,18},{10... | collective-permute-start | bytes 258056 | tf_op jit(solution)/shard_map/ppermute | solution.py:620
  61.8 5.4 %collective-permute-start.24 = (bf16[336,128]{1,0:T(8,128)(2,1)S(1)}, bf16[336,128]{1,0:T(8,128)(2,1)S(1)}, u32[]{:S(2)}, u32[]{:S(2)}) collective-permute-start(bf16[336,128]{1,0:T(8,128)(2,1)S(1)} %get-tuple-element.147), channel_id=1, source_target_pairs={{0,24},{8,16},{16,8},{24,0},{1,25},{9,17},{17,9},{25,1},{2,26},{10... | collective-permute-start | bytes 258056 | tf_op jit(solution)/shard_map/ppermute | solution.py:620
  71.6 14.9 %collective-permute-start.28 = (bf16[2048,128]{1,0:T(8,128)(2,1)S(1)}, bf16[2048,128]{1,0:T(8,128)(2,1)S(1)}, u32[]{:S(2)}, u32[]{:S(2)}) collective-permute-start(bf16[2048,128]{1,0:T(8,128)(2,1)S(1)} %joined0.4), channel_id=1, source_target_pairs={{0,2},{1,3},{2,6},{3,7},{4,0},{5,1},{6,4},{7,5},{8,10},{9,11},{10,... | collective-permute-start | bytes 1572872 | tf_op jit(solution)/shard_map/ppermute | solution.py:656
  73.0 13.0 %collective-permute-start.29 = (f32[48,256]{1,0:T(8,128)S(1)}, f32[48,256]{1,0:T(8,128)S(1)}, u32[]{:S(2)}, u32[]{:S(2)}) collective-permute-start(f32[48,256]{1,0:T(8,128)S(1)} %add.6), channel_id=1, source_target_pairs={{0,4},{1,5},{2,6},{3,7},{4,0},{5,1},{6,2},{7,3},{8,12},{9,13},{10,... | collective-permute-start | bytes 147464 | tf_op jit(solution)/shard_map/ppermute | solution.py:620
  76.6 9.4 %collective-permute-start.30 = (bf16[1024,128]{1,0:T(8,128)(2,1)S(1)}, bf16[1024,128]{1,0:T(8,128)(2,1)S(1)}, u32[]{:S(2)}, u32[]{:S(2)}) collective-permute-start(bf16[1024,128]{1,0:T(8,128)(2,1)S(1)} %get-tuple-element.157), channel_id=1, source_target_pairs={{0,1},{1,0},{2,3},{3,2},{4,5},{5,4},{6,7},{7,6},{8,9},{9,8},{10,11... | collective-permute-start | bytes 786440 | tf_op jit(solution)/shard_map/ppermute | solution.py:620
  76.7 9.3 %collective-permute-start.31 = (bf16[1024,128]{1,0:T(8,128)(2,1)S(1)}, bf16[1024,128]{1,0:T(8,128)(2,1)S(1)}, u32[]{:S(2)}, u32[]{:S(2)}) collective-permute-start(bf16[1024,128]{1,0:T(8,128)(2,1)S(1)} %get-tuple-element.158), channel_id=1, source_target_pairs={{0,1},{1,0},{2,3},{3,2},{4,5},{5,4},{6,7},{7,6},{8,9},{9,8},{10,11... | collective-permute-start | bytes 786440 | tf_op jit(solution)/shard_map/ppermute | solution.py:620
  77.2 9.3 %collective-permute-start.32 = (bf16[1024,128]{1,0:T(8,128)(2,1)S(1)}, bf16[1024,128]{1,0:T(8,128)(2,1)S(1)}, u32[]{:S(2)}, u32[]{:S(2)}) collective-permute-start(bf16[1024,128]{1,0:T(8,128)(2,1)S(1)} %get-tuple-element.161), channel_id=1, source_target_pairs={{0,1},{1,0},{2,3},{3,2},{4,5},{5,4},{6,7},{7,6},{8,9},{9,8},{10,11... | collective-permute-start | bytes 786440 | tf_op jit(solution)/shard_map/ppermute | solution.py:620
  87.7 14.9 %collective-permute-start.34 = (bf16[2048,128]{1,0:T(8,128)(2,1)S(1)}, bf16[2048,128]{1,0:T(8,128)(2,1)S(1)}, u32[]{:S(2)}, u32[]{:S(2)}) collective-permute-start(bf16[2048,128]{1,0:T(8,128)(2,1)S(1)} %joined0.5), channel_id=1, source_target_pairs={{0,2},{1,3},{2,6},{3,7},{4,0},{5,1},{6,4},{7,5},{8,10},{9,11},{10,... | collective-permute-start | bytes 1572872 | tf_op jit(solution)/shard_map/ppermute | solution.py:656
  88.4 5.1 %collective-permute-start.37 = (f32[48,256]{1,0:T(8,128)S(1)}, f32[48,256]{1,0:T(8,128)S(1)}, u32[]{:S(2)}, u32[]{:S(2)}) collective-permute-start(f32[48,256]{1,0:T(8,128)S(1)} %add.7.refs_0_), channel_id=1, source_target_pairs={{0,24},{8,16},{16,8},{24,0},{1,25},{9,17},{17,9},{25,1},{2,26},{10... | collective-permute-start | bytes 147464 | tf_op jit(solution)/shard_map/ppermute | solution.py:620
  (27 other events, 158.0 us)

commit v5 on v4

--- a/solution.py
+++ b/solution.py
@@ -13,6 +13,7 @@
 ROWS_PER = 4
 CHUNKS = 2
 PARTS = 2
+SUM_CHUNKS = 2
 VMEM = 28 * 1024 * 1024
 
 
@@ -550,32 +551,33 @@
     )(grad_pre, w_self, keeps, *come, *arrived)
 
 
-def joined_kernel(*refs, more):
-    out_ref = refs[-1]
-    keep_ref, parts = refs[more], refs[more + 1 : -1]
-    tall = parts[0].shape[0]
-    for j, part in enumerate(parts):
-        rows = pl.ds(j * tall, tall)
-        total = keep_ref[rows, :].astype(F32) + part[...].astype(F32)
-        if more:
-            total = total + refs[0][rows, :].astype(F32)
-        out_ref[rows, :] = total.astype(BF16)
-
-
-def joined(got, keeps, come, s):
+def joined_kernel(*refs):
+    total = refs[0][...].astype(F32)
+    for ref in refs[1:-1]:
+        total = total + ref[...].astype(F32)
+    refs[-1][...] = total.astype(BF16)
+
+
+def joined(j, got, keeps, come, s):
     _, rows, width = keeps.shape
-    keep = pl.BlockSpec((None, rows, width), lambda i: (s, 0, 0))
+    tall = rows // SUM_CHUNKS
+    keep = pl.BlockSpec((None, tall, width), lambda i: (s, j, 0))
+    part = pl.BlockSpec((tall, width), lambda i: (j, 0))
     more = () if got is None else (got,)
-    out = jax.ShapeDtypeStruct((rows, width), BF16)
-    return pl.pallas_call(
-        partial(joined_kernel, more=len(more)),
+    out = jax.ShapeDtypeStruct((tall, width), BF16)
+    if len(come) > 1:
+        per = len(come) // SUM_CHUNKS
+        assert per == 1
+        come, part = [come[j]], spec(come[j])
+    return pl.pallas_call(
+        joined_kernel,
         grid=(1,),
-        in_specs=[spec(x) for x in more] + [keep] + [spec(x) for x in come],
+        in_specs=[spec(x) for x in more] + [keep, part],
         out_specs=spec(out),
         out_shape=out,
         compiler_params=params(),
-        cost_estimate=cost(3 * rows * width, 8 * rows * width),
-        name=f"joined{s}",
+        cost_estimate=cost(3 * tall * width, 8 * tall * width),
+        name=f"joined{s}_{j}",
     )(*more, keeps, *come)
 
 
@@ -701,41 +703,40 @@
     mine, other, *pushed = grads(
         asked, row, valid, off_tiles, signal, features, aggregate, grad_pre
     )
-    come, mine, other, keep2, *more = tie(come, mine, other, keep2, *send2, *pushed)
-    send2, pushed = more[: len(send2)], more[len(send2) :]
-    got = onward(joined(None, keep[None], [come], 0))
     come2 = [swap(x) for x in send2]
+    come, mine, other, keep2, *more = tie(come, mine, other, keep2, *come2, *pushed)
+    come2, pushed = more[: len(come2)], more[len(come2) :]
+    each = range(SUM_CHUNKS)
+    got = [onward(joined(j, None, keep[None], [come], 0)) for j in each]
     packed = pack(mine, swap(other), pushed)
     arrived = [packed[0]] + [to_peer(packed[k], "wide", k) for k in range(1, wide)]
     total = piece_sum(arrived)
     if not power(steps):
         total = lax.psum(total, "narrow", axis_index_groups=[list(range(c, n, 2)) for c in (0, 1)])
     later = tuple((s + 3) % steps for s in range(steps - 2))
-    k = 1
     for s in range(steps - 2):
-        if power(steps) and k < steps:
-            total = total + to_peer(total, "narrow", 2 * k)
-            k *= 2
-        got, total = tie(got, total)
         if s == 0:
-            got, signal = tie(got, signal)
-            going = joined(got, keep2, come2, 0)
+            got[0], _ = tie(got[0], total)
+            if power(steps):
+                total = tree_sum([total] + [to_peer(total, "narrow", 2 * k) for k in range(1, steps)])
+        elif s == 1:
+            got[0], total = tie(got[0], total)
+            pieces = [total] + [to_peer(total, "wide", k) for k in range(1, wide)]
+        if s == 0:
+            got[0], signal = tie(got[0], signal)
+            going = [joined(j, got[j], keep2, come2, 0) for j in each]
             keeps, sends = push(cols, signal, halved, later)
             comes = [swap(x) for x in sends]
             rest = base(grad_pre, weight_self, keeps, comes[-PARTS:], arrived)
         else:
-            if s == 1:
-                got, rest = tie(got, rest)
-            going = joined(got, keeps, comes[(s - 1) * PARTS : s * PARTS], s - 1)
-        got = onward(going)
-    while power(steps) and k < steps:
-        total = total + to_peer(total, "narrow", 2 * k)
-        k *= 2
-    pieces = [total] + [to_peer(total, "wide", k) for k in range(1, wide)]
+            mid = comes[(s - 1) * PARTS : s * PARTS]
+            going = [joined(j, got[j], keeps, mid, s - 1) for j in each]
+        got = [onward(x) for x in going]
+    got[0], rest, *pieces = tie(got[0], rest, *pieces)
     whole = half(pieces, (wide * n * row_count) ** (-0.5))
     grad_self, grad_neigh, grad_bias = finish(whole, swap(whole))
-    got, grad_self, grad_neigh, grad_bias = tie(got, grad_self, grad_neigh, grad_bias)
-    grad_features = last(rest, [got])
+    got[-1], grad_self, grad_neigh, grad_bias = tie(got[-1], grad_self, grad_neigh, grad_bias)
+    grad_features = last(rest, got)
     return layer_out, grad_features, grad_self, grad_neigh, grad_bias.reshape(-1)
 
 

time: 104 us -> 97.6 us (0.938)
  waiting for transfers between devices: 42.9 us -> 27.3 us
  starting transfers between devices: 35.5 us -> 44.8 us
    ppermute x30 -> x31, waiting for transfers between devices: 33 us -> 16.6 us  [to_peer(): lax.ppermute(x, axis, [(i, i ^ k if power(size) else (i + k) % size) for...]
    ppermute x9 -> x12, starting transfers between devices: 17.8 us -> 22.9 us  [onward(): lax.ppermute(x, 'narrow', [(i, after[i // 2] * 2 + i % 2) for i in range(...]
    ppermute x30 -> x31, starting transfers between devices: 17.7 us -> 21.9 us  [to_peer(): lax.ppermute(x, axis, [(i, i ^ k if power(size) else (i + k) % size) for...]
    ppermute x9 -> x12, waiting for transfers between devices: 9.87 us -> 10.7 us  [onward(): lax.ppermute(x, 'narrow', [(i, after[i // 2] * 2 + i % 2) for i in range(...]
  transfers between devices with their start and end apart: 39 -> 43, of which waited for: 18 -> 19; matrix products, arithmetic and copies ran while one was open for 1% -> 1% of each run, Pallas kernels for 12% -> 13%
where the time goes in v5:
time: 97.6 us; the launch traced here: 97.4 us
  starting transfers between devices  44.8 us (46%)
  waiting for transfers between devices  27.3 us (28%)
  Pallas kernels  19.1 us (20%)
  local copies, waits for them, and re-layouts  5.19 us (5%)
    ppermute x12, starting transfers between devices, onward(): lax.ppermute(x, 'narrow', [(i, after[i // 2] * 2 + i % 2) for i in range(...  22.9 us
    ppermute x31, starting transfers between devices, to_peer(): lax.ppermute(x, axis, [(i, i ^ k if power(size) else (i + k) % size) for...  21.9 us
    ppermute x31, waiting for transfers between devices, to_peer(): lax.ppermute(x, axis, [(i, i ^ k if power(size) else (i + k) % size) for...  16.6 us
    ppermute x12, waiting for transfers between devices, onward(): lax.ppermute(x, 'narrow', [(i, after[i // 2] * 2 + i % 2) for i in range(...  10.7 us
    pallas_call x3, Pallas kernels, pull(): pl.pallas_call(partial(pull_kernel, n=n, step=step, chunks=len(own) + len...  5.41 us
    pallas_call x1, Pallas kernels, middle(): pl.pallas_call(partial(middle_kernel, n=n, steps=steps, chunks=len(own)),...  5.35 us
    unnamed x24, local copies, waits for them, and re-layouts  4.12 us
    pallas_call x2, Pallas kernels, push(): pl.pallas_call(partial(push_kernel, n=n, which=which), grid_spec=pltpu.Pr...  3.2 us
  transfers between devices with their start and end apart: 43, of which 19 were waited for; matrix products, arithmetic and copies ran while one was open for 1% of the time, Pallas kernels for 13%

profile of v5, /device:TPU:0, one launch (start us, length us, event | category | flops | bytes accessed | tf_op | source)
XLA Modules:
  0.0 97.4 jit_solution(16415597303465450073)
XLA Ops:
  2.2 2.6 %collective-permute-start.5 = (bf16[1024,128]{1,0:T(8,128)(2,1)S(1)}, bf16[1024,128]{1,0:T(8,128)(2,1)S(1)}, u32[]{:S(2)}, u32[]{:S(2)}) collective-permute-start(bf16[1024,128]{1,0:T(8,128)(2,1)S(1)} %get-tuple-element.177.refs_1_), channel_id=1, source_target_pairs={{0,2},{1,3},{2,6},{3,7},{4,0},{5,1},{6,4},{7,5},{8,10},{9,11},{10,... | collective-permute-start | bytes 786440 | tf_op jit(solution)/shard_map/ppermute | solution.py:658
  4.9 2.6 %collective-permute-start = (bf16[1024,128]{1,0:T(8,128)(2,1)S(1)}, bf16[1024,128]{1,0:T(8,128)(2,1)S(1)}, u32[]{:S(2)}, u32[]{:S(2)}) collective-permute-start(bf16[1024,128]{1,0:T(8,128)(2,1)S(1)} %get-tuple-element.178.refs_2_), channel_id=1, source_target_pairs={{0,2},{1,3},{2,6},{3,7},{4,0},{5,1},{6,4},{7,5},{8,10},{9,11},{10,... | collective-permute-start | bytes 786440 | tf_op jit(solution)/shard_map/ppermute | solution.py:658
  7.5 3.4 %copy-done = s32[16,8,128,128]{3,2,1,0:T(8,128)S(1)} copy-done((s32[16,8,128,128]{3,2,1,0:T(8,128)S(1)}, s32[16,8,128,128]{3,2,1,0:T(8,128)}, u32[]{:S(2)}) %copy-start) | copy-done | bytes 8388632
  11.5 1.8 %pull0.1 = (f32[2048,128]{1,0:T(8,128)S(1)}, f32[2048,128]{1,0:T(8,128)S(1)}) custom-call(s32[8,16]{1,0:T(8,128)S(1)} %bitcast.8, s32[16,8,128,128]{3,2,1,0:T(8,128)S(1)} %copy-done, bf16[1024,128]{1,0:T(8,128)(2,1)S(1)} %get-tuple-element.177.refs_1_, bf16[1024,128]{1,0:T(8,128)(2,1)S(1)} %get-tuple-element.178.refs_2_, ...), custom_call_target="tpu_custom_call" | custom-call | flops 134217728 | bytes 3145728 | tf_op jit(solution)/shard_map/pull0/pallas_call | solution.py:158
  14.1 2.4 %collective-permute-start.3 = (s32[4]{0:T(128)S(1)}, s32[4]{0:T(128)S(1)}, u32[]{:S(2)}, u32[]{:S(2)}) collective-permute-start(s32[4]{0:T(128)S(1)} %bitcast.18), channel_id=1, source_target_pairs={{0,24},{8,16},{16,8},{24,0},{1,25},{9,17},{17,9},{25,1},{2,26},{10... | collective-permute-start | bytes 56 | tf_op jit(solution)/shard_map/ppermute | solution.py:622
  21.1 3.4 %collective-permute-start.4 = (bf16[1024,128]{1,0:T(8,128)(2,1)S(1)}, bf16[1024,128]{1,0:T(8,128)(2,1)S(1)}, u32[]{:S(2)}, u32[]{:S(2)}) collective-permute-start(bf16[1024,128]{1,0:T(8,128)(2,1)S(1)} %collective-permute-done.refs_2_), channel_id=1, source_target_pairs={{0,2},{1,3},{2,6},{3,7},{4,0},{5,1},{6,4},{7,5},{8,10},{9,11},{10,... | collective-permute-start | bytes 786440 | tf_op jit(solution)/shard_map/ppermute | solution.py:658
  25.5 2.0 %collective-permute-start.9 = (bf16[128,128]{1,0:T(8,128)(2,1)S(1)}, bf16[128,128]{1,0:T(8,128)(2,1)S(1)}, u32[]{:S(2)}, u32[]{:S(2)}) collective-permute-start(bf16[128,128]{1,0:T(8,128)(2,1)S(1)} %get-tuple-element.108), channel_id=1, source_target_pairs={{0,8},{8,0},{16,24},{24,16},{1,9},{9,1},{17,25},{25,17},{2,10},{10... | collective-permute-start | bytes 98312 | tf_op jit(solution)/shard_map/ppermute | solution.py:622
  29.1 1.8 %pull1.1 = (f32[2048,128]{1,0:T(8,128)S(1)}, f32[2048,128]{1,0:T(8,128)S(1)}) custom-call(s32[8,16]{1,0:T(8,128)S(1)} %bitcast.9, s32[16,8,128,128]{3,2,1,0:T(8,128)S(1)} %copy-done.1, bf16[1024,128]{1,0:T(8,128)(2,1)S(1)} %collective-permute-done.5.refs_1_, bf16[1024,128]{1,0:T(8,128)(2,1)S(1)} %collective-permute-done.refs_2_, ...), custom_call_target="tpu_custom_call" | custom-call | flops 134217728 | bytes 3145728 | tf_op jit(solution)/shard_map/pull1/pallas_call | solution.py:158
  31.7 2.1 %collective-permute-done.11.refs_13_ = bf16[128,128]{1,0:T(8,128)(2,1)S(1)} collective-permute-done((bf16[128,128]{1,0:T(8,128)(2,1)S(1)}, bf16[128,128]{1,0:T(8,128)(2,1)S(1)}, u32[]{:S(2)}, u32[]{:S(2)}) %collective-permute-start.11) | collective-permute-done | bytes 32800 | tf_op jit(solution)/shard_map/ppermute | solution.py:622
  34.3 3.4 %collective-permute-start.12 = (bf16[1024,128]{1,0:T(8,128)(2,1)S(1)}, bf16[1024,128]{1,0:T(8,128)(2,1)S(1)}, u32[]{:S(2)}, u32[]{:S(2)}) collective-permute-start(bf16[1024,128]{1,0:T(8,128)(2,1)S(1)} %collective-permute-done.4.refs_4_), channel_id=1, source_target_pairs={{0,2},{1,3},{2,6},{3,7},{4,0},{5,1},{6,4},{7,5},{8,10},{9,11},{10,... | collective-permute-start | bytes 786440 | tf_op jit(solution)/shard_map/ppermute | solution.py:658
  38.4 1.8 %pull2.1 = (f32[2048,128]{1,0:T(8,128)S(1)}, f32[2048,128]{1,0:T(8,128)S(1)}) custom-call(s32[8,16]{1,0:T(8,128)S(1)} %bitcast.10, s32[4]{0:T(128)S(1)} %bitcast.14, s32[4]{0:T(128)S(1)} %bitcast.16, s32[16,8,128,128]{3,2,1,0:T(8,128)S(1)} %copy-done.1, bf16[1024,128]{1,0:T(8,128)(2,1)S(1)} %collective-permute-done.13.refs_3_, ...), custom_call_target="tpu_custom_call" | custom-call | flops 134217728 | bytes 3145728 | tf_op jit(solution)/shard_map/pull2/pallas_call | solution.py:158
  40.3 3.1 %collective-permute-done.12.refs_1_ = bf16[1024,128]{1,0:T(8,128)(2,1)S(1)} collective-permute-done((bf16[1024,128]{1,0:T(8,128)(2,1)S(1)}, bf16[1024,128]{1,0:T(8,128)(2,1)S(1)}, u32[]{:S(2)}, u32[]{:S(2)}) %collective-permute-start.12) | collective-permute-done | bytes 262176 | tf_op jit(solution)/shard_map/ppermute | solution.py:658
  45.0 5.4 %middle.1 = (bf16[2048,256]{1,0:T(8,128)(2,1)}, bf16[2048,256]{1,0:T(8,128)(2,1)S(1)}, bf16[2048,128]{1,0:T(8,128)(2,1)S(1)}, bf16[2048,128]{1,0:T(8,128)(2,1)S(...) custom-call(s32[8,16]{1,0:T(8,128)S(1)} %bitcast.11, bf16[16,8,128,128]{3,2,1,0:T(8,128)(2,1)S(1)} %halve.1.tiles_ref, ...), custom_call_target="tpu_custom_call" | custom-call | flops 671088640 | bytes 7864320 | tf_op jit(solution)/shard_map/middle/pallas_call | solution.py:278
  54.3 2.5 %collective-permute-start.22 = (bf16[1024,128]{1,0:T(8,128)(2,1)S(1)}, bf16[1024,128]{1,0:T(8,128)(2,1)S(1)}, u32[]{:S(2)}, u32[]{:S(2)}) collective-permute-start(bf16[1024,128]{1,0:T(8,128)(2,1)S(1)} %joined0_0.3), channel_id=1, source_target_pairs={{0,2},{1,3},{2,6},{3,7},{4,0},{5,1},{6,4},{7,5},{8,10},{9,11},{10,... | collective-permute-start | bytes 786440 | tf_op jit(solution)/shard_map/ppermute | solution.py:658
  57.7 2.8 %collective-permute-start.26 = (bf16[336,128]{1,0:T(8,128)(2,1)S(1)}, bf16[336,128]{1,0:T(8,128)(2,1)S(1)}, u32[]{:S(2)}, u32[]{:S(2)}) collective-permute-start(bf16[336,128]{1,0:T(8,128)(2,1)S(1)} %get-tuple-element.150), channel_id=1, source_target_pairs={{0,24},{8,16},{16,8},{24,0},{1,25},{9,17},{17,9},{25,1},{2,26},{10... | collective-permute-start | bytes 258056 | tf_op jit(solution)/shard_map/ppermute | solution.py:622
  64.2 2.0 %collective-permute-start.27 = (bf16[1024,128]{1,0:T(8,128)(2,1)S(1)}, bf16[1024,128]{1,0:T(8,128)(2,1)S(1)}, u32[]{:S(2)}, u32[]{:S(2)}) collective-permute-start(bf16[1024,128]{1,0:T(8,128)(2,1)S(1)} %joined0_0.4), channel_id=1, source_target_pairs={{0,2},{1,3},{2,6},{3,7},{4,0},{5,1},{6,4},{7,5},{8,10},{9,11},{10,... | collective-permute-start | bytes 786440 | tf_op jit(solution)/shard_map/ppermute | solution.py:658
  66.1 1.6 %collective-permute-start.30 = (f32[48,256]{1,0:T(8,128)S(1)}, f32[48,256]{1,0:T(8,128)S(1)}, u32[]{:S(2)}, u32[]{:S(2)}) collective-permute-start(f32[48,256]{1,0:T(8,128)S(1)} %piece_sum.1), channel_id=1, source_target_pairs={{0,6},{1,7},{2,4},{3,5},{4,2},{5,3},{6,0},{7,1},{8,14},{9,15},{10,... | collective-permute-start | bytes 147464 | tf_op jit(solution)/shard_map/ppermute | solution.py:622
  67.7 1.9 %collective-permute-start.29 = (f32[48,256]{1,0:T(8,128)S(1)}, f32[48,256]{1,0:T(8,128)S(1)}, u32[]{:S(2)}, u32[]{:S(2)}) collective-permute-start(f32[48,256]{1,0:T(8,128)S(1)} %piece_sum.1), channel_id=1, source_target_pairs={{0,4},{1,5},{2,6},{3,7},{4,0},{5,1},{6,2},{7,3},{8,12},{9,13},{10,... | collective-permute-start | bytes 147464 | tf_op jit(solution)/shard_map/ppermute | solution.py:622
  70.5 1.9 %push.3 = (bf16[2,2048,128]{2,1,0:T(8,128)(2,1)S(1)}, bf16[1024,128]{1,0:T(8,128)(2,1)S(1)}, bf16[1024,128]{1,0:T(8,128)(2,1)S(1)}, bf16[1024,128]{1,0:T(8,128)(2,1)S(1)}, bf16[1024,128]{1,0:T(8,128)(2,1)S(1)}) custom-call(s32[8,16]{1,0:T(8,128)S(1)} %bitcast.13, bf16[16,8,128,128]{3,2,1,0:T(8,128)(2,1)S(1)} %halve.1.tiles_ref, ...), custom_call_target="tpu_custom_call" | custom-call | flops 268435456 | bytes 4194304 | tf_op jit(solution)/shard_map/push/pallas_call | solution.py:322
  72.6 4.3 %collective-permute-done.30 = f32[48,256]{1,0:T(8,128)S(1)} collective-permute-done((f32[48,256]{1,0:T(8,128)S(1)}, f32[48,256]{1,0:T(8,128)S(1)}, u32[]{:S(2)}, u32[]{:S(2)}) %collective-permute-start.30) | collective-permute-done | bytes 49184 | tf_op jit(solution)/shard_map/ppermute | solution.py:622
  76.9 2.2 %collective-permute-start.39 = (bf16[1024,128]{1,0:T(8,128)(2,1)S(1)}, bf16[1024,128]{1,0:T(8,128)(2,1)S(1)}, u32[]{:S(2)}, u32[]{:S(2)}) collective-permute-start(bf16[1024,128]{1,0:T(8,128)(2,1)S(1)} %joined0_1.4), channel_id=1, source_target_pairs={{0,2},{1,3},{2,6},{3,7},{4,0},{5,1},{6,4},{7,5},{8,10},{9,11},{10,... | collective-permute-start | bytes 786440 | tf_op jit(solution)/shard_map/ppermute | solution.py:658
  81.4 4.9 %collective-permute-done.39.refs_0_ = bf16[1024,128]{1,0:T(8,128)(2,1)S(1)} collective-permute-done((bf16[1024,128]{1,0:T(8,128)(2,1)S(1)}, bf16[1024,128]{1,0:T(8,128)(2,1)S(1)}, u32[]{:S(2)}, u32[]{:S(2)}) %collective-permute-start.39) | collective-permute-done | bytes 262176 | tf_op jit(solution)/shard_map/ppermute | solution.py:658
  88.3 1.9 %collective-permute-start.35 = (f32[48,256]{1,0:T(8,128)S(1)}, f32[48,256]{1,0:T(8,128)S(1)}, u32[]{:S(2)}, u32[]{:S(2)}) collective-permute-start(f32[48,256]{1,0:T(8,128)S(1)} %add_add_fusion.refs_0_), channel_id=1, source_target_pairs={{0,8},{8,0},{16,24},{24,16},{1,9},{9,1},{17,25},{25,17},{2,10},{10... | collective-permute-start | bytes 147464 | tf_op jit(solution)/shard_map/ppermute | solution.py:622
  94.6 1.7 %collective-permute-done.41.refs_1_ = bf16[1024,128]{1,0:T(8,128)(2,1)S(1)} collective-permute-done((bf16[1024,128]{1,0:T(8,128)(2,1)S(1)}, bf16[1024,128]{1,0:T(8,128)(2,1)S(1)}, u32[]{:S(2)}, u32[]{:S(2)}) %collective-permute-start.41) | collective-permute-done | bytes 262176 | tf_op jit(solution)/shard_map/ppermute | solution.py:658
  (110 shorter events, 32.9 us)
Async XLA Ops:
  0.7 6.8 %collective-permute-start.6 = (bf16[2048,128]{1,0:T(8,128)(2,1)}, bf16[2048,128]{1,0:T(8,128)(2,1)S(1)}, u32[]{:S(2)}, u32[]{:S(2)}) collective-permute-start(bf16[2048,128]{1,0:T(8,128)(2,1)} %feat_ref.3), channel_id=1, source_target_pairs={{0,1},{1,0},{2,3},{3,2},{4,5},{5,4},{6,7},{7,6},{8,9},{9,8},{10,11... | collective-permute-start | bytes 1572872 | tf_op jit(solution)/shard_map/ppermute | solution.py:622
  2.2 11.1 %collective-permute-start.5 = (bf16[1024,128]{1,0:T(8,128)(2,1)S(1)}, bf16[1024,128]{1,0:T(8,128)(2,1)S(1)}, u32[]{:S(2)}, u32[]{:S(2)}) collective-permute-start(bf16[1024,128]{1,0:T(8,128)(2,1)S(1)} %get-tuple-element.177.refs_1_), channel_id=1, source_target_pairs={{0,2},{1,3},{2,6},{3,7},{4,0},{5,1},{6,4},{7,5},{8,10},{9,11},{10,... | collective-permute-start | bytes 786440 | tf_op jit(solution)/shard_map/ppermute | solution.py:658
  4.9 15.7 %collective-permute-start = (bf16[1024,128]{1,0:T(8,128)(2,1)S(1)}, bf16[1024,128]{1,0:T(8,128)(2,1)S(1)}, u32[]{:S(2)}, u32[]{:S(2)}) collective-permute-start(bf16[1024,128]{1,0:T(8,128)(2,1)S(1)} %get-tuple-element.178.refs_2_), channel_id=1, source_target_pairs={{0,2},{1,3},{2,6},{3,7},{4,0},{5,1},{6,4},{7,5},{8,10},{9,11},{10,... | collective-permute-start | bytes 786440 | tf_op jit(solution)/shard_map/ppermute | solution.py:658
  13.3 11.2 %collective-permute-start.13 = (bf16[1024,128]{1,0:T(8,128)(2,1)S(1)}, bf16[1024,128]{1,0:T(8,128)(2,1)S(1)}, u32[]{:S(2)}, u32[]{:S(2)}) collective-permute-start(bf16[1024,128]{1,0:T(8,128)(2,1)S(1)} %collective-permute-done.5.refs_1_), channel_id=1, source_target_pairs={{0,2},{1,3},{2,6},{3,7},{4,0},{5,1},{6,4},{7,5},{8,10},{9,11},{10,... | collective-permute-start | bytes 786440 | tf_op jit(solution)/shard_map/ppermute | solution.py:658
  20.6 6.9 %collective-permute-start.8 = (bf16[1024,128]{1,0:T(8,128)(2,1)S(1)}, bf16[1024,128]{1,0:T(8,128)(2,1)S(1)}, u32[]{:S(2)}, u32[]{:S(2)}) collective-permute-start(bf16[1024,128]{1,0:T(8,128)(2,1)S(1)} %collective-permute-done.refs_2_), channel_id=1, source_target_pairs={{0,1},{1,0},{2,3},{3,2},{4,5},{5,4},{6,7},{7,6},{8,9},{9,8},{10,11... | collective-permute-start | bytes 786440 | tf_op jit(solution)/shard_map/ppermute | solution.py:622
  20.6 8.4 %collective-permute-start.7 = (bf16[1024,128]{1,0:T(8,128)(2,1)S(1)}, bf16[1024,128]{1,0:T(8,128)(2,1)S(1)}, u32[]{:S(2)}, u32[]{:S(2)}) collective-permute-start(bf16[1024,128]{1,0:T(8,128)(2,1)S(1)} %collective-permute-done.5.refs_1_), channel_id=1, source_target_pairs={{0,1},{1,0},{2,3},{3,2},{4,5},{5,4},{6,7},{7,6},{8,9},{9,8},{10,11... | collective-permute-start | bytes 786440 | tf_op jit(solution)/shard_map/ppermute | solution.py:622
  21.1 10.1 %collective-permute-start.4 = (bf16[1024,128]{1,0:T(8,128)(2,1)S(1)}, bf16[1024,128]{1,0:T(8,128)(2,1)S(1)}, u32[]{:S(2)}, u32[]{:S(2)}) collective-permute-start(bf16[1024,128]{1,0:T(8,128)(2,1)S(1)} %collective-permute-done.refs_2_), channel_id=1, source_target_pairs={{0,2},{1,3},{2,6},{3,7},{4,0},{5,1},{6,4},{7,5},{8,10},{9,11},{10,... | collective-permute-start | bytes 786440 | tf_op jit(solution)/shard_map/ppermute | solution.py:658
  24.5 13.2 %collective-permute-start.16 = (bf16[1024,128]{1,0:T(8,128)(2,1)S(1)}, bf16[1024,128]{1,0:T(8,128)(2,1)S(1)}, u32[]{:S(2)}, u32[]{:S(2)}) collective-permute-start(bf16[1024,128]{1,0:T(8,128)(2,1)S(1)} %collective-permute-done.13.refs_3_), channel_id=1, source_target_pairs={{0,2},{1,3},{2,6},{3,7},{4,0},{5,1},{6,4},{7,5},{8,10},{9,11},{10,... | collective-permute-start | bytes 786440 | tf_op jit(solution)/shard_map/ppermute | solution.py:658
  34.3 9.1 %collective-permute-start.12 = (bf16[1024,128]{1,0:T(8,128)(2,1)S(1)}, bf16[1024,128]{1,0:T(8,128)(2,1)S(1)}, u32[]{:S(2)}, u32[]{:S(2)}) collective-permute-start(bf16[1024,128]{1,0:T(8,128)(2,1)S(1)} %collective-permute-done.4.refs_4_), channel_id=1, source_target_pairs={{0,2},{1,3},{2,6},{3,7},{4,0},{5,1},{6,4},{7,5},{8,10},{9,11},{10,... | collective-permute-start | bytes 786440 | tf_op jit(solution)/shard_map/ppermute | solution.py:658
  54.3 9.8 %collective-permute-start.22 = (bf16[1024,128]{1,0:T(8,128)(2,1)S(1)}, bf16[1024,128]{1,0:T(8,128)(2,1)S(1)}, u32[]{:S(2)}, u32[]{:S(2)}) collective-permute-start(bf16[1024,128]{1,0:T(8,128)(2,1)S(1)} %joined0_0.3), channel_id=1, source_target_pairs={{0,2},{1,3},{2,6},{3,7},{4,0},{5,1},{6,4},{7,5},{8,10},{9,11},{10,... | collective-permute-start | bytes 786440 | tf_op jit(solution)/shard_map/ppermute | solution.py:658
  57.1 6.3 %collective-permute-start.25 = (bf16[336,128]{1,0:T(8,128)(2,1)S(1)}, bf16[336,128]{1,0:T(8,128)(2,1)S(1)}, u32[]{:S(2)}, u32[]{:S(2)}) collective-permute-start(bf16[336,128]{1,0:T(8,128)(2,1)S(1)} %get-tuple-element.149), channel_id=1, source_target_pairs={{0,16},{8,24},{16,0},{24,8},{1,17},{9,25},{17,1},{25,9},{2,18},{10... | collective-permute-start | bytes 258056 | tf_op jit(solution)/shard_map/ppermute | solution.py:622
  57.7 5.7 %collective-permute-start.26 = (bf16[336,128]{1,0:T(8,128)(2,1)S(1)}, bf16[336,128]{1,0:T(8,128)(2,1)S(1)}, u32[]{:S(2)}, u32[]{:S(2)}) collective-permute-start(bf16[336,128]{1,0:T(8,128)(2,1)S(1)} %get-tuple-element.150), channel_id=1, source_target_pairs={{0,24},{8,16},{16,8},{24,0},{1,25},{9,17},{17,9},{25,1},{2,26},{10... | collective-permute-start | bytes 258056 | tf_op jit(solution)/shard_map/ppermute | solution.py:622
  60.5 11.9 %collective-permute-start.38 = (bf16[1024,128]{1,0:T(8,128)(2,1)S(1)}, bf16[1024,128]{1,0:T(8,128)(2,1)S(1)}, u32[]{:S(2)}, u32[]{:S(2)}) collective-permute-start(bf16[1024,128]{1,0:T(8,128)(2,1)S(1)} %joined0_1.3), channel_id=1, source_target_pairs={{0,2},{1,3},{2,6},{3,7},{4,0},{5,1},{6,4},{7,5},{8,10},{9,11},{10,... | collective-permute-start | bytes 786440 | tf_op jit(solution)/shard_map/ppermute | solution.py:658
  64.2 15.5 %collective-permute-start.27 = (bf16[1024,128]{1,0:T(8,128)(2,1)S(1)}, bf16[1024,128]{1,0:T(8,128)(2,1)S(1)}, u32[]{:S(2)}, u32[]{:S(2)}) collective-permute-start(bf16[1024,128]{1,0:T(8,128)(2,1)S(1)} %joined0_0.4), channel_id=1, source_target_pairs={{0,2},{1,3},{2,6},{3,7},{4,0},{5,1},{6,4},{7,5},{8,10},{9,11},{10,... | collective-permute-start | bytes 786440 | tf_op jit(solution)/shard_map/ppermute | solution.py:658
  66.1 10.8 %collective-permute-start.30 = (f32[48,256]{1,0:T(8,128)S(1)}, f32[48,256]{1,0:T(8,128)S(1)}, u32[]{:S(2)}, u32[]{:S(2)}) collective-permute-start(f32[48,256]{1,0:T(8,128)S(1)} %piece_sum.1), channel_id=1, source_target_pairs={{0,6},{1,7},{2,4},{3,5},{4,2},{5,3},{6,0},{7,1},{8,14},{9,15},{10,... | collective-permute-start | bytes 147464 | tf_op jit(solution)/shard_map/ppermute | solution.py:622
  67.7 11.4 %collective-permute-start.29 = (f32[48,256]{1,0:T(8,128)S(1)}, f32[48,256]{1,0:T(8,128)S(1)}, u32[]{:S(2)}, u32[]{:S(2)}) collective-permute-start(f32[48,256]{1,0:T(8,128)S(1)} %piece_sum.1), channel_id=1, source_target_pairs={{0,4},{1,5},{2,6},{3,7},{4,0},{5,1},{6,2},{7,3},{8,12},{9,13},{10,... | collective-permute-start | bytes 147464 | tf_op jit(solution)/shard_map/ppermute | solution.py:622
  69.7 9.5 %collective-permute-start.28 = (f32[48,256]{1,0:T(8,128)S(1)}, f32[48,256]{1,0:T(8,128)S(1)}, u32[]{:S(2)}, u32[]{:S(2)}) collective-permute-start(f32[48,256]{1,0:T(8,128)S(1)} %piece_sum.1), channel_id=1, source_target_pairs={{0,2},{1,3},{2,0},{3,1},{4,6},{5,7},{6,4},{7,5},{8,10},{9,11},{10,... | collective-permute-start | bytes 147464 | tf_op jit(solution)/shard_map/ppermute | solution.py:622
  72.4 7.3 %collective-permute-start.31 = (bf16[1024,128]{1,0:T(8,128)(2,1)S(1)}, bf16[1024,128]{1,0:T(8,128)(2,1)S(1)}, u32[]{:S(2)}, u32[]{:S(2)}) collective-permute-start(bf16[1024,128]{1,0:T(8,128)(2,1)S(1)} %get-tuple-element.158), channel_id=1, source_target_pairs={{0,1},{1,0},{2,3},{3,2},{4,5},{5,4},{6,7},{7,6},{8,9},{9,8},{10,11... | collective-permute-start | bytes 786440 | tf_op jit(solution)/shard_map/ppermute | solution.py:622
  76.9 9.4 %collective-permute-start.39 = (bf16[1024,128]{1,0:T(8,128)(2,1)S(1)}, bf16[1024,128]{1,0:T(8,128)(2,1)S(1)}, u32[]{:S(2)}, u32[]{:S(2)}) collective-permute-start(bf16[1024,128]{1,0:T(8,128)(2,1)S(1)} %joined0_1.4), channel_id=1, source_target_pairs={{0,2},{1,3},{2,6},{3,7},{4,0},{5,1},{6,4},{7,5},{8,10},{9,11},{10,... | collective-permute-start | bytes 786440 | tf_op jit(solution)/shard_map/ppermute | solution.py:658
  79.1 9.0 %collective-permute-start.33 = (bf16[1024,128]{1,0:T(8,128)(2,1)S(1)}, bf16[1024,128]{1,0:T(8,128)(2,1)S(1)}, u32[]{:S(2)}, u32[]{:S(2)}) collective-permute-start(bf16[1024,128]{1,0:T(8,128)(2,1)S(1)} %get-tuple-element.159), channel_id=1, source_target_pairs={{0,1},{1,0},{2,3},{3,2},{4,5},{5,4},{6,7},{7,6},{8,9},{9,8},{10,11... | collective-permute-start | bytes 786440 | tf_op jit(solution)/shard_map/ppermute | solution.py:622
  79.1 9.1 %collective-permute-start.34 = (bf16[1024,128]{1,0:T(8,128)(2,1)S(1)}, bf16[1024,128]{1,0:T(8,128)(2,1)S(1)}, u32[]{:S(2)}, u32[]{:S(2)}) collective-permute-start(bf16[1024,128]{1,0:T(8,128)(2,1)S(1)} %get-tuple-element.160), channel_id=1, source_target_pairs={{0,1},{1,0},{2,3},{3,2},{4,5},{5,4},{6,7},{7,6},{8,9},{9,8},{10,11... | collective-permute-start | bytes 786440 | tf_op jit(solution)/shard_map/ppermute | solution.py:622
  79.6 6.7 %collective-permute-start.40 = (bf16[1024,128]{1,0:T(8,128)(2,1)S(1)}, bf16[1024,128]{1,0:T(8,128)(2,1)S(1)}, u32[]{:S(2)}, u32[]{:S(2)}) collective-permute-start(bf16[1024,128]{1,0:T(8,128)(2,1)S(1)} %get-tuple-element.165), channel_id=1, source_target_pairs={{0,1},{1,0},{2,3},{3,2},{4,5},{5,4},{6,7},{7,6},{8,9},{9,8},{10,11... | collective-permute-start | bytes 786440 | tf_op jit(solution)/shard_map/ppermute | solution.py:622
  79.8 12.5 %collective-permute-start.32 = (bf16[1024,128]{1,0:T(8,128)(2,1)S(1)}, bf16[1024,128]{1,0:T(8,128)(2,1)S(1)}, u32[]{:S(2)}, u32[]{:S(2)}) collective-permute-start(bf16[1024,128]{1,0:T(8,128)(2,1)S(1)} %joined0_0.5), channel_id=1, source_target_pairs={{0,2},{1,3},{2,6},{3,7},{4,0},{5,1},{6,4},{7,5},{8,10},{9,11},{10,... | collective-permute-start | bytes 786440 | tf_op jit(solution)/shard_map/ppermute | solution.py:658
  86.4 9.9 %collective-permute-start.41 = (bf16[1024,128]{1,0:T(8,128)(2,1)S(1)}, bf16[1024,128]{1,0:T(8,128)(2,1)S(1)}, u32[]{:S(2)}, u32[]{:S(2)}) collective-permute-start(bf16[1024,128]{1,0:T(8,128)(2,1)S(1)} %joined0_1.5), channel_id=1, source_target_pairs={{0,2},{1,3},{2,6},{3,7},{4,0},{5,1},{6,4},{7,5},{8,10},{9,11},{10,... | collective-permute-start | bytes 786440 | tf_op jit(solution)/shard_map/ppermute | solution.py:658
  (31 other events, 179.2 us)

commit v6 on v5

--- a/solution.py
+++ b/solution.py
@@ -720,14 +720,14 @@
             if power(steps):
                 total = tree_sum([total] + [to_peer(total, "narrow", 2 * k) for k in range(1, steps)])
         elif s == 1:
-            got[0], total = tie(got[0], total)
+            got[0], total, *own = tie(got[0], total, *sends[-PARTS:])
+            rest = base(grad_pre, weight_self, keeps, [swap(x) for x in own], arrived)
             pieces = [total] + [to_peer(total, "wide", k) for k in range(1, wide)]
         if s == 0:
             got[0], signal = tie(got[0], signal)
             going = [joined(j, got[j], keep2, come2, 0) for j in each]
             keeps, sends = push(cols, signal, halved, later)
-            comes = [swap(x) for x in sends]
-            rest = base(grad_pre, weight_self, keeps, comes[-PARTS:], arrived)
+            comes = [swap(x) for x in sends[:-PARTS]]
         else:
             mid = comes[(s - 1) * PARTS : s * PARTS]
             going = [joined(j, got[j], keeps, mid, s - 1) for j in each]

time: 97.6 us -> 97.2 us (level)
  starting transfers between devices: 44.8 us -> 41 us
  waiting for transfers between devices: 27.3 us -> 30.7 us
    ppermute x12, waiting for transfers between devices: 10.7 us -> 17.1 us  [onward(): lax.ppermute(x, 'narrow', [(i, after[i // 2] * 2 + i % 2) for i in range(...]
    ppermute x12, starting transfers between devices: 22.9 us -> 18.6 us  [onward(): lax.ppermute(x, 'narrow', [(i, after[i // 2] * 2 + i % 2) for i in range(...]
    ppermute x31, waiting for transfers between devices: 16.6 us -> 13.6 us  [to_peer(): lax.ppermute(x, axis, [(i, i ^ k if power(size) else (i + k) % size) for...]
where the time goes in v6:
time: 97.2 us; the launch traced here: 97 us
  starting transfers between devices  41 us (42%)
  waiting for transfers between devices  30.7 us (32%)
  Pallas kernels  19.1 us (20%)
  local copies, waits for them, and re-layouts  5.19 us (5%)
    ppermute x31, starting transfers between devices, to_peer(): lax.ppermute(x, axis, [(i, i ^ k if power(size) else (i + k) % size) for...  22.3 us
    ppermute x12, starting transfers between devices, onward(): lax.ppermute(x, 'narrow', [(i, after[i // 2] * 2 + i % 2) for i in range(...  18.6 us
    ppermute x12, waiting for transfers between devices, onward(): lax.ppermute(x, 'narrow', [(i, after[i // 2] * 2 + i % 2) for i in range(...  17.1 us
    ppermute x31, waiting for transfers between devices, to_peer(): lax.ppermute(x, axis, [(i, i ^ k if power(size) else (i + k) % size) for...  13.6 us
    pallas_call x3, Pallas kernels, pull(): pl.pallas_call(partial(pull_kernel, n=n, step=step, chunks=len(own) + len...  5.4 us
    pallas_call x1, Pallas kernels, middle(): pl.pallas_call(partial(middle_kernel, n=n, steps=steps, chunks=len(own)),...  5.36 us
    unnamed x24, local copies, waits for them, and re-layouts  4.12 us
    pallas_call x2, Pallas kernels, push(): pl.pallas_call(partial(push_kernel, n=n, which=which), grid_spec=pltpu.Pr...  3.2 us
  transfers between devices with their start and end apart: 43, of which 19 were waited for; matrix products, arithmetic and copies ran while one was open for 1% of the time, Pallas kernels for 13%

profile of v6, /device:TPU:0, one launch (start us, length us, event | category | flops | bytes accessed | tf_op | source)
XLA Modules:
  0.0 97.0 jit_solution(9138734331601742349)
XLA Ops:
  2.2 2.6 %collective-permute-start.5 = (bf16[1024,128]{1,0:T(8,128)(2,1)S(1)}, bf16[1024,128]{1,0:T(8,128)(2,1)S(1)}, u32[]{:S(2)}, u32[]{:S(2)}) collective-permute-start(bf16[1024,128]{1,0:T(8,128)(2,1)S(1)} %get-tuple-element.181.refs_1_), channel_id=1, source_target_pairs={{0,2},{1,3},{2,6},{3,7},{4,0},{5,1},{6,4},{7,5},{8,10},{9,11},{10,... | collective-permute-start | bytes 786440 | tf_op jit(solution)/shard_map/ppermute | solution.py:658
  4.9 2.6 %collective-permute-start = (bf16[1024,128]{1,0:T(8,128)(2,1)S(1)}, bf16[1024,128]{1,0:T(8,128)(2,1)S(1)}, u32[]{:S(2)}, u32[]{:S(2)}) collective-permute-start(bf16[1024,128]{1,0:T(8,128)(2,1)S(1)} %get-tuple-element.182.refs_2_), channel_id=1, source_target_pairs={{0,2},{1,3},{2,6},{3,7},{4,0},{5,1},{6,4},{7,5},{8,10},{9,11},{10,... | collective-permute-start | bytes 786440 | tf_op jit(solution)/shard_map/ppermute | solution.py:658
  7.5 3.4 %copy-done = s32[16,8,128,128]{3,2,1,0:T(8,128)S(1)} copy-done((s32[16,8,128,128]{3,2,1,0:T(8,128)S(1)}, s32[16,8,128,128]{3,2,1,0:T(8,128)}, u32[]{:S(2)}) %copy-start) | copy-done | bytes 8388632
  11.5 1.8 %pull0.1 = (f32[2048,128]{1,0:T(8,128)S(1)}, f32[2048,128]{1,0:T(8,128)S(1)}) custom-call(s32[8,16]{1,0:T(8,128)S(1)} %bitcast.8, s32[16,8,128,128]{3,2,1,0:T(8,128)S(1)} %copy-done, bf16[1024,128]{1,0:T(8,128)(2,1)S(1)} %get-tuple-element.181.refs_1_, bf16[1024,128]{1,0:T(8,128)(2,1)S(1)} %get-tuple-element.182.refs_2_, ...), custom_call_target="tpu_custom_call" | custom-call | flops 134217728 | bytes 3145728 | tf_op jit(solution)/shard_map/pull0/pallas_call | solution.py:158
  14.1 2.4 %collective-permute-start.3 = (s32[4]{0:T(128)S(1)}, s32[4]{0:T(128)S(1)}, u32[]{:S(2)}, u32[]{:S(2)}) collective-permute-start(s32[4]{0:T(128)S(1)} %bitcast.18), channel_id=1, source_target_pairs={{0,24},{8,16},{16,8},{24,0},{1,25},{9,17},{17,9},{25,1},{2,26},{10... | collective-permute-start | bytes 56 | tf_op jit(solution)/shard_map/ppermute | solution.py:622
  18.5 1.5 %collective-permute-done.2.refs_2_ = s32[4]{0:T(128)S(1)} collective-permute-done((s32[4]{0:T(128)S(1)}, s32[4]{0:T(128)S(1)}, u32[]{:S(2)}, u32[]{:S(2)}) %collective-permute-start.2) | collective-permute-done | bytes 48 | tf_op jit(solution)/shard_map/ppermute | solution.py:622
  21.1 3.4 %collective-permute-start.4 = (bf16[1024,128]{1,0:T(8,128)(2,1)S(1)}, bf16[1024,128]{1,0:T(8,128)(2,1)S(1)}, u32[]{:S(2)}, u32[]{:S(2)}) collective-permute-start(bf16[1024,128]{1,0:T(8,128)(2,1)S(1)} %collective-permute-done.refs_2_), channel_id=1, source_target_pairs={{0,2},{1,3},{2,6},{3,7},{4,0},{5,1},{6,4},{7,5},{8,10},{9,11},{10,... | collective-permute-start | bytes 786440 | tf_op jit(solution)/shard_map/ppermute | solution.py:658
  25.5 2.0 %collective-permute-start.9 = (bf16[128,128]{1,0:T(8,128)(2,1)S(1)}, bf16[128,128]{1,0:T(8,128)(2,1)S(1)}, u32[]{:S(2)}, u32[]{:S(2)}) collective-permute-start(bf16[128,128]{1,0:T(8,128)(2,1)S(1)} %get-tuple-element.110), channel_id=1, source_target_pairs={{0,8},{8,0},{16,24},{24,16},{1,9},{9,1},{17,25},{25,17},{2,10},{10... | collective-permute-start | bytes 98312 | tf_op jit(solution)/shard_map/ppermute | solution.py:622
  29.1 1.8 %pull1.1 = (f32[2048,128]{1,0:T(8,128)S(1)}, f32[2048,128]{1,0:T(8,128)S(1)}) custom-call(s32[8,16]{1,0:T(8,128)S(1)} %bitcast.9, s32[16,8,128,128]{3,2,1,0:T(8,128)S(1)} %copy-done.1, bf16[1024,128]{1,0:T(8,128)(2,1)S(1)} %collective-permute-done.5.refs_1_, bf16[1024,128]{1,0:T(8,128)(2,1)S(1)} %collective-permute-done.refs_2_, ...), custom_call_target="tpu_custom_call" | custom-call | flops 134217728 | bytes 3145728 | tf_op jit(solution)/shard_map/pull1/pallas_call | solution.py:158
  31.7 2.1 %collective-permute-done.11.refs_13_ = bf16[128,128]{1,0:T(8,128)(2,1)S(1)} collective-permute-done((bf16[128,128]{1,0:T(8,128)(2,1)S(1)}, bf16[128,128]{1,0:T(8,128)(2,1)S(1)}, u32[]{:S(2)}, u32[]{:S(2)}) %collective-permute-start.11) | collective-permute-done | bytes 32800 | tf_op jit(solution)/shard_map/ppermute | solution.py:622
  34.3 3.4 %collective-permute-start.12 = (bf16[1024,128]{1,0:T(8,128)(2,1)S(1)}, bf16[1024,128]{1,0:T(8,128)(2,1)S(1)}, u32[]{:S(2)}, u32[]{:S(2)}) collective-permute-start(bf16[1024,128]{1,0:T(8,128)(2,1)S(1)} %collective-permute-done.4.refs_4_), channel_id=1, source_target_pairs={{0,2},{1,3},{2,6},{3,7},{4,0},{5,1},{6,4},{7,5},{8,10},{9,11},{10,... | collective-permute-start | bytes 786440 | tf_op jit(solution)/shard_map/ppermute | solution.py:658
  38.4 1.8 %pull2.1 = (f32[2048,128]{1,0:T(8,128)S(1)}, f32[2048,128]{1,0:T(8,128)S(1)}) custom-call(s32[8,16]{1,0:T(8,128)S(1)} %bitcast.10, s32[4]{0:T(128)S(1)} %bitcast.14, s32[4]{0:T(128)S(1)} %bitcast.16, s32[16,8,128,128]{3,2,1,0:T(8,128)S(1)} %copy-done.1, bf16[1024,128]{1,0:T(8,128)(2,1)S(1)} %collective-permute-done.13.refs_3_, ...), custom_call_target="tpu_custom_call" | custom-call | flops 134217728 | bytes 3145728 | tf_op jit(solution)/shard_map/pull2/pallas_call | solution.py:158
  40.3 3.2 %collective-permute-done.12.refs_1_ = bf16[1024,128]{1,0:T(8,128)(2,1)S(1)} collective-permute-done((bf16[1024,128]{1,0:T(8,128)(2,1)S(1)}, bf16[1024,128]{1,0:T(8,128)(2,1)S(1)}, u32[]{:S(2)}, u32[]{:S(2)}) %collective-permute-start.12) | collective-permute-done | bytes 262176 | tf_op jit(solution)/shard_map/ppermute | solution.py:658
  45.0 5.4 %middle.1 = (bf16[2048,256]{1,0:T(8,128)(2,1)}, bf16[2048,256]{1,0:T(8,128)(2,1)S(1)}, bf16[2048,128]{1,0:T(8,128)(2,1)S(1)}, bf16[2048,128]{1,0:T(8,128)(2,1)S(...) custom-call(s32[8,16]{1,0:T(8,128)S(1)} %bitcast.11, bf16[16,8,128,128]{3,2,1,0:T(8,128)(2,1)S(1)} %halve.1.tiles_ref, ...), custom_call_target="tpu_custom_call" | custom-call | flops 671088640 | bytes 7864320 | tf_op jit(solution)/shard_map/middle/pallas_call | solution.py:278
  54.3 2.5 %collective-permute-start.22 = (bf16[1024,128]{1,0:T(8,128)(2,1)S(1)}, bf16[1024,128]{1,0:T(8,128)(2,1)S(1)}, u32[]{:S(2)}, u32[]{:S(2)}) collective-permute-start(bf16[1024,128]{1,0:T(8,128)(2,1)S(1)} %joined0_0.3), channel_id=1, source_target_pairs={{0,2},{1,3},{2,6},{3,7},{4,0},{5,1},{6,4},{7,5},{8,10},{9,11},{10,... | collective-permute-start | bytes 786440 | tf_op jit(solution)/shard_map/ppermute | solution.py:658
  59.3 2.4 %collective-permute-start.26 = (bf16[336,128]{1,0:T(8,128)(2,1)S(1)}, bf16[336,128]{1,0:T(8,128)(2,1)S(1)}, u32[]{:S(2)}, u32[]{:S(2)}) collective-permute-start(bf16[336,128]{1,0:T(8,128)(2,1)S(1)} %get-tuple-element.152), channel_id=1, source_target_pairs={{0,24},{8,16},{16,8},{24,0},{1,25},{9,17},{17,9},{25,1},{2,26},{10... | collective-permute-start | bytes 258056 | tf_op jit(solution)/shard_map/ppermute | solution.py:622
  61.7 1.8 %collective-permute-done.24.refs_1_.refs_3_ = bf16[336,128]{1,0:T(8,128)(2,1)S(1)} collective-permute-done((bf16[336,128]{1,0:T(8,128)(2,1)S(1)}, bf16[336,128]{1,0:T(8,128)(2,1)S(1)}, u32[]{:S(2)}, u32[]{:S(2)}) %collective-permute-start.24) | collective-permute-done | bytes 86048 | tf_op jit(solution)/shard_map/ppermute | solution.py:622
  66.4 2.8 %collective-permute-start.28 = (f32[48,256]{1,0:T(8,128)S(1)}, f32[48,256]{1,0:T(8,128)S(1)}, u32[]{:S(2)}, u32[]{:S(2)}) collective-permute-start(f32[48,256]{1,0:T(8,128)S(1)} %piece_sum.1), channel_id=1, source_target_pairs={{0,2},{1,3},{2,0},{3,1},{4,6},{5,7},{6,4},{7,5},{8,10},{9,11},{10,... | collective-permute-start | bytes 147464 | tf_op jit(solution)/shard_map/ppermute | solution.py:622
  69.4 2.5 %collective-permute-done.38.refs_0_ = bf16[1024,128]{1,0:T(8,128)(2,1)S(1)} collective-permute-done((bf16[1024,128]{1,0:T(8,128)(2,1)S(1)}, bf16[1024,128]{1,0:T(8,128)(2,1)S(1)}, u32[]{:S(2)}, u32[]{:S(2)}) %collective-permute-start.38) | collective-permute-done | bytes 262176 | tf_op jit(solution)/shard_map/ppermute | solution.py:658
  72.2 1.9 %push.3 = (bf16[2,2048,128]{2,1,0:T(8,128)(2,1)S(1)}, bf16[1024,128]{1,0:T(8,128)(2,1)S(1)}, bf16[1024,128]{1,0:T(8,128)(2,1)S(1)}, bf16[1024,128]{1,0:T(8,128)(2,1)S(1)}, bf16[1024,128]{1,0:T(8,128)(2,1)S(1)}) custom-call(s32[8,16]{1,0:T(8,128)S(1)} %bitcast.13, bf16[16,8,128,128]{3,2,1,0:T(8,128)(2,1)S(1)} %halve.1.tiles_ref, ...), custom_call_target="tpu_custom_call" | custom-call | flops 268435456 | bytes 4194304 | tf_op jit(solution)/shard_map/push/pallas_call | solution.py:322
  74.7 5.1 %collective-permute-done.27.refs_0_ = bf16[1024,128]{1,0:T(8,128)(2,1)S(1)} collective-permute-done((bf16[1024,128]{1,0:T(8,128)(2,1)S(1)}, bf16[1024,128]{1,0:T(8,128)(2,1)S(1)}, u32[]{:S(2)}, u32[]{:S(2)}) %collective-permute-start.27) | collective-permute-done | bytes 262176 | tf_op jit(solution)/shard_map/ppermute | solution.py:658
  81.0 4.2 %collective-permute-done.39.refs_0_ = bf16[1024,128]{1,0:T(8,128)(2,1)S(1)} collective-permute-done((bf16[1024,128]{1,0:T(8,128)(2,1)S(1)}, bf16[1024,128]{1,0:T(8,128)(2,1)S(1)}, u32[]{:S(2)}, u32[]{:S(2)}) %collective-permute-start.39) | collective-permute-done | bytes 262176 | tf_op jit(solution)/shard_map/ppermute | solution.py:658
  87.7 1.9 %collective-permute-start.35 = (f32[48,256]{1,0:T(8,128)S(1)}, f32[48,256]{1,0:T(8,128)S(1)}, u32[]{:S(2)}, u32[]{:S(2)}) collective-permute-start(f32[48,256]{1,0:T(8,128)S(1)} %add_add_fusion.refs_0_), channel_id=1, source_target_pairs={{0,8},{8,0},{16,24},{24,16},{1,9},{9,1},{17,25},{25,17},{2,10},{10... | collective-permute-start | bytes 147464 | tf_op jit(solution)/shard_map/ppermute | solution.py:622
  94.1 1.8 %collective-permute-done.41.refs_1_ = bf16[1024,128]{1,0:T(8,128)(2,1)S(1)} collective-permute-done((bf16[1024,128]{1,0:T(8,128)(2,1)S(1)}, bf16[1024,128]{1,0:T(8,128)(2,1)S(1)}, u32[]{:S(2)}, u32[]{:S(2)}) %collective-permute-start.41) | collective-permute-done | bytes 262176 | tf_op jit(solution)/shard_map/ppermute | solution.py:658
  (110 shorter events, 31.6 us)
Async XLA Ops:
  0.7 6.8 %collective-permute-start.6 = (bf16[2048,128]{1,0:T(8,128)(2,1)}, bf16[2048,128]{1,0:T(8,128)(2,1)S(1)}, u32[]{:S(2)}, u32[]{:S(2)}) collective-permute-start(bf16[2048,128]{1,0:T(8,128)(2,1)} %feat_ref.3), channel_id=1, source_target_pairs={{0,1},{1,0},{2,3},{3,2},{4,5},{5,4},{6,7},{7,6},{8,9},{9,8},{10,11... | collective-permute-start | bytes 1572872 | tf_op jit(solution)/shard_map/ppermute | solution.py:622
  2.2 11.1 %collective-permute-start.5 = (bf16[1024,128]{1,0:T(8,128)(2,1)S(1)}, bf16[1024,128]{1,0:T(8,128)(2,1)S(1)}, u32[]{:S(2)}, u32[]{:S(2)}) collective-permute-start(bf16[1024,128]{1,0:T(8,128)(2,1)S(1)} %get-tuple-element.181.refs_1_), channel_id=1, source_target_pairs={{0,2},{1,3},{2,6},{3,7},{4,0},{5,1},{6,4},{7,5},{8,10},{9,11},{10,... | collective-permute-start | bytes 786440 | tf_op jit(solution)/shard_map/ppermute | solution.py:658
  4.9 15.7 %collective-permute-start = (bf16[1024,128]{1,0:T(8,128)(2,1)S(1)}, bf16[1024,128]{1,0:T(8,128)(2,1)S(1)}, u32[]{:S(2)}, u32[]{:S(2)}) collective-permute-start(bf16[1024,128]{1,0:T(8,128)(2,1)S(1)} %get-tuple-element.182.refs_2_), channel_id=1, source_target_pairs={{0,2},{1,3},{2,6},{3,7},{4,0},{5,1},{6,4},{7,5},{8,10},{9,11},{10,... | collective-permute-start | bytes 786440 | tf_op jit(solution)/shard_map/ppermute | solution.py:658
  13.3 11.2 %collective-permute-start.13 = (bf16[1024,128]{1,0:T(8,128)(2,1)S(1)}, bf16[1024,128]{1,0:T(8,128)(2,1)S(1)}, u32[]{:S(2)}, u32[]{:S(2)}) collective-permute-start(bf16[1024,128]{1,0:T(8,128)(2,1)S(1)} %collective-permute-done.5.refs_1_), channel_id=1, source_target_pairs={{0,2},{1,3},{2,6},{3,7},{4,0},{5,1},{6,4},{7,5},{8,10},{9,11},{10,... | collective-permute-start | bytes 786440 | tf_op jit(solution)/shard_map/ppermute | solution.py:658
  20.6 6.9 %collective-permute-start.8 = (bf16[1024,128]{1,0:T(8,128)(2,1)S(1)}, bf16[1024,128]{1,0:T(8,128)(2,1)S(1)}, u32[]{:S(2)}, u32[]{:S(2)}) collective-permute-start(bf16[1024,128]{1,0:T(8,128)(2,1)S(1)} %collective-permute-done.refs_2_), channel_id=1, source_target_pairs={{0,1},{1,0},{2,3},{3,2},{4,5},{5,4},{6,7},{7,6},{8,9},{9,8},{10,11... | collective-permute-start | bytes 786440 | tf_op jit(solution)/shard_map/ppermute | solution.py:622
  20.6 8.4 %collective-permute-start.7 = (bf16[1024,128]{1,0:T(8,128)(2,1)S(1)}, bf16[1024,128]{1,0:T(8,128)(2,1)S(1)}, u32[]{:S(2)}, u32[]{:S(2)}) collective-permute-start(bf16[1024,128]{1,0:T(8,128)(2,1)S(1)} %collective-permute-done.5.refs_1_), channel_id=1, source_target_pairs={{0,1},{1,0},{2,3},{3,2},{4,5},{5,4},{6,7},{7,6},{8,9},{9,8},{10,11... | collective-permute-start | bytes 786440 | tf_op jit(solution)/shard_map/ppermute | solution.py:622
  21.1 10.1 %collective-permute-start.4 = (bf16[1024,128]{1,0:T(8,128)(2,1)S(1)}, bf16[1024,128]{1,0:T(8,128)(2,1)S(1)}, u32[]{:S(2)}, u32[]{:S(2)}) collective-permute-start(bf16[1024,128]{1,0:T(8,128)(2,1)S(1)} %collective-permute-done.refs_2_), channel_id=1, source_target_pairs={{0,2},{1,3},{2,6},{3,7},{4,0},{5,1},{6,4},{7,5},{8,10},{9,11},{10,... | collective-permute-start | bytes 786440 | tf_op jit(solution)/shard_map/ppermute | solution.py:658
  24.5 13.2 %collective-permute-start.16 = (bf16[1024,128]{1,0:T(8,128)(2,1)S(1)}, bf16[1024,128]{1,0:T(8,128)(2,1)S(1)}, u32[]{:S(2)}, u32[]{:S(2)}) collective-permute-start(bf16[1024,128]{1,0:T(8,128)(2,1)S(1)} %collective-permute-done.13.refs_3_), channel_id=1, source_target_pairs={{0,2},{1,3},{2,6},{3,7},{4,0},{5,1},{6,4},{7,5},{8,10},{9,11},{10,... | collective-permute-start | bytes 786440 | tf_op jit(solution)/shard_map/ppermute | solution.py:658
  25.5 5.7 %collective-permute-start.9 = (bf16[128,128]{1,0:T(8,128)(2,1)S(1)}, bf16[128,128]{1,0:T(8,128)(2,1)S(1)}, u32[]{:S(2)}, u32[]{:S(2)}) collective-permute-start(bf16[128,128]{1,0:T(8,128)(2,1)S(1)} %get-tuple-element.110), channel_id=1, source_target_pairs={{0,8},{8,0},{16,24},{24,16},{1,9},{9,1},{17,25},{25,17},{2,10},{10... | collective-permute-start | bytes 98312 | tf_op jit(solution)/shard_map/ppermute | solution.py:622
  34.3 9.1 %collective-permute-start.12 = (bf16[1024,128]{1,0:T(8,128)(2,1)S(1)}, bf16[1024,128]{1,0:T(8,128)(2,1)S(1)}, u32[]{:S(2)}, u32[]{:S(2)}) collective-permute-start(bf16[1024,128]{1,0:T(8,128)(2,1)S(1)} %collective-permute-done.4.refs_4_), channel_id=1, source_target_pairs={{0,2},{1,3},{2,6},{3,7},{4,0},{5,1},{6,4},{7,5},{8,10},{9,11},{10,... | collective-permute-start | bytes 786440 | tf_op jit(solution)/shard_map/ppermute | solution.py:658
  37.7 5.7 %collective-permute-start.17 = (bf16[1024,128]{1,0:T(8,128)(2,1)S(1)}, bf16[1024,128]{1,0:T(8,128)(2,1)S(1)}, u32[]{:S(2)}, u32[]{:S(2)}) collective-permute-start(bf16[1024,128]{1,0:T(8,128)(2,1)S(1)} %collective-permute-done.16.refs_0_), channel_id=1, source_target_pairs={{0,1},{1,0},{2,3},{3,2},{4,5},{5,4},{6,7},{7,6},{8,9},{9,8},{10,11... | collective-permute-start | bytes 786440 | tf_op jit(solution)/shard_map/ppermute | solution.py:622
  54.3 14.9 %collective-permute-start.22 = (bf16[1024,128]{1,0:T(8,128)(2,1)S(1)}, bf16[1024,128]{1,0:T(8,128)(2,1)S(1)}, u32[]{:S(2)}, u32[]{:S(2)}) collective-permute-start(bf16[1024,128]{1,0:T(8,128)(2,1)S(1)} %joined0_0.3), channel_id=1, source_target_pairs={{0,2},{1,3},{2,6},{3,7},{4,0},{5,1},{6,4},{7,5},{8,10},{9,11},{10,... | collective-permute-start | bytes 786440 | tf_op jit(solution)/shard_map/ppermute | solution.py:658
  56.9 15.0 %collective-permute-start.38 = (bf16[1024,128]{1,0:T(8,128)(2,1)S(1)}, bf16[1024,128]{1,0:T(8,128)(2,1)S(1)}, u32[]{:S(2)}, u32[]{:S(2)}) collective-permute-start(bf16[1024,128]{1,0:T(8,128)(2,1)S(1)} %joined0_1.3), channel_id=1, source_target_pairs={{0,2},{1,3},{2,6},{3,7},{4,0},{5,1},{6,4},{7,5},{8,10},{9,11},{10,... | collective-permute-start | bytes 786440 | tf_op jit(solution)/shard_map/ppermute | solution.py:658
  64.7 9.4 %collective-permute-start.30 = (f32[48,256]{1,0:T(8,128)S(1)}, f32[48,256]{1,0:T(8,128)S(1)}, u32[]{:S(2)}, u32[]{:S(2)}) collective-permute-start(f32[48,256]{1,0:T(8,128)S(1)} %piece_sum.1), channel_id=1, source_target_pairs={{0,6},{1,7},{2,4},{3,5},{4,2},{5,3},{6,0},{7,1},{8,14},{9,15},{10,... | collective-permute-start | bytes 147464 | tf_op jit(solution)/shard_map/ppermute | solution.py:622
  65.5 8.7 %collective-permute-start.29 = (f32[48,256]{1,0:T(8,128)S(1)}, f32[48,256]{1,0:T(8,128)S(1)}, u32[]{:S(2)}, u32[]{:S(2)}) collective-permute-start(f32[48,256]{1,0:T(8,128)S(1)} %piece_sum.1), channel_id=1, source_target_pairs={{0,4},{1,5},{2,6},{3,7},{4,0},{5,1},{6,2},{7,3},{8,12},{9,13},{10,... | collective-permute-start | bytes 147464 | tf_op jit(solution)/shard_map/ppermute | solution.py:622
  66.4 8.3 %collective-permute-start.28 = (f32[48,256]{1,0:T(8,128)S(1)}, f32[48,256]{1,0:T(8,128)S(1)}, u32[]{:S(2)}, u32[]{:S(2)}) collective-permute-start(f32[48,256]{1,0:T(8,128)S(1)} %piece_sum.1), channel_id=1, source_target_pairs={{0,2},{1,3},{2,0},{3,1},{4,6},{5,7},{6,4},{7,5},{8,10},{9,11},{10,... | collective-permute-start | bytes 147464 | tf_op jit(solution)/shard_map/ppermute | solution.py:622
  69.3 10.5 %collective-permute-start.27 = (bf16[1024,128]{1,0:T(8,128)(2,1)S(1)}, bf16[1024,128]{1,0:T(8,128)(2,1)S(1)}, u32[]{:S(2)}, u32[]{:S(2)}) collective-permute-start(bf16[1024,128]{1,0:T(8,128)(2,1)S(1)} %joined0_0.4), channel_id=1, source_target_pairs={{0,2},{1,3},{2,6},{3,7},{4,0},{5,1},{6,4},{7,5},{8,10},{9,11},{10,... | collective-permute-start | bytes 786440 | tf_op jit(solution)/shard_map/ppermute | solution.py:658
  72.0 13.3 %collective-permute-start.39 = (bf16[1024,128]{1,0:T(8,128)(2,1)S(1)}, bf16[1024,128]{1,0:T(8,128)(2,1)S(1)}, u32[]{:S(2)}, u32[]{:S(2)}) collective-permute-start(bf16[1024,128]{1,0:T(8,128)(2,1)S(1)} %joined0_1.4), channel_id=1, source_target_pairs={{0,2},{1,3},{2,6},{3,7},{4,0},{5,1},{6,4},{7,5},{8,10},{9,11},{10,... | collective-permute-start | bytes 786440 | tf_op jit(solution)/shard_map/ppermute | solution.py:658
  74.1 6.2 %collective-permute-start.31 = (bf16[1024,128]{1,0:T(8,128)(2,1)S(1)}, bf16[1024,128]{1,0:T(8,128)(2,1)S(1)}, u32[]{:S(2)}, u32[]{:S(2)}) collective-permute-start(bf16[1024,128]{1,0:T(8,128)(2,1)S(1)} %get-tuple-element.162), channel_id=1, source_target_pairs={{0,1},{1,0},{2,3},{3,2},{4,5},{5,4},{6,7},{7,6},{8,9},{9,8},{10,11... | collective-permute-start | bytes 786440 | tf_op jit(solution)/shard_map/ppermute | solution.py:622
  74.2 11.0 %collective-permute-start.40 = (bf16[1024,128]{1,0:T(8,128)(2,1)S(1)}, bf16[1024,128]{1,0:T(8,128)(2,1)S(1)}, u32[]{:S(2)}, u32[]{:S(2)}) collective-permute-start(bf16[1024,128]{1,0:T(8,128)(2,1)S(1)} %get-tuple-element.169), channel_id=1, source_target_pairs={{0,1},{1,0},{2,3},{3,2},{4,5},{5,4},{6,7},{7,6},{8,9},{9,8},{10,11... | collective-permute-start | bytes 786440 | tf_op jit(solution)/shard_map/ppermute | solution.py:622
  79.8 6.4 %collective-permute-start.33 = (bf16[1024,128]{1,0:T(8,128)(2,1)S(1)}, bf16[1024,128]{1,0:T(8,128)(2,1)S(1)}, u32[]{:S(2)}, u32[]{:S(2)}) collective-permute-start(bf16[1024,128]{1,0:T(8,128)(2,1)S(1)} %get-tuple-element.163), channel_id=1, source_target_pairs={{0,1},{1,0},{2,3},{3,2},{4,5},{5,4},{6,7},{7,6},{8,9},{9,8},{10,11... | collective-permute-start | bytes 786440 | tf_op jit(solution)/shard_map/ppermute | solution.py:622
  79.8 7.9 %collective-permute-start.34 = (bf16[1024,128]{1,0:T(8,128)(2,1)S(1)}, bf16[1024,128]{1,0:T(8,128)(2,1)S(1)}, u32[]{:S(2)}, u32[]{:S(2)}) collective-permute-start(bf16[1024,128]{1,0:T(8,128)(2,1)S(1)} %get-tuple-element.164), channel_id=1, source_target_pairs={{0,1},{1,0},{2,3},{3,2},{4,5},{5,4},{6,7},{7,6},{8,9},{9,8},{10,11... | collective-permute-start | bytes 786440 | tf_op jit(solution)/shard_map/ppermute | solution.py:622
  80.5 11.3 %collective-permute-start.32 = (bf16[1024,128]{1,0:T(8,128)(2,1)S(1)}, bf16[1024,128]{1,0:T(8,128)(2,1)S(1)}, u32[]{:S(2)}, u32[]{:S(2)}) collective-permute-start(bf16[1024,128]{1,0:T(8,128)(2,1)S(1)} %joined0_0.5), channel_id=1, source_target_pairs={{0,2},{1,3},{2,6},{3,7},{4,0},{5,1},{6,4},{7,5},{8,10},{9,11},{10,... | collective-permute-start | bytes 786440 | tf_op jit(solution)/shard_map/ppermute | solution.py:658
  85.4 10.5 %collective-permute-start.41 = (bf16[1024,128]{1,0:T(8,128)(2,1)S(1)}, bf16[1024,128]{1,0:T(8,128)(2,1)S(1)}, u32[]{:S(2)}, u32[]{:S(2)}) collective-permute-start(bf16[1024,128]{1,0:T(8,128)(2,1)S(1)} %joined0_1.5), channel_id=1, source_target_pairs={{0,2},{1,3},{2,6},{3,7},{4,0},{5,1},{6,4},{7,5},{8,10},{9,11},{10,... | collective-permute-start | bytes 786440 | tf_op jit(solution)/shard_map/ppermute | solution.py:658
  (31 other events, 180.7 us)
